TPU v7x, 32 devices: a whole 2x2x4 slice. The times are simulated.
32 devices in a mesh: grid: 4 (over x, core), mark: 8 (over z, y).
Axes of the slice: x: 2, y: 2, z: 4, core: 2. Of those that a mesh axis runs over, the one named last changes fastest.
Arguments:
- velocity: float32 [3, 128, 128, 256], P(None, 'grid', 'mark'), may hold values from -6 to 6
- pressure: float32 [128, 128, 256], P('grid', 'mark'), may hold values from -6 to 6
- cell_visc: float32 [128, 128, 256], P('grid', 'mark'), may hold values from 0.2 to 5
- cell_dens: float32 [128, 128, 256], P('grid', 'mark'), may hold values from 0.5 to 1.5
- block_brick: int32 [256, 48], P(('grid', 'mark')), may hold values from 0 to 1023
- block_counts: int32 [32, 8], P(('grid', 'mark')), may hold values from 0 to 48, as said below
- positions: float32 [256, 3, 48, 256], P(('grid', 'mark')), may hold values from 0 to 1
- start_visc: float32 [256, 48, 256], P(('grid', 'mark')), may hold values from 0.2 to 5
- marker_dens: float32 [256, 48, 256], P(('grid', 'mark')), may hold values from 0.5 to 1.5
Outputs:
- velocity_next: float32 [3, 128, 128, 256], P(None, 'grid', 'mark')
- pressure_next: float32 [128, 128, 256], P('grid', 'mark')
- visc_next: float32 [128, 128, 256], P('grid', 'mark')
- dens_next: float32 [128, 128, 256], P('grid', 'mark')
- marker_visc: float32 [256, 48, 256], P(('grid', 'mark'))
Inputs may be any that keep to these rules, and one draw needn't show every extreme that they name: `block_counts`: entry q of a marker device's row counts its live slots toward the grid device of mark index q in its group; in every group some grid device gets exactly 48 live slots from every marker device. `block_brick`: dead slots name bricks too.
All inputs are finite; a program needn't handle non-finite values.
Results may differ from a plain program's by a relative error of at most 0.0003.
Values sent between devices are 32-bit elements; how exact they have to be, the bound alone decides.
No kernel may reach another device: no remote copies, remote signals or barrier semaphores. Data moves between devices by JAX's collectives and lax.ppermute only.
A program may use at most 128 MiB of HBM per device.

v0:
```python
import jax
import jax.numpy as jnp
from jax import lax
from jax.sharding import PartitionSpec as P

ITERS = 4


relax_weight = 0.6
pressure_rate = 0.25
gravity = 1.0
strain_scale = 0.5


def extended(value, sides, width):
    for axis, dim in sides:
        size, length = (lax.axis_size(axis), value.shape[dim])
        up = [(i, (i + 1) % size) for i in range(size - 1)]
        down = [(j, i) for i, j in up]
        last = lax.slice_in_dim(value, length - width, length, axis=dim)
        initial = lax.slice_in_dim(value, 0, width, axis=dim)
        before = lax.ppermute(last, axis, up)
        after = lax.ppermute(initial, axis, down)
        value = jnp.concatenate([before, value, after], axis=dim)
    return value


def neighbours(padded):
    centre = padded[1:-1, 1:-1, 1:-1]
    return (
        centre,
        [
            padded[2:, 1:-1, 1:-1],
            padded[:-2, 1:-1, 1:-1],
            padded[1:-1, 2:, 1:-1],
            padded[1:-1, :-2, 1:-1],
            padded[1:-1, 1:-1, 2:],
            padded[1:-1, 1:-1, :-2],
        ],
    )


def relax_sweep(padded_velocity, padded_pressure, padded_visc, density):
    viscosity, visc_near = neighbours(padded_visc)
    couplings = [0.5 * (viscosity + nearby) for nearby in visc_near]
    diagonal = sum(couplings)
    pressure, pressure_near = neighbours(padded_pressure)
    divergence = jnp.zeros_like(pressure)
    updated = []
    for component in range(3):
        current, current_near = neighbours(padded_velocity[component])
        laplace = sum(
            (weight * (nearby - current) for weight, nearby in zip(couplings, current_near))
        )
        forcing = laplace - (pressure - pressure_near[2 * component + 1])
        if component == 2:
            forcing = forcing - gravity * density
        updated.append(current + relax_weight * forcing / diagonal)
        divergence = divergence + current_near[2 * component] - current
    return (jnp.stack(updated), pressure - pressure_rate * viscosity * divergence)


def kernel(fraction, number_cells):
    position = fraction * number_cells
    centres = jnp.arange(number_cells, dtype=jnp.float32) + 0.5
    offset = position[:, None, :] - centres[None, :, None]
    gaussian = jnp.exp(-offset * offset)
    weights = gaussian / jnp.sum(gaussian, axis=1, keepdims=True)
    slopes = weights * (2.0 * jnp.sum(weights * offset, axis=1, keepdims=True) - 2.0 * offset)
    return (weights, slopes)


def marker_blocks(bricks, positions, start_visc, density, live_slots):
    highest = lax.Precision.HIGHEST
    blocks = bricks.shape[0]
    markers = positions.shape[-1]
    across_x, slope_x = kernel(positions[0], 4)
    across_y, slope_y = kernel(positions[1], 4)
    across_z, slope_z = kernel(positions[2], 8)
    values = bricks.reshape(blocks, 48, 8)
    interpolated = jnp.einsum("kcz,kzm->kcm", values, across_z, precision=highest).reshape(
        blocks, 3, 4, 4, markers
    )
    rising = jnp.einsum("kcz,kzm->kcm", values, slope_z, precision=highest).reshape(
        blocks, 3, 4, 4, markers
    )
    plane_xy = across_x[:, :, None, :] * across_y[:, None, :, :]
    plane_dx = slope_x[:, :, None, :] * across_y[:, None, :, :]
    plane_dy = across_x[:, :, None, :] * slope_y[:, None, :, :]
    grad_x = jnp.sum(interpolated * plane_dx[:, None], axis=(2, 3))
    grad_y = jnp.sum(interpolated * plane_dy[:, None], axis=(2, 3))
    grad_z = jnp.sum(rising * plane_xy[:, None], axis=(2, 3))
    normal = grad_x[:, 0] ** 2 + grad_y[:, 1] ** 2 + grad_z[:, 2] ** 2
    shear_xy = 0.5 * (grad_y[:, 0] + grad_x[:, 1])
    shear_xz = 0.5 * (grad_z[:, 0] + grad_x[:, 2])
    shear_yz = 0.5 * (grad_z[:, 1] + grad_y[:, 2])
    invariant = 0.5 * normal + shear_xy**2 + shear_xz**2 + shear_yz**2
    weakened = start_visc * jnp.exp(-jnp.log(1.0 + invariant / (strain_scale * strain_scale)) / 3.0)
    marker_visc = jnp.where(live_slots[:, None], weakened, 0.0)
    filled = jnp.broadcast_to(live_slots[:, None], weakened.shape).astype(jnp.float32)
    carried = jnp.stack([filled, filled * jnp.log(weakened), filled * density], axis=1)
    spread = (carried[:, :, None, None, :] * plane_xy[:, None]).reshape(blocks, 48, markers)
    moments = jnp.einsum("kcm,kzm->kcz", spread, across_z, precision=highest).reshape(blocks, 384)
    return (marker_visc, moments)


def per_device(
    velocity,
    pressure,
    cell_visc,
    cell_dens,
    block_brick,
    block_counts,
    positions,
    start_visc,
    marker_dens,
):
    highest = lax.Precision.HIGHEST
    size_x, size_y, size_z = cell_visc.shape
    near_visc = jnp.pad(
        extended(cell_visc, (("grid", 0), ("mark", 1)), 1), ((0, 0), (0, 0), (1, 1))
    )
    unknowns = jnp.concatenate([velocity, pressure[None]], axis=0)
    for iteration in range(ITERS):
        padded = jnp.pad(
            extended(unknowns, (("grid", 1), ("mark", 2)), 1), ((0, 0), (0, 0), (0, 0), (1, 1))
        )
        velocity_now, pressure_now = relax_sweep(padded[:3], padded[3], near_visc, cell_dens)
        unknowns = jnp.concatenate([velocity_now, pressure_now[None]], axis=0)
    bricks = (
        velocity.reshape(3, size_x // 4, 4, size_y // 4, 4, size_z // 8, 8)
        .transpose(1, 3, 5, 0, 2, 4, 6)
        .reshape(-1, 384)
    )
    owners = lax.axis_size("mark")
    whole_slab = lax.all_gather(bricks, "mark", axis=0, tiled=True)
    slab_rows = jnp.arange(owners, dtype=jnp.int32)[:, None] * bricks.shape[0] + block_brick
    fetched = whole_slab[slab_rows]
    live_slots = (
        jnp.arange(block_brick.shape[1], dtype=jnp.int32)[None, :] < block_counts[0][:, None]
    )

    def owner_work(inputs):
        received, places, visc_start, dens_start, slot_live = inputs
        return marker_blocks(received, places, visc_start, dens_start, slot_live)

    marker_visc, moments = lax.map(
        owner_work, (fetched, positions, start_visc, marker_dens, live_slots)
    )
    catalog = jnp.arange(bricks.shape[0], dtype=jnp.int32)
    one_hot = (block_brick[:, :, None] == catalog).astype(jnp.float32)
    per_owner = jnp.einsum("psb,psq->pbq", one_hot, moments, precision=highest)
    moment_sums = lax.psum_scatter(per_owner, "mark", scatter_dimension=0, tiled=True)[0]
    cell_moments = (
        moment_sums.reshape(size_x // 4, size_y // 4, size_z // 8, 3, 4, 4, 8)
        .transpose(3, 0, 4, 1, 5, 2, 6)
        .reshape(3, size_x, size_y, size_z)
    )
    visc_next = jnp.exp((cell_moments[1] + jnp.log(cell_visc)) / (cell_moments[0] + 1.0))
    dens_next = (cell_moments[2] + cell_dens) / (cell_moments[0] + 1.0)
    return (unknowns[:3], unknowns[3], visc_next, dens_next, marker_visc)


def solution(mesh):
    in_specs = (
        P(None, "grid", "mark", None),
        P("grid", "mark", None),
        P("grid", "mark", None),
        P("grid", "mark", None),
        P(("grid", "mark"), None),
        P(("grid", "mark"), None),
        P(("grid", "mark"), None, None, None),
        P(("grid", "mark"), None, None),
        P(("grid", "mark"), None, None),
    )
    out_specs = (
        P(None, "grid", "mark", None),
        P("grid", "mark", None),
        P("grid", "mark", None),
        P("grid", "mark", None),
        P(("grid", "mark"), None, None),
    )
    return jax.shard_map(
        per_device, mesh=mesh, in_specs=in_specs, out_specs=out_specs, check_vma=False
    )
```

profile of v0, /device:TPU:18, one launch (start us, length us, event | category | flops | bytes accessed | tf_op | source)
XLA Modules:
  0.0 835.7 jit_solution(12636131611808753909)
XLA Ops:
  7.2 17.1 %reshape.311 = f32[3,8,4,4,4,32,8]{6,5,4,3,2,1,0:T(8,128)} reshape(f32[3,32,16,256]{3,2,1,0:T(8,128)} %param.11) | data formatting | bytes 3145728 | tf_op jit(solution)/shard_map/reshape | solution.py:131
  24.4 16.7 %copy.38 = f32[8,4,32,3,4,4,8]{2,1,0,6,5,4,3:T(4,128)} copy(f32[8,4,32,3,4,4,8]{6,2,5,1,4,0,3:T(8,128)} %bitcast.127) | data formatting | bytes 3145728 | tf_op jit(solution)/shard_map/transpose | solution.py:132
  41.1 7.5 reshape.312
  51.1 175.8 %all-gather.2.cloned.1.call-done = f32[8192,384]{1,0:T(8,128)} async-done(((f32[1024,384]{1,0:T(8,128)}), f32[8192,384]{1,0:T(8,128)}) %all-gather.2.cloned.1.call-update) | async-done | bytes 12582928 | tf_op jit(solution)/shard_map/all_gather | solution.py:136
  226.9 7.0 gather_fusion
  233.9 252.4 %while.12 = (s32[]{:T(128)}, f32[8,48,256]{2,1,0:T(8,128)}, f32[8,48,384]{1,2,0:T(8,128)}, pred[8,48]{1,0:T(8,128)(4,1)}, f32[8,48,256]{2,1,0:T(8,128)}, /*index...) while((s32[]{:T(128)}, f32[8,48,256]{2,1,0:T(8,128)}, ...), condition=%wide.region_10.11_spmd, body=%wide.region_0.10_spmd.sunk | while | flops 178716736 | bytes 41927868 | solution.py:147
  486.3 10.3 %fusion.78 = f32[8,1024,384]{2,1,0:T(8,128)} fusion(f32[8,48,384]{1,2,0:T(8,128)} %get-tuple-element.48, s32[8,48]{1,0:T(8,128)S(1)} %copy-done.13), kind=kOutput, calls=%fused_computation.147 | convolution fusion | flops 1812725760 | bytes 13174272 | tf_op jit(solution)/shard_map/psb,psq->pbq/dot_general | solution.py:152
  507.9 3.9 collective-permute-start.2
  518.3 5.0 collective-permute-done.2
  523.3 5.1 select_maximum_fusion
  536.1 5.3 collective-permute-done.7
  555.9 4.1 collective-permute-start.10
  560.0 6.4 collective-permute-done.11
  566.3 4.9 collective-permute-done.10
  580.0 128.2 %reduce-scatter.2.cloned.1.call-done = f32[1,1024,384]{2,1,0:T(8,128)} async-done(((f32[8,1024,384]{2,1,0:T(8,128)}), f32[1,1024,384]{2,1,0:T(8,128)}) %reduce-scatter.2.cloned.1.call-update) | async-done | bytes 1572880 | tf_op jit(solution)/shard_map/reduce_scatter | solution.py:153
  711.2 6.1 reshape_squeeze.3
  717.3 6.4 copy.68
  726.6 6.5 copy.47
  733.2 7.7 add.574
  740.8 6.4 copy.48
  747.2 7.7 squeeze.98
  754.8 6.4 copy.46
  761.2 7.7 squeeze.97
  768.9 6.0 add_divide_fusion
  (398 shorter events, 360.7 us)
Async XLA Ops:
  7.2 219.8 %all-gather.2.cloned.1.call-start = ((), (), s32[]{:S(2)}) async-start(), calls=%async_computation.1 | async-start | bytes 14155776 | tf_op jit(solution)/shard_map/all_gather | solution.py:136
  50.2 658.0 %reduce-scatter.2.cloned.1.call-start = ((), (), s32[]{:S(2)}) async-start(), calls=%async_computation.2 | async-start | bytes 14155776 | tf_op jit(solution)/shard_map/reduce_scatter | solution.py:153
  498.1 13.7 %copy-start = (f32[32,16,256]{2,1,0:T(8,128)S(1)}, f32[32,16,256]{2,1,0:T(8,128)}, u32[]{:S(2)}) copy-start(f32[32,16,256]{2,1,0:T(8,128)} %param.13) | copy-start | bytes 1572868
  498.1 4.5 collective-permute-start.1
  500.2 5.6 collective-permute-start
  505.9 12.4 %collective-permute-start.3 = (f32[4,34,1,256]{3,2,1,0:T(1,128)S(1)}, f32[4,34,1,256]{3,2,1,0:T(1,128)S(1)}, u32[]{:S(2)}, u32[]{:S(2)}) collective-permute-start(f32[4,34,1,256]{3,2,1,0:T(1,128)S(1)} %get-tuple-element.158), channel_id=1, source_target_pairs={{1,0},{2,1},{3,2},{4,3},{5,4},{6,5},{7,6},{9,8},{10,9},{11,10},{12... | collective-permute-start | bytes 417800 | tf_op jit(solution)/shard_map/ppermute | solution.py:23
  507.9 15.4 %collective-permute-start.2 = (f32[4,34,1,256]{3,2,1,0:T(1,128)S(1)}, f32[4,34,1,256]{3,2,1,0:T(1,128)S(1)}, u32[]{:S(2)}, u32[]{:S(2)}) collective-permute-start(f32[4,34,1,256]{3,2,1,0:T(1,128)S(1)} %get-tuple-element.157), channel_id=1, source_target_pairs={{0,1},{1,2},{2,3},{3,4},{4,5},{5,6},{6,7},{8,9},{9,10},{10,11},{11... | collective-permute-start | bytes 417800 | tf_op jit(solution)/shard_map/ppermute | solution.py:22
  511.8 5.6 collective-permute-start.5
  513.8 16.1 %collective-permute-start.4 = (f32[1,16,256]{2,1,0:T(8,128)S(1)}, f32[1,16,256]{2,1,0:T(8,128)S(1)}, u32[]{:S(2)}, u32[]{:S(2)}) collective-permute-start(f32[1,16,256]{2,1,0:T(8,128)S(1)} %get-tuple-element.175), channel_id=1, source_target_pairs={{8,0},{16,8},{24,16},{9,1},{17,9},{25,17},{10,2},{18,10},{26,18},{... | collective-permute-start | bytes 49160 | tf_op jit(solution)/shard_map/ppermute | solution.py:23
  529.9 6.2 collective-permute-start.6
  531.9 9.6 %collective-permute-start.7 = (f32[34,1,256]{2,1,0:T(1,128)S(1)}, f32[34,1,256]{2,1,0:T(1,128)S(1)}, u32[]{:S(2)}, u32[]{:S(2)}) collective-permute-start(f32[34,1,256]{2,1,0:T(1,128)S(1)} %get-tuple-element.167), channel_id=1, source_target_pairs={{0,1},{1,2},{2,3},{3,4},{4,5},{5,6},{6,7},{8,9},{9,10},{10,11},{11... | collective-permute-start | bytes 104456 | tf_op jit(solution)/shard_map/ppermute | solution.py:22
  546.2 4.3 collective-permute-start.9
  548.1 5.6 collective-permute-start.8
  553.9 12.4 %collective-permute-start.11 = (f32[4,34,1,256]{3,2,1,0:T(1,128)S(1)}, f32[4,34,1,256]{3,2,1,0:T(1,128)S(1)}, u32[]{:S(2)}, u32[]{:S(2)}) collective-permute-start(f32[4,34,1,256]{3,2,1,0:T(1,128)S(1)} %get-tuple-element.156), channel_id=1, source_target_pairs={{1,0},{2,1},{3,2},{4,3},{5,4},{6,5},{7,6},{9,8},{10,9},{11,10},{12... | collective-permute-start | bytes 417800 | tf_op jit(solution)/shard_map/ppermute | solution.py:23
  555.9 15.4 %collective-permute-start.10 = (f32[4,34,1,256]{3,2,1,0:T(1,128)S(1)}, f32[4,34,1,256]{3,2,1,0:T(1,128)S(1)}, u32[]{:S(2)}, u32[]{:S(2)}) collective-permute-start(f32[4,34,1,256]{3,2,1,0:T(1,128)S(1)} %get-tuple-element.155), channel_id=1, source_target_pairs={{0,1},{1,2},{2,3},{3,4},{4,5},{5,6},{6,7},{8,9},{9,10},{10,11},{11... | collective-permute-start | bytes 417800 | tf_op jit(solution)/shard_map/ppermute | solution.py:22
  768.9 6.0 copy-start.11
  774.9 4.3 collective-permute-start.13
  776.9 5.6 collective-permute-start.12
  782.7 8.4 %collective-permute-start.15 = (f32[4,34,1,256]{3,2,1,0:T(1,128)S(1)}, f32[4,34,1,256]{3,2,1,0:T(1,128)S(1)}, u32[]{:S(2)}, u32[]{:S(2)}) collective-permute-start(f32[4,34,1,256]{3,2,1,0:T(1,128)S(1)} %get-tuple-element.154), channel_id=1, source_target_pairs={{1,0},{2,1},{3,2},{4,3},{5,4},{6,5},{7,6},{9,8},{10,9},{11,10},{12... | collective-permute-start | bytes 417800 | tf_op jit(solution)/shard_map/ppermute | solution.py:23
  785.2 7.8 collective-permute-start.14
  800.5 4.3 collective-permute-start.17
  802.4 5.6 collective-permute-start.16
  808.2 8.4 %collective-permute-start.19 = (f32[4,34,1,256]{3,2,1,0:T(1,128)S(1)}, f32[4,34,1,256]{3,2,1,0:T(1,128)S(1)}, u32[]{:S(2)}, u32[]{:S(2)}) collective-permute-start(f32[4,34,1,256]{3,2,1,0:T(1,128)S(1)} %get-tuple-element.152), channel_id=1, source_target_pairs={{1,0},{2,1},{3,2},{4,3},{5,4},{6,5},{7,6},{9,8},{10,9},{11,10},{12... | collective-permute-start | bytes 417800 | tf_op jit(solution)/shard_map/ppermute | solution.py:23
  811.0 7.8 collective-permute-start.18
  (27 other events, 80.0 us)
Sparse Core Ops, SparseCore 0:
  50.3 176.5 all-gather.1
  496.7 211.3 reduce-scatter.1
where the time goes:
time: 846 us; the launch traced here: 836 us
  waiting for transfers between devices  349 us (41%)
  local copies, waits for them, and re-layouts  199 us (24%)
  other arithmetic  146 us (17%)
  matrix products  72.3 us (9%)
  starting transfers between devices  52.5 us (6%)
  between operations  15.1 us (2%)
    all_gather x1, waiting for transfers between devices, per_device(): whole_slab = lax.all_gather(bricks, 'mark', axis=0, tiled=True)  176 us
    reduce_scatter x1, waiting for transfers between devices, per_device(): lax.psum_scatter(per_owner, 'mark', scatter_dimension=0, tiled=True)[0]  128 us
    ppermute x10, waiting for transfers between devices, extended(): before = lax.ppermute(last, axis, up)  32.1 us
    ppermute x10, starting transfers between devices, extended(): before = lax.ppermute(last, axis, up)  29.8 us
    dot_general x8, matrix products, marker_blocks(): jnp.einsum('kcz,kzm->kcm', values, across_z, precision=highest)  27.9 us
    reduce_sum x8, other arithmetic, marker_blocks(): grad_x = jnp.sum(interpolated * plane_dx[:, None], axis=(2, 3))  24.8 us
    reduce_sum x8, other arithmetic, marker_blocks(): grad_z = jnp.sum(rising * plane_xy[:, None], axis=(2, 3))  23 us
    ppermute x10, starting transfers between devices, extended(): after = lax.ppermute(initial, axis, down)  22.5 us
  transfers between devices with their start and end apart: 22, of which 16 were waited for; matrix products, arithmetic and copies ran while one was open for 3% of the time, Pallas kernels for 0%

commit v1 on v0

v1 whole, which is shorter than its diff:
```python
import functools

import jax
import jax.numpy as jnp
import numpy as np
from jax import lax
from jax.experimental import pallas as pl
from jax.experimental.pallas import tpu as pltpu
from jax.sharding import PartitionSpec as P

SWEEPS = 4
RELAX = 0.6
PRESSURE_RATE = 0.25
GRAVITY = 1.0
STRAIN_SCALE = 0.5

BX, BY, BZ = 4, 4, 8
PLANE = BX * BY
ROWS = 3 * PLANE
LANES = 128
GROUP = LANES // BZ
HALF = 8

f32, bf16 = jnp.float32, jnp.bfloat16


def vmem_limit(mib):
    return pltpu.CompilerParams(vmem_limit_bytes=mib * 1024 * 1024)


def pick_body(asked, vel, out, table):
    size_x, size_y, size_z = vel.shape[1:]
    bricks_y, halves = size_y // BY, size_z // LANES

    def repack(block_x, carry):
        for block_y in range(bricks_y):
            for half in range(halves):
                place = (block_x * bricks_y + block_y) * halves + half
                for c in range(3):
                    for i in range(BX):
                        row = (c * BX + i) * BY
                        table[place, row : row + BY, :] = vel[
                            c,
                            block_x * BX + i,
                            block_y * BY : (block_y + 1) * BY,
                            half * LANES : (half + 1) * LANES,
                        ]
        return carry

    lax.fori_loop(0, size_x // BX, repack, 0)
    groups = out.shape[1]
    lane_slot = lax.broadcasted_iota(jnp.int32, (ROWS, LANES), 1) // BZ

    def one_group(step, carry):
        device, group = step // groups, step % groups
        packed = jnp.zeros((ROWS, LANES), f32)
        for slot in range(GROUP):
            brick = asked[device, group * GROUP + slot]
            shift = (BZ * slot - BZ * (brick % GROUP) + LANES) % LANES
            rolled = pltpu.roll(table[brick // GROUP], shift, 1)
            packed = jnp.where(lane_slot == slot, rolled, packed)
        out[device, group] = packed
        return carry

    lax.fori_loop(0, out.shape[0] * groups, one_group, 0)


def pick_bricks(asked, velocity):
    devices, slots = asked.shape
    size_x, size_y, size_z = velocity.shape[1:]
    places = (size_x // BX) * (size_y // BY) * (size_z // LANES)
    return pl.pallas_call(
        pick_body,
        out_shape=jax.ShapeDtypeStruct((devices, slots // GROUP, ROWS, LANES), f32),
        in_specs=[
            pl.BlockSpec(memory_space=pltpu.SMEM),
            pl.BlockSpec(memory_space=pltpu.VMEM),
        ],
        out_specs=pl.BlockSpec(memory_space=pltpu.VMEM),
        scratch_shapes=[pltpu.VMEM((places, ROWS, LANES), f32)],
        compiler_params=vmem_limit(32),
        name="pick_bricks",
    )(asked, velocity)


def permutations():
    spread = np.zeros((2, 2, LANES, 4 * BZ * HALF), np.float32)
    gather = np.zeros((2, 2 * BZ * HALF, LANES), np.float32)
    for half in range(2):
        for slot in range(HALF):
            for z in range(BZ):
                outer, inner = (half * HALF + slot) * BZ + z, z * HALF + slot
                for part in range(4):
                    spread[half, part // 2, outer, part * BZ * HALF + inner] = 1
                for part in range(2):
                    gather[half, part * BZ * HALF + inner, outer] = 1
    return jnp.asarray(spread, bf16), jnp.asarray(gather, bf16)


def split(value):
    high = value.astype(bf16)
    return high, (value - high.astype(f32)).astype(bf16)


def axis_weights(position, cells):
    offsets = [position - (i + 0.5) for i in range(cells)]
    bells = [jnp.exp(-offset * offset) for offset in offsets]
    scale = 1.0 / functools.reduce(jnp.add, bells)
    weights = [bell * scale for bell in bells]
    mean = functools.reduce(jnp.add, [w * offset for w, offset in zip(weights, offsets)])
    slopes = [w * (2.0 * (mean - offset)) for w, offset in zip(weights, offsets)]
    return weights, slopes


def dot(a, b):
    return jnp.dot(a, b, preferred_element_type=f32)


def marker_half(half, live_count, spread, gather, places, start, dens, brick, visc_out, work):
    permuted, left, right, products, heights, lows = work
    lo, hi = half * HALF, (half + 1) * HALF
    markers = places.shape[-1]
    brick_high, brick_low = split(brick)
    permuted[...] = dot(brick_high, spread[half, 0]) + dot(brick_low, spread[half, 1])
    lane = lax.broadcasted_iota(jnp.int32, (HALF, 4 * BZ * HALF), 1)
    sub = lax.broadcasted_iota(jnp.int32, (HALF, 4 * BZ * HALF), 0)
    own = (lane % HALF == sub).astype(f32)
    for row in range(0, ROWS, 2):
        pair = [
            jnp.broadcast_to(permuted[r : r + 1, :], own.shape) * own for r in (row, row + 1)
        ]
        left[row * HALF : (row + 2) * HALF, :] = jnp.concatenate(pair, axis=0).astype(bf16)

    weight_x, slope_x = axis_weights(places[0, 0, lo:hi, :] * BX, BX)
    weight_y, slope_y = axis_weights(places[0, 1, lo:hi, :] * BY, BY)
    weight_z, slope_z = axis_weights(places[0, 2, lo:hi, :] * BZ, BZ)
    part_rows = BZ * HALF
    for z in range(0, BZ, 2):
        rows = slice(z * HALF, (z + 2) * HALF)
        for column, values in ((0, weight_z), (1, slope_z)):
            high, low = split(jnp.concatenate(values[z : z + 2], axis=0))
            columns = slice(column * markers, (column + 1) * markers)
            for part in range(4):
                begin = part * part_rows + z * HALF
                right[begin : begin + 2 * HALF, columns] = low if part % 2 else high
    products[...] = dot(left[...], right[...])

    grads = []
    for c in range(3):
        along_x = along_y = along_z = None
        for i in range(BX):
            sum_w = sum_d = sum_r = None
            for j in range(BY):
                row = ((c * BX + i) * BY + j) * HALF
                still = products[row : row + HALF, :markers]
                rising = products[row : row + HALF, markers:]
                terms = (weight_y[j] * still, slope_y[j] * still, weight_y[j] * rising)
                if j == 0:
                    sum_w, sum_d, sum_r = terms
                else:
                    sum_w, sum_d, sum_r = sum_w + terms[0], sum_d + terms[1], sum_r + terms[2]
            terms = (slope_x[i] * sum_w, weight_x[i] * sum_d, weight_x[i] * sum_r)
            if i == 0:
                along_x, along_y, along_z = terms
            else:
                along_x, along_y, along_z = (
                    along_x + terms[0],
                    along_y + terms[1],
                    along_z + terms[2],
                )
        grads.append((along_x, along_y, along_z))
    normal = grads[0][0] ** 2 + grads[1][1] ** 2 + grads[2][2] ** 2
    shear_xy = 0.5 * (grads[0][1] + grads[1][0])
    shear_xz = 0.5 * (grads[0][2] + grads[2][0])
    shear_yz = 0.5 * (grads[1][2] + grads[2][1])
    invariant = 0.5 * normal + shear_xy**2 + shear_xz**2 + shear_yz**2
    third = jnp.log(1.0 + invariant * (1.0 / (STRAIN_SCALE * STRAIN_SCALE))) * (1.0 / 3.0)
    first = start[0, lo:hi, :]
    weakened = first * jnp.exp(-third)
    slot = lax.broadcasted_iota(jnp.int32, first.shape, 0) + lo
    live = slot < live_count
    visc_out[0, lo:hi, :] = jnp.where(live, weakened, 0.0)
    filled = live.astype(f32)
    carried = (filled, filled * (jnp.log(first) - third), filled * dens[0, lo:hi, :])

    for c in range(3):
        for i in range(BX):
            line = carried[c] * weight_x[i]
            for j in range(0, BY, 2):
                row = ((c * BX + i) * BY + j) * HALF
                pair = jnp.concatenate([line * weight_y[j], line * weight_y[j + 1]], axis=0)
                high, low = split(pair)
                heights[row : row + 2 * HALF, :] = high
                lows[row : row + 2 * HALF, :] = low
    vertical = right[: 2 * part_rows, :markers]
    contract = (((1,), (1,)), ((), ()))
    sums = lax.dot_general(
        heights[...], vertical, contract, preferred_element_type=f32
    ) + lax.dot_general(lows[...], vertical, contract, preferred_element_type=f32)
    chosen = sums.reshape(ROWS, HALF, 2 * part_rows) * own[None, :, : 2 * part_rows]
    moments = jnp.sum(chosen, axis=1)
    high, low = split(moments)
    return dot(high, gather[half]) + dot(low, gather[half])


def marker_body(counts, spread, gather, places, start, dens, brick, visc_out, moments_out, *work):
    owner, group = pl.program_id(0), pl.program_id(1)
    live_count = counts[0, owner] - group * GROUP

    @pl.when(live_count <= 0)
    def _():
        visc_out[...] = jnp.zeros_like(visc_out)
        moments_out[...] = jnp.zeros_like(moments_out)

    @pl.when(live_count > 0)
    def _():
        total = None
        for half in range(2):
            part = marker_half(
                half, live_count, spread, gather, places, start, dens, brick[0, 0], visc_out, work
            )
            total = part if total is None else total + part
        moments_out[0, 0] = total


def marker_work(counts, positions, start_visc, marker_dens, bricks):
    owners, _, slots, markers = positions.shape
    groups = slots // GROUP
    spread, gather = permutations()
    width = 4 * BZ * HALF
    return pl.pallas_call(
        marker_body,
        grid=(owners, groups),
        out_shape=(
            jax.ShapeDtypeStruct((owners, slots, markers), f32),
            jax.ShapeDtypeStruct((owners, groups, ROWS, LANES), f32),
        ),
        in_specs=[
            pl.BlockSpec(memory_space=pltpu.SMEM),
            pl.BlockSpec(spread.shape, lambda q, g: (0, 0, 0, 0)),
            pl.BlockSpec(gather.shape, lambda q, g: (0, 0, 0)),
            pl.BlockSpec((1, 3, GROUP, markers), lambda q, g: (q, 0, g, 0)),
            pl.BlockSpec((1, GROUP, markers), lambda q, g: (q, g, 0)),
            pl.BlockSpec((1, GROUP, markers), lambda q, g: (q, g, 0)),
            pl.BlockSpec((1, 1, ROWS, LANES), lambda q, g: (q, g, 0, 0)),
        ],
        out_specs=(
            pl.BlockSpec((1, GROUP, markers), lambda q, g: (q, g, 0)),
            pl.BlockSpec((1, 1, ROWS, LANES), lambda q, g: (q, g, 0, 0)),
        ),
        scratch_shapes=[
            pltpu.VMEM((ROWS, width), f32),
            pltpu.VMEM((ROWS * HALF, width), bf16),
            pltpu.VMEM((width, 2 * markers), bf16),
            pltpu.VMEM((ROWS * HALF, 2 * markers), f32),
            pltpu.VMEM((ROWS * HALF, markers), bf16),
            pltpu.VMEM((ROWS * HALF, markers), bf16),
        ],
        compiler_params=vmem_limit(32),
        name="marker_work",
    )(counts, spread, gather, positions, start_visc, marker_dens, bricks)


def settle_body(asked, moments, visc, dens, visc_out, dens_out, table):
    size_x, size_y, size_z = visc.shape
    bricks_y, halves = size_y // BY, size_z // LANES
    table[...] = jnp.zeros_like(table)
    groups = moments.shape[1]
    lane_slot = lax.broadcasted_iota(jnp.int32, (ROWS, LANES), 1) // BZ

    def one_group(step, carry):
        device, group = step // groups, step % groups
        packed = moments[device, group]
        for slot in range(GROUP):
            brick = asked[device, group * GROUP + slot]
            shift = (BZ * (brick % GROUP) - BZ * slot + LANES) % LANES
            piece = pltpu.roll(jnp.where(lane_slot == slot, packed, 0.0), shift, 1)
            place = brick // GROUP
            table[place] = table[place] + piece
        return carry

    lax.fori_loop(0, moments.shape[0] * groups, one_group, 0)

    def finish(block_x, carry):
        for block_y in range(bricks_y):
            for half in range(halves):
                place = (block_x * bricks_y + block_y) * halves + half
                for i in range(BX):
                    here = (
                        block_x * BX + i,
                        slice(block_y * BY, (block_y + 1) * BY),
                        slice(half * LANES, (half + 1) * LANES),
                    )
                    sums = [
                        table[place, (c * BX + i) * BY : (c * BX + i + 1) * BY, :]
                        for c in range(3)
                    ]
                    scale = 1.0 / (sums[0] + 1.0)
                    visc_out[here] = jnp.exp((sums[1] + jnp.log(visc[here])) * scale)
                    dens_out[here] = (sums[2] + dens[here]) * scale
        return carry

    lax.fori_loop(0, size_x // BX, finish, 0)


def settle(asked, moments, cell_visc, cell_dens):
    size_x, size_y, size_z = cell_visc.shape
    places = (size_x // BX) * (size_y // BY) * (size_z // LANES)
    whole = pl.BlockSpec(memory_space=pltpu.VMEM)
    shape = jax.ShapeDtypeStruct(cell_visc.shape, f32)
    return pl.pallas_call(
        settle_body,
        out_shape=(shape, shape),
        in_specs=[pl.BlockSpec(memory_space=pltpu.SMEM), whole, whole, whole],
        out_specs=(whole, whole),
        scratch_shapes=[pltpu.VMEM((places, ROWS, LANES), f32)],
        compiler_params=vmem_limit(32),
        name="settle",
    )(asked, moments, cell_visc, cell_dens)


def sweep_body(vel, pres, visc, dens, low_x, high_x, side_y, vel_out, pres_out, *work):
    fields, coefs, rate, relax, forcing = work
    size_x, size_y, size_z = visc.shape
    width = low_x.shape[1]
    long_x = size_x + 2 * width
    ring = fields.shape[3]
    inner = slice(width, width + size_x)
    own = slice(0, size_y)
    for c in range(3):
        fields[0, c, inner, own, :] = vel[c]
    fields[0, 3, inner, own, :] = pres[...]
    fields[1, 0, inner, own, :] = visc[...]
    fields[1, 1, inner, own, :] = dens[...]
    for f in range(6):
        slot = (0, f) if f < 4 else (1, f - 4)
        fields[slot[0], slot[1], :width, own, :] = low_x[f]
        fields[slot[0], slot[1], width + size_x :, own, :] = high_x[f]
        fields[slot[0], slot[1], :, size_y:, :] = side_y[f]

    lane = lax.broadcasted_iota(jnp.int32, (ring, size_z), 1)
    not_last = (lane < size_z - 1).astype(f32)
    not_first = (lane > 0).astype(f32)

    def up_y(a):
        return pltpu.roll(a, ring - 1, 0)

    def down_y(a):
        return pltpu.roll(a, 1, 0)

    def up_z(a):
        return pltpu.roll(a, size_z - 1, 1)

    def down_z(a):
        return pltpu.roll(a, 1, 1)

    def prepare(i, carry):
        here = fields[1, 0, i]
        near = [
            fields[1, 0, i + 1],
            fields[1, 0, i - 1],
            up_y(here),
            down_y(here),
            up_z(here) * not_last,
            down_z(here) * not_first,
        ]
        links = [0.5 * (here + other) for other in near]
        diagonal = functools.reduce(jnp.add, links)
        scale = jnp.where(here > 0.0, RELAX / diagonal, 0.0)
        links[4] = links[4] * not_last
        links[5] = links[5] * not_first
        for n in range(6):
            coefs[n, i] = links[n] * scale
        relax[i] = scale
        forcing[i] = fields[1, 1, i] * (-GRAVITY * scale)
        rate[i] = PRESSURE_RATE * here
        return carry

    lax.fori_loop(1, long_x - 1, prepare, 0)

    for sweep in range(SWEEPS):
        old, new = sweep % 2, (sweep + 1) % 2
        last = sweep == SWEEPS - 1

        def one_plane(i, carry, old=old, new=new, last=last):
            pressure = fields[old, 3, i]
            links = [coefs[n, i] for n in range(6)]
            scale = relax[i]
            before = (
                fields[old, 3, i - 1],
                down_y(pressure),
                down_z(pressure) * not_first,
            )
            divergence = None
            for c in range(3):
                here = fields[old, c, i]
                near = [
                    fields[old, c, i + 1],
                    fields[old, c, i - 1],
                    up_y(here),
                    down_y(here),
                    up_z(here),
                    down_z(here),
                ]
                total = (1.0 - RELAX) * here - scale * (pressure - before[c])
                for link, other in zip(links, near):
                    total = total + link * other
                ahead = near[2 * c]
                if c == 2:
                    total = total + forcing[i]
                    ahead = ahead * not_last
                change = ahead - here
                divergence = change if divergence is None else divergence + change
                if last:
                    vel_out[c, i - width] = total[:size_y]
                else:
                    fields[new, c, i] = total
            pressed = pressure - rate[i] * divergence
            if last:
                pres_out[i - width] = pressed[:size_y]
            else:
                fields[new, 3, i] = pressed
            return carry

        lax.fori_loop(1 + sweep, long_x - 1 - sweep, one_plane, 0)


def all_sweeps(velocity, pressure, cell_visc, cell_dens, low_x, high_x, side_y):
    size_x, size_y, size_z = cell_visc.shape
    width = low_x.shape[1]
    long_x, ring = size_x + 2 * width, size_y + side_y.shape[2]
    whole = pl.BlockSpec(memory_space=pltpu.VMEM)
    block = (long_x, ring, size_z)
    return pl.pallas_call(
        sweep_body,
        out_shape=(
            jax.ShapeDtypeStruct(velocity.shape, f32),
            jax.ShapeDtypeStruct(pressure.shape, f32),
        ),
        in_specs=[whole] * 7,
        out_specs=(whole, whole),
        scratch_shapes=[
            pltpu.VMEM((2, 4) + block, f32),
            pltpu.VMEM((6,) + block, f32),
            pltpu.VMEM(block, f32),
            pltpu.VMEM(block, f32),
            pltpu.VMEM(block, f32),
        ],
        compiler_params=vmem_limit(48),
        name="all_sweeps",
    )(velocity, pressure, cell_visc, cell_dens, low_x, high_x, side_y)


def shift(value, axis, step):
    size = lax.axis_size(axis)
    pairs = [(i, i + step) for i in range(size) if 0 <= i + step < size]
    return lax.ppermute(value, axis, pairs)


def per_device(
    velocity,
    pressure,
    cell_visc,
    cell_dens,
    block_brick,
    block_counts,
    positions,
    start_visc,
    marker_dens,
):
    width = SWEEPS
    size_x, size_y, _ = cell_visc.shape
    asked = lax.all_to_all(block_brick, "mark", 0, 0, tiled=True)

    fields = (velocity, pressure[None], cell_visc[None], cell_dens[None])
    low_x = shift(jnp.concatenate([f[:, size_x - width :] for f in fields]), "grid", 1)
    high_x = shift(jnp.concatenate([f[:, :width] for f in fields]), "grid", -1)

    def face_y(rows):
        own = jnp.concatenate([f[:, :, rows] for f in fields])
        return jnp.concatenate([low_x[:, :, rows], own, high_x[:, :, rows]], axis=1)

    low_y = shift(face_y(slice(size_y - width, size_y)), "mark", 1)
    high_y = shift(face_y(slice(0, width)), "mark", -1)
    side_y = jnp.concatenate([high_y, low_y], axis=2)

    picked = pick_bricks(asked, velocity)
    bricks = lax.all_to_all(picked, "mark", 0, 0, tiled=True)
    marker_visc, moments = marker_work(
        block_counts, positions, start_visc, marker_dens, bricks
    )
    gathered = lax.all_to_all(moments, "mark", 0, 0, tiled=True)
    velocity_next, pressure_next = all_sweeps(
        velocity, pressure, cell_visc, cell_dens, low_x, high_x, side_y
    )
    visc_next, dens_next = settle(asked, gathered, cell_visc, cell_dens)
    return velocity_next, pressure_next, visc_next, dens_next, marker_visc


def solution(mesh):
    in_specs = (
        P(None, "grid", "mark", None),
        P("grid", "mark", None),
        P("grid", "mark", None),
        P("grid", "mark", None),
        P(("grid", "mark"), None),
        P(("grid", "mark"), None),
        P(("grid", "mark"), None, None, None),
        P(("grid", "mark"), None, None),
        P(("grid", "mark"), None, None),
    )
    out_specs = (
        P(None, "grid", "mark", None),
        P("grid", "mark", None),
        P("grid", "mark", None),
        P("grid", "mark", None),
        P(("grid", "mark"), None, None),
    )
    return jax.shard_map(
        per_device, mesh=mesh, in_specs=in_specs, out_specs=out_specs, check_vma=False
    )
```

time: 846 us -> 131 us (0.15)
  the two profiles are of different devices: /device:TPU:18 before, /device:TPU:0 now
where the time goes in v1:
time: 131 us
  Pallas kernels  60.7 us (46%)
  starting transfers between devices  41.2 us (31%)
  local copies, waits for them, and re-layouts  12.1 us (9%)
  waiting for transfers between devices  9.05 us (7%)
  other arithmetic  6.9 us (5%)
    pallas_call x1, Pallas kernels, all_sweeps(): pl.pallas_call(sweep_body, out_shape=(jax.ShapeDtypeStruct(velocity.shape...  23.4 us
    pallas_call x1, Pallas kernels, marker_work(): pl.pallas_call(marker_body, grid=(owners, groups), out_shape=(jax.ShapeDt...  22.4 us
    all_to_all x1, starting transfers between devices, per_device(): gathered = lax.all_to_all(moments, 'mark', 0, 0, tiled=True)  18.5 us
    ppermute x4, starting transfers between devices, shift(): return lax.ppermute(value, axis, pairs)  11.8 us
    pallas_call x1, Pallas kernels, settle(): pl.pallas_call(settle_body, out_shape=(shape, shape), in_specs=[pl.BlockS...  8.18 us
    all_to_all x1, starting transfers between devices, per_device(): asked = lax.all_to_all(block_brick, 'mark', 0, 0, tiled=True)  7.3 us
    pallas_call x1, Pallas kernels, pick_bricks(): pl.pallas_call(pick_body, out_shape=jax.ShapeDtypeStruct((devices, slots...  6.67 us
    unnamed x34, local copies, waits for them, and re-layouts  4.97 us
  transfers between devices with their start and end apart: 7, of which 2 were waited for; matrix products, arithmetic and copies ran while one was open for 8% of the time, Pallas kernels for 40%

profile of v1, /device:TPU:0, one launch (start us, length us, event | category | flops | bytes accessed | tf_op | source)
XLA Modules:
  0.0 130.7 jit_solution(5329428956721883402)
XLA Ops:
  0.6 1.0 fusion.7
  1.6 1.1 fusion.1
  4.5 1.3 collective-permute-start.1
  6.5 3.8 %collective-permute-start = (f32[6,4,16,256]{3,2,1,0:T(8,128)}, f32[6,4,16,256]{3,2,1,0:T(8,128)}, u32[]{:S(2)}, u32[]{:S(2)}) collective-permute-start(f32[6,4,16,256]{3,2,1,0:T(8,128)} %pad_maximum_fusion.3), channel_id=1, source_target_pairs={{0,8},{8,16},{16,24},{1,9},{9,17},{17,25},{2,10},{10,18},{18,26},{... | collective-permute-start | bytes 1179656 | tf_op jit(solution)/shard_map/ppermute | solution.py:457
  10.3 7.3 %all-to-all-start = ((s32[8,1,48]{2,1,0:T(1,128)}), s32[8,1,48]{2,1,0:T(1,128)S(1)}, u32[]{:S(2)}, u32[]{:S(2)}) async-start(s32[8,1,48]{2,1,0:T(1,128)} %bitcast.3), calls=%async_computation | async-start | bytes 8192 | tf_op jit(solution)/shard_map/all_to_all | solution.py:473
  17.6 1.0 fusion
  19.5 4.5 %all-to-all-done = s32[8,1,48]{2,1,0:T(1,128)S(1)} async-done(((s32[8,1,48]{2,1,0:T(1,128)}), s32[8,1,48]{2,1,0:T(1,128)S(1)}, u32[]{:S(2)}, u32[]{:S(2)}) %all-to-all-start) | async-done | bytes 1568 | tf_op jit(solution)/shard_map/all_to_all | solution.py:473
  24.0 6.7 %pick_bricks.1 = f32[8,3,48,128]{3,2,1,0:T(8,128)S(1)} custom-call(s32[8,48]{1,0:T(8,128)S(1)} %bitcast.11, f32[3,32,16,256]{3,2,1,0:T(8,128)S(1)} %copy-done), custom_call_target="tpu_custom_call" | custom-call | tf_op jit(solution)/shard_map/pick_bricks/pallas_call | solution.py:72
  31.5 3.5 %all-to-all-start.1 = ((f32[8,3,48,128]{3,2,1,0:T(8,128)}), f32[8,3,48,128]{3,2,1,0:T(8,128)S(1)}, u32[]{:S(2)}, u32[]{:S(2)}) async-start(f32[8,3,48,128]{3,2,1,0:T(8,128)} %copy-done.3), calls=%async_computation.1 | async-start | bytes 1179648 | tf_op jit(solution)/shard_map/all_to_all | solution.py:488
  35.2 1.1 fusion.9
  36.3 1.1 fusion.8
  37.4 2.2 %pad_maximum_fusion.1 = f32[6,40,4,256]{3,2,1,0:T(4,128)} fusion(f32[6,4,4,256]{3,2,1,0:T(4,128)S(1)} %get-tuple-element.35, f32[1,32,4,256]{3,2,1,0:T(4,128)S(1)} %get-tuple-element.25, f32[1,32,4,256]{3,2,1,0:T(4,128)} %get-tuple-element.40, f32[1,32,4,256]{3,2,1,0:T(4,128)} %get-tuple-element.21, f32[3,32,4,256]{3,2,1,0:T(4,128)S(1)} %copy-done.14, ...), kind=kLoop, calls=%fused_computation.1 | loop fusion | flops 1228800 | bytes 1966080 | tf_op jit(solution)/shard_map/concatenate | solution.py:481
  39.6 1.3 collective-permute-start.2
  40.9 1.2 pad_maximum_fusion.2
  42.1 5.5 %collective-permute-start.3 = (f32[6,40,4,256]{3,2,1,0:T(4,128)}, f32[6,40,4,256]{3,2,1,0:T(4,128)}, u32[]{:S(2)}, u32[]{:S(2)}) collective-permute-start(f32[6,40,4,256]{3,2,1,0:T(4,128)} %pad_maximum_fusion.2), channel_id=1, source_target_pairs={{0,1},{1,2},{2,3},{3,4},{4,5},{5,6},{6,7},{8,9},{9,10},{10,11},{11... | collective-permute-start | bytes 2949128 | tf_op jit(solution)/shard_map/ppermute | solution.py:457
  47.6 4.5 %all-to-all-done.1.brick = f32[8,3,48,128]{3,2,1,0:T(8,128)S(1)} async-done(((f32[8,3,48,128]{3,2,1,0:T(8,128)}), f32[8,3,48,128]{3,2,1,0:T(8,128)S(1)}, u32[]{:S(2)}, u32[]{:S(2)}) %all-to-all-start.1) | async-done | bytes 589856 | tf_op jit(solution)/shard_map/all_to_all | solution.py:488
  52.2 1.3 copy-done.6
  53.4 1.0 copy-done.8
  54.4 1.0 copy-done.9
  55.4 22.4 %marker_work.1 = (f32[8,48,256]{2,1,0:T(8,128)}, f32[8,3,48,128]{3,2,1,0:T(8,128)S(1)}) custom-call(s32[1,8]{1,0:T(1,128)S(1)} %copy-done.12, bf16[2,2,128,256]{3,2,1,0:T(8,128)(2,1)S(1)} %copy-done.10, bf16[2,128,128]{2,1,0:T(8,128)(2,1)S(1)} %copy-done.11, f32[8,3,48,256]{3,2,1,0:T(8,128)S(1)} %copy-done.6, f32[8,48,256]{2,1,0:T(8,128)S(1)} %copy-done.8, ...), custom_call_target="tpu_custom_call" | custom-call | tf_op jit(solution)/shard_map/marker_work/pallas_call | solution.py:231
  78.6 18.5 %all-to-all-start.2 = ((f32[8,3,48,128]{3,2,1,0:T(8,128)}), f32[8,3,48,128]{3,2,1,0:T(8,128)S(1)}, u32[]{:S(2)}, u32[]{:S(2)}) async-start(f32[8,3,48,128]{3,2,1,0:T(8,128)} %copy-done.7), calls=%async_computation.2 | async-start | bytes 1179648 | tf_op jit(solution)/shard_map/all_to_all | solution.py:492
  97.2 2.0 %pad_maximum_fusion.side_y = f32[6,40,8,256]{3,2,1,0:T(8,128)S(1)} fusion(f32[6,40,4,256]{3,2,1,0:T(4,128)} %collective-permute-done.3, f32[6,40,4,256]{3,2,1,0:T(4,128)} %collective-permute-done.2), kind=kLoop, calls=%fused_computation | loop fusion | flops 491520 | bytes 3932160 | tf_op jit(solution)/shard_map/concatenate | solution.py:485
  99.1 23.4 %all_sweeps.1 = (f32[3,32,16,256]{3,2,1,0:T(8,128)}, f32[32,16,256]{2,1,0:T(8,128)}) custom-call(f32[3,32,16,256]{3,2,1,0:T(8,128)S(1)} %copy-done, f32[32,16,256]{2,1,0:T(8,128)S(1)} %copy-done.5, f32[32,16,256]{2,1,0:T(8,128)S(1)} %copy-done.2, f32[32,16,256]{2,1,0:T(8,128)S(1)} %copy-done.1, f32[6,4,16,256]{3,2,1,0:T(8,128)} %collective-permute-done.low_x, ...), custom_call_target="tpu_custom_call" | custom-call | tf_op jit(solution)/shard_map/all_sweeps/pallas_call | solution.py:434
  122.5 8.2 %settle.1 = (f32[32,16,256]{2,1,0:T(8,128)}, f32[32,16,256]{2,1,0:T(8,128)}) custom-call(s32[8,48]{1,0:T(8,128)S(1)} %bitcast.12, f32[8,3,48,128]{3,2,1,0:T(8,128)S(1)} %all-to-all-done.2.moments, f32[32,16,256]{2,1,0:T(8,128)S(1)} %copy-done.2, f32[32,16,256]{2,1,0:T(8,128)S(1)} %copy-done.1), custom_call_target="tpu_custom_call" | custom-call | tf_op jit(solution)/shard_map/settle/pallas_call | solution.py:311
  (41 shorter events, 5.1 us)
Async XLA Ops:
  0.6 17.0 %copy-start = (f32[3,32,16,256]{3,2,1,0:T(8,128)S(1)}, f32[3,32,16,256]{3,2,1,0:T(8,128)}, u32[]{:S(2)}) copy-start(f32[3,32,16,256]{3,2,1,0:T(8,128)} %vel.3) | copy-start | bytes 4718596
  3.7 15.0 %copy-start.2 = (f32[32,16,256]{2,1,0:T(8,128)S(1)}, f32[32,16,256]{2,1,0:T(8,128)}, u32[]{:S(2)}) copy-start(f32[32,16,256]{2,1,0:T(8,128)} %visc.3) | copy-start | bytes 1572868
  3.7 15.0 %copy-start.4 = (f32[32,16,256]{2,1,0:T(8,128)S(1)}, f32[32,16,256]{2,1,0:T(8,128)}, u32[]{:S(2)}) copy-start(f32[32,16,256]{2,1,0:T(8,128)} %pres.1) | copy-start | bytes 1572868
  4.5 30.7 %collective-permute-start.1 = (f32[6,4,16,256]{3,2,1,0:T(8,128)}, f32[6,4,16,256]{3,2,1,0:T(8,128)}, u32[]{:S(2)}, u32[]{:S(2)}) collective-permute-start(f32[6,4,16,256]{3,2,1,0:T(8,128)} %pad_maximum_fusion.4), channel_id=1, source_target_pairs={{8,0},{16,8},{24,16},{9,1},{17,9},{25,17},{10,2},{18,10},{26,18},{... | collective-permute-start | bytes 1179656 | tf_op jit(solution)/shard_map/ppermute | solution.py:457
  6.5 29.8 %collective-permute-start = (f32[6,4,16,256]{3,2,1,0:T(8,128)}, f32[6,4,16,256]{3,2,1,0:T(8,128)}, u32[]{:S(2)}, u32[]{:S(2)}) collective-permute-start(f32[6,4,16,256]{3,2,1,0:T(8,128)} %pad_maximum_fusion.3), channel_id=1, source_target_pairs={{0,8},{8,16},{16,24},{1,9},{9,17},{17,25},{2,10},{10,18},{18,26},{... | collective-permute-start | bytes 1179656 | tf_op jit(solution)/shard_map/ppermute | solution.py:457
  10.3 13.7 %all-to-all-start = ((s32[8,1,48]{2,1,0:T(1,128)}), s32[8,1,48]{2,1,0:T(1,128)S(1)}, u32[]{:S(2)}, u32[]{:S(2)}) async-start(s32[8,1,48]{2,1,0:T(1,128)} %bitcast.3), calls=%async_computation | async-start | bytes 8192 | tf_op jit(solution)/shard_map/all_to_all | solution.py:473
  24.0 11.0 %copy-start.1 = (f32[32,16,256]{2,1,0:T(8,128)S(1)}, f32[32,16,256]{2,1,0:T(8,128)}, u32[]{:S(2)}) copy-start(f32[32,16,256]{2,1,0:T(8,128)} %dens.5) | copy-start | bytes 1572868
  30.7 0.8 copy-start.3
  31.5 20.6 %all-to-all-start.1 = ((f32[8,3,48,128]{3,2,1,0:T(8,128)}), f32[8,3,48,128]{3,2,1,0:T(8,128)S(1)}, u32[]{:S(2)}, u32[]{:S(2)}) async-start(f32[8,3,48,128]{3,2,1,0:T(8,128)} %copy-done.3), calls=%async_computation.1 | async-start | bytes 1179648 | tf_op jit(solution)/shard_map/all_to_all | solution.py:488
  35.0 2.3 %copy-start.14 = (f32[3,32,4,256]{3,2,1,0:T(4,128)S(1)}, f32[3,32,4,256]{3,2,1,0:T(4,128)}, u32[]{:S(2)}) copy-start(f32[3,32,4,256]{3,2,1,0:T(4,128)} %get-tuple-element.17) | copy-start | bytes 1179652
  35.1 5.8 %copy-start.13 = (f32[3,32,4,256]{3,2,1,0:T(4,128)S(1)}, f32[3,32,4,256]{3,2,1,0:T(4,128)}, u32[]{:S(2)}) copy-start(f32[3,32,4,256]{3,2,1,0:T(4,128)} %get-tuple-element.18) | copy-start | bytes 1179652
  35.1 5.8 %copy-start.15 = (f32[1,32,4,256]{3,2,1,0:T(4,128)S(1)}, f32[1,32,4,256]{3,2,1,0:T(4,128)}, u32[]{:S(2)}) copy-start(f32[1,32,4,256]{3,2,1,0:T(4,128)} %get-tuple-element.22) | copy-start | bytes 393220
  35.1 5.8 %copy-start.16 = (f32[1,32,4,256]{3,2,1,0:T(4,128)S(1)}, f32[1,32,4,256]{3,2,1,0:T(4,128)}, u32[]{:S(2)}) copy-start(f32[1,32,4,256]{3,2,1,0:T(4,128)} %get-tuple-element.39) | copy-start | bytes 393220
  37.4 14.8 %copy-start.10 = (bf16[2,2,128,256]{3,2,1,0:T(8,128)(2,1)S(1)}, bf16[2,2,128,256]{3,2,1,0:T(8,128)(2,1)}, u32[]{:S(2)}) copy-start(bf16[2,2,128,256]{3,2,1,0:T(8,128)(2,1)} %constant.4.clone.spread) | copy-start | bytes 786436
  37.4 14.8 %copy-start.11 = (bf16[2,128,128]{2,1,0:T(8,128)(2,1)S(1)}, bf16[2,128,128]{2,1,0:T(8,128)(2,1)}, u32[]{:S(2)}) copy-start(bf16[2,128,128]{2,1,0:T(8,128)(2,1)} %constant.5.clone.gather) | copy-start | bytes 196612
  37.4 14.7 %copy-start.12 = (s32[1,8]{1,0:T(1,128)S(1)}, s32[1,8]{1,0:T(1,128)}, u32[]{:S(2)}) copy-start(s32[1,8]{1,0:T(1,128)} %counts.1) | copy-start | bytes 100
  39.6 57.5 %collective-permute-start.2 = (f32[6,40,4,256]{3,2,1,0:T(4,128)}, f32[6,40,4,256]{3,2,1,0:T(4,128)}, u32[]{:S(2)}, u32[]{:S(2)}) collective-permute-start(f32[6,40,4,256]{3,2,1,0:T(4,128)} %pad_maximum_fusion.1), channel_id=1, source_target_pairs={{1,0},{2,1},{3,2},{4,3},{5,4},{6,5},{7,6},{9,8},{10,9},{11,10},{12... | collective-permute-start | bytes 2949128 | tf_op jit(solution)/shard_map/ppermute | solution.py:457
  42.1 55.0 %collective-permute-start.3 = (f32[6,40,4,256]{3,2,1,0:T(4,128)}, f32[6,40,4,256]{3,2,1,0:T(4,128)}, u32[]{:S(2)}, u32[]{:S(2)}) collective-permute-start(f32[6,40,4,256]{3,2,1,0:T(4,128)} %pad_maximum_fusion.2), channel_id=1, source_target_pairs={{0,1},{1,2},{2,3},{3,4},{4,5},{5,6},{6,7},{8,9},{9,10},{10,11},{11... | collective-permute-start | bytes 2949128 | tf_op jit(solution)/shard_map/ppermute | solution.py:457
  52.1 1.3 copy-start.6
  53.4 1.0 copy-start.8
  54.4 1.0 copy-start.9
  77.8 0.8 copy-start.7
  78.6 43.9 %all-to-all-start.2 = ((f32[8,3,48,128]{3,2,1,0:T(8,128)}), f32[8,3,48,128]{3,2,1,0:T(8,128)S(1)}, u32[]{:S(2)}, u32[]{:S(2)}) async-start(f32[8,3,48,128]{3,2,1,0:T(8,128)} %copy-done.7), calls=%async_computation.2 | async-start | bytes 1179648 | tf_op jit(solution)/shard_map/all_to_all | solution.py:492
  97.1 2.0 %copy-start.5 = (f32[32,16,256]{2,1,0:T(8,128)S(1)}, f32[32,16,256]{2,1,0:T(8,128)}, u32[]{:S(2)}) copy-start(f32[32,16,256]{2,1,0:T(8,128)} %pres.1) | copy-start | bytes 1572868

commit v2 on v1

--- a/solution.py
+++ b/solution.py
@@ -84,16 +84,17 @@
 
 
 def permutations():
-    spread = np.zeros((2, 2, LANES, 4 * BZ * HALF), np.float32)
-    gather = np.zeros((2, 2 * BZ * HALF, LANES), np.float32)
+    inside = BZ * HALF
+    spread = np.zeros((2, 2, LANES, 4 * inside), np.float32)
+    gather = np.zeros((2 * BY * inside, BY * LANES), np.float32)
     for half in range(2):
         for slot in range(HALF):
             for z in range(BZ):
                 outer, inner = (half * HALF + slot) * BZ + z, z * HALF + slot
                 for part in range(4):
-                    spread[half, part // 2, outer, part * BZ * HALF + inner] = 1
-                for part in range(2):
-                    gather[half, part * BZ * HALF + inner, outer] = 1
+                    spread[half, part // 2, outer, part * inside + inner] = 1
+                for j in range(BY):
+                    gather[(half * BY + j) * inside + inner, j * LANES + outer] = 1
     return jnp.asarray(spread, bf16), jnp.asarray(gather, bf16)
 
 
@@ -102,13 +103,27 @@
     return high, (value - high.astype(f32)).astype(bf16)
 
 
-def axis_weights(position, cells):
-    offsets = [position - (i + 0.5) for i in range(cells)]
-    bells = [jnp.exp(-offset * offset) for offset in offsets]
-    scale = 1.0 / functools.reduce(jnp.add, bells)
-    weights = [bell * scale for bell in bells]
-    mean = functools.reduce(jnp.add, [w * offset for w, offset in zip(weights, offsets)])
-    slopes = [w * (2.0 * (mean - offset)) for w, offset in zip(weights, offsets)]
+def add_all(values):
+    return functools.reduce(jnp.add, values)
+
+
+def axis_weights(fraction, cells):
+    middle = (cells - 1) / 2
+    base = jnp.exp(fraction * (2.0 * cells) - float(cells))
+    powers = [None, base]
+    for i in range(2, cells):
+        powers.append(powers[i // 2] * powers[i - i // 2])
+    factors = [float(np.exp(middle**2 - (i - middle) ** 2)) for i in range(cells)]
+    bells = [None] + [powers[i] * factors[i] for i in range(1, cells)]
+    scale = 1.0 / (add_all(bells[1:]) + factors[0])
+    weights = [scale * factors[0]] + [bell * scale for bell in bells[1:]]
+    mean = add_all(
+        [
+            (weights[cells - 1 - i] - weights[i]) * (2.0 * (middle - i))
+            for i in range(cells // 2)
+        ]
+    )
+    slopes = [w * (2.0 * (i - middle) - mean) for i, w in enumerate(weights)]
     return weights, slopes
 
 
@@ -116,111 +131,136 @@
     return jnp.dot(a, b, preferred_element_type=f32)
 
 
-def marker_half(half, live_count, spread, gather, places, start, dens, brick, visc_out, work):
-    permuted, left, right, products, heights, lows = work
-    lo, hi = half * HALF, (half + 1) * HALF
-    markers = places.shape[-1]
-    brick_high, brick_low = split(brick)
-    permuted[...] = dot(brick_high, spread[half, 0]) + dot(brick_low, spread[half, 1])
-    lane = lax.broadcasted_iota(jnp.int32, (HALF, 4 * BZ * HALF), 1)
-    sub = lax.broadcasted_iota(jnp.int32, (HALF, 4 * BZ * HALF), 0)
-    own = (lane % HALF == sub).astype(f32)
-    for row in range(0, ROWS, 2):
-        pair = [
-            jnp.broadcast_to(permuted[r : r + 1, :], own.shape) * own for r in (row, row + 1)
-        ]
-        left[row * HALF : (row + 2) * HALF, :] = jnp.concatenate(pair, axis=0).astype(bf16)
-
-    weight_x, slope_x = axis_weights(places[0, 0, lo:hi, :] * BX, BX)
-    weight_y, slope_y = axis_weights(places[0, 1, lo:hi, :] * BY, BY)
-    weight_z, slope_z = axis_weights(places[0, 2, lo:hi, :] * BZ, BZ)
-    part_rows = BZ * HALF
-    for z in range(0, BZ, 2):
-        rows = slice(z * HALF, (z + 2) * HALF)
-        for column, values in ((0, weight_z), (1, slope_z)):
-            high, low = split(jnp.concatenate(values[z : z + 2], axis=0))
-            columns = slice(column * markers, (column + 1) * markers)
-            for part in range(4):
-                begin = part * part_rows + z * HALF
-                right[begin : begin + 2 * HALF, columns] = low if part % 2 else high
-    products[...] = dot(left[...], right[...])
-
+def gradients(products, weights_x, weights_y, markers):
+    (weight_x, slope_x), (weight_y, slope_y) = weights_x, weights_y
     grads = []
     for c in range(3):
-        along_x = along_y = along_z = None
+        lines = [[], [], []]
         for i in range(BX):
-            sum_w = sum_d = sum_r = None
-            for j in range(BY):
-                row = ((c * BX + i) * BY + j) * HALF
-                still = products[row : row + HALF, :markers]
-                rising = products[row : row + HALF, markers:]
-                terms = (weight_y[j] * still, slope_y[j] * still, weight_y[j] * rising)
-                if j == 0:
-                    sum_w, sum_d, sum_r = terms
-                else:
-                    sum_w, sum_d, sum_r = sum_w + terms[0], sum_d + terms[1], sum_r + terms[2]
-            terms = (slope_x[i] * sum_w, weight_x[i] * sum_d, weight_x[i] * sum_r)
-            if i == 0:
-                along_x, along_y, along_z = terms
-            else:
-                along_x, along_y, along_z = (
-                    along_x + terms[0],
-                    along_y + terms[1],
-                    along_z + terms[2],
-                )
-        grads.append((along_x, along_y, along_z))
-    normal = grads[0][0] ** 2 + grads[1][1] ** 2 + grads[2][2] ** 2
-    shear_xy = 0.5 * (grads[0][1] + grads[1][0])
-    shear_xz = 0.5 * (grads[0][2] + grads[2][0])
-    shear_yz = 0.5 * (grads[1][2] + grads[2][1])
-    invariant = 0.5 * normal + shear_xy**2 + shear_xz**2 + shear_yz**2
-    third = jnp.log(1.0 + invariant * (1.0 / (STRAIN_SCALE * STRAIN_SCALE))) * (1.0 / 3.0)
-    first = start[0, lo:hi, :]
-    weakened = first * jnp.exp(-third)
-    slot = lax.broadcasted_iota(jnp.int32, first.shape, 0) + lo
-    live = slot < live_count
-    visc_out[0, lo:hi, :] = jnp.where(live, weakened, 0.0)
-    filled = live.astype(f32)
-    carried = (filled, filled * (jnp.log(first) - third), filled * dens[0, lo:hi, :])
-
-    for c in range(3):
-        for i in range(BX):
-            line = carried[c] * weight_x[i]
-            for j in range(0, BY, 2):
-                row = ((c * BX + i) * BY + j) * HALF
-                pair = jnp.concatenate([line * weight_y[j], line * weight_y[j + 1]], axis=0)
-                high, low = split(pair)
-                heights[row : row + 2 * HALF, :] = high
-                lows[row : row + 2 * HALF, :] = low
-    vertical = right[: 2 * part_rows, :markers]
+            rows = [((c * BX + i) * BY + j) * HALF for j in range(BY)]
+            still = [products[row : row + HALF, :markers] for row in rows]
+            rising = [products[row : row + HALF, markers:] for row in rows]
+            lines[0].append(slope_x[i] * add_all([w * t for w, t in zip(weight_y, still)]))
+            lines[1].append(weight_x[i] * add_all([w * t for w, t in zip(slope_y, still)]))
+            lines[2].append(weight_x[i] * add_all([w * t for w, t in zip(weight_y, rising)]))
+        grads.append([add_all(line) for line in lines])
+    return grads
+
+
+def marker_halves(halves, live_count, spread, gather, places, start, dens, brick, visc_out, work):
+    permuted, left, right, products, factors, planes_high, planes_low, sums = work
+    markers = places.shape[-1]
+    inside = BZ * HALF
+    lane = lax.broadcasted_iota(jnp.int32, (HALF, 4 * inside), 1)
+    sub = lax.broadcasted_iota(jnp.int32, (HALF, 4 * inside), 0)
+    own = (lane % HALF == sub).astype(f32)
+    parts = split(brick)
+    weights = {}
+    for half in halves:
+        permuted[half] = dot(parts[0], spread[half, 0]) + dot(parts[1], spread[half, 1])
+        lo, hi = half * HALF, (half + 1) * HALF
+        weight_z, slope_z = axis_weights(places[0, 2, lo:hi, :], BZ)
+        for z in range(0, BZ, 2):
+            for column, values in ((0, weight_z), (1, slope_z)):
+                high, low = split(jnp.concatenate(values[z : z + 2], axis=0))
+                columns = slice(column * markers, (column + 1) * markers)
+                for part in range(4):
+                    begin = part * inside + z * HALF
+                    right[half, begin : begin + 2 * HALF, columns] = low if part % 2 else high
+        for row in range(0, ROWS, 2):
+            pair = [
+                jnp.broadcast_to(permuted[half, r : r + 1, :], own.shape) * own
+                for r in (row, row + 1)
+            ]
+            left[half, row * HALF : (row + 2) * HALF, :] = jnp.concatenate(pair, axis=0).astype(
+                bf16
+            )
+        products[half] = dot(left[half], right[half])
+
+        weights_x = axis_weights(places[0, 0, lo:hi, :], BX)
+        weights_y = axis_weights(places[0, 1, lo:hi, :], BY)
+        weights[half] = (weights_x, weights_y)
+        for j in range(BY):
+            for z in range(0, BZ, 2):
+                pair = [weights_y[0][j] * weight_z[z + k] for k in range(2)]
+                rows = slice((j * BZ + z) * HALF, (j * BZ + z + 2) * HALF)
+                high, low = split(jnp.concatenate(pair, axis=0))
+                planes_high[half, rows, :] = high
+                planes_low[half, rows, :] = low
+
     contract = (((1,), (1,)), ((), ()))
-    sums = lax.dot_general(
-        heights[...], vertical, contract, preferred_element_type=f32
-    ) + lax.dot_general(lows[...], vertical, contract, preferred_element_type=f32)
-    chosen = sums.reshape(ROWS, HALF, 2 * part_rows) * own[None, :, : 2 * part_rows]
-    moments = jnp.sum(chosen, axis=1)
-    high, low = split(moments)
-    return dot(high, gather[half]) + dot(low, gather[half])
+    for half in halves:
+        lo, hi = half * HALF, (half + 1) * HALF
+        weights_x, weights_y = weights[half]
+        grads = gradients(products.at[half], weights_x, weights_y, markers)
+        normal = grads[0][0] ** 2 + grads[1][1] ** 2 + grads[2][2] ** 2
+        shear_xy = 0.5 * (grads[0][1] + grads[1][0])
+        shear_xz = 0.5 * (grads[0][2] + grads[2][0])
+        shear_yz = 0.5 * (grads[1][2] + grads[2][1])
+        invariant = 0.5 * normal + shear_xy**2 + shear_xz**2 + shear_yz**2
+        third = jnp.log(1.0 + invariant * (1.0 / (STRAIN_SCALE * STRAIN_SCALE))) * (1.0 / 3.0)
+        first = start[0, lo:hi, :]
+        slot = lax.broadcasted_iota(jnp.int32, first.shape, 0) + lo
+        live = slot < live_count
+        visc_out[0, lo:hi, :] = jnp.where(live, first * jnp.exp(-third), 0.0)
+        carried = (
+            live.astype(f32),
+            jnp.where(live, jnp.log(first) - third, 0.0),
+            jnp.where(live, dens[0, lo:hi, :], 0.0),
+        )
+        count = 3 * BX * HALF
+        for c in range(3):
+            for i in range(0, BX, 2):
+                pair = [carried[c] * weights_x[0][i + k] for k in range(2)]
+                row = (c * BX + i) * HALF
+                high, low = split(jnp.concatenate(pair, axis=0))
+                factors[half, row : row + 2 * HALF, :] = high
+                factors[half, count + row : count + row + 2 * HALF, :] = low
+        both = lax.dot_general(
+            factors[half], planes_high[half], contract, preferred_element_type=f32
+        )
+        rest = lax.dot_general(
+            factors[half, :count], planes_low[half], contract, preferred_element_type=f32
+        )
+        total = both[:count] + both[count:] + rest
+        chosen = total.reshape(3 * BX, HALF, BY * inside) * own[None]
+        packed = jnp.sum(chosen, axis=1)
+        high, low = split(packed)
+        columns = slice(half * BY * inside, (half + 1) * BY * inside)
+        sums[: 3 * BX, columns] = high.astype(f32)
+        sums[16 : 16 + 3 * BX, columns] = low.astype(f32)
 
 
 def marker_body(counts, spread, gather, places, start, dens, brick, visc_out, moments_out, *work):
     owner, group = pl.program_id(0), pl.program_id(1)
     live_count = counts[0, owner] - group * GROUP
+    sums = work[-1]
+
+    def run(halves):
+        marker_halves(
+            halves, live_count, spread, gather, places, start, dens, brick[0, 0], visc_out, work
+        )
+        moved = dot(sums[...].astype(bf16), gather[...])
+        moved = moved[: 3 * BX] + moved[16 : 16 + 3 * BX]
+        for j in range(BY):
+            rows = pl.ds(j, 3 * BX, stride=BY)
+            moments_out[0, 0, rows, :] = moved[:, j * LANES : (j + 1) * LANES]
 
     @pl.when(live_count <= 0)
     def _():
         visc_out[...] = jnp.zeros_like(visc_out)
         moments_out[...] = jnp.zeros_like(moments_out)
 
-    @pl.when(live_count > 0)
+    @pl.when(jnp.logical_and(live_count > 0, live_count <= HALF))
     def _():
-        total = None
-        for half in range(2):
-            part = marker_half(
-                half, live_count, spread, gather, places, start, dens, brick[0, 0], visc_out, work
-            )
-            total = part if total is None else total + part
-        moments_out[0, 0] = total
+        sums[...] = jnp.zeros_like(sums)
+        visc_out[:, HALF:, :] = jnp.zeros((1, HALF, visc_out.shape[-1]), f32)
+        run((0,))
+
+    @pl.when(live_count > HALF)
+    def _():
+        sums[...] = jnp.zeros_like(sums)
+        run((0, 1))
 
 
 def marker_work(counts, positions, start_visc, marker_dens, bricks):
@@ -238,7 +278,7 @@
         in_specs=[
             pl.BlockSpec(memory_space=pltpu.SMEM),
             pl.BlockSpec(spread.shape, lambda q, g: (0, 0, 0, 0)),
-            pl.BlockSpec(gather.shape, lambda q, g: (0, 0, 0)),
+            pl.BlockSpec(gather.shape, lambda q, g: (0, 0)),
             pl.BlockSpec((1, 3, GROUP, markers), lambda q, g: (q, 0, g, 0)),
             pl.BlockSpec((1, GROUP, markers), lambda q, g: (q, g, 0)),
             pl.BlockSpec((1, GROUP, markers), lambda q, g: (q, g, 0)),
@@ -249,14 +289,16 @@
             pl.BlockSpec((1, 1, ROWS, LANES), lambda q, g: (q, g, 0, 0)),
         ),
         scratch_shapes=[
-            pltpu.VMEM((ROWS, width), f32),
-            pltpu.VMEM((ROWS * HALF, width), bf16),
-            pltpu.VMEM((width, 2 * markers), bf16),
-            pltpu.VMEM((ROWS * HALF, 2 * markers), f32),
-            pltpu.VMEM((ROWS * HALF, markers), bf16),
-            pltpu.VMEM((ROWS * HALF, markers), bf16),
+            pltpu.VMEM((2, ROWS, width), f32),
+            pltpu.VMEM((2, ROWS * HALF, width), bf16),
+            pltpu.VMEM((2, width, 2 * markers), bf16),
+            pltpu.VMEM((2, ROWS * HALF, 2 * markers), f32),
+            pltpu.VMEM((2, 2 * 3 * BX * HALF, markers), bf16),
+            pltpu.VMEM((2, BY * BZ * HALF, markers), bf16),
+            pltpu.VMEM((2, BY * BZ * HALF, markers), bf16),
+            pltpu.VMEM((32, 2 * BY * BZ * HALF), f32),
         ],
-        compiler_params=vmem_limit(32),
+        compiler_params=vmem_limit(60),
         name="marker_work",
     )(counts, spread, gather, positions, start_visc, marker_dens, bricks)
 

time: 131 us -> 127 us (0.969)
  the two profiles are of different devices: /device:TPU:0 before, /device:TPU:12 now
where the time goes in v2:
time: 127 us; the launch traced here: 125 us
  Pallas kernels  60.5 us (48%)
  starting transfers between devices  34.4 us (27%)
  waiting for transfers between devices  16.7 us (13%)
  other arithmetic  6.84 us (5%)
  local copies, waits for them, and re-layouts  5.82 us (5%)
    pallas_call x1, Pallas kernels, marker_work(): pl.pallas_call(marker_body, grid=(owners, groups), out_shape=(jax.ShapeDt...  22.8 us
    pallas_call x1, Pallas kernels, all_sweeps(): pl.pallas_call(sweep_body, out_shape=(jax.ShapeDtypeStruct(velocity.shape...  22.1 us
    ppermute x4, waiting for transfers between devices, shift(): return lax.ppermute(value, axis, pairs)  12.8 us
    ppermute x4, starting transfers between devices, shift(): return lax.ppermute(value, axis, pairs)  11 us
    all_to_all x1, starting transfers between devices, per_device(): gathered = lax.all_to_all(moments, 'mark', 0, 0, tiled=True)  10.7 us
    pallas_call x1, Pallas kernels, settle(): pl.pallas_call(settle_body, out_shape=(shape, shape), in_specs=[pl.BlockS...  8.17 us
    pallas_call x1, Pallas kernels, pick_bricks(): pl.pallas_call(pick_body, out_shape=jax.ShapeDtypeStruct((devices, slots...  7.48 us
    all_to_all x1, starting transfers between devices, per_device(): bricks = lax.all_to_all(picked, 'mark', 0, 0, tiled=True)  6.44 us
  transfers between devices with their start and end apart: 7, of which 4 were waited for; matrix products, arithmetic and copies ran while one was open for 6% of the time, Pallas kernels for 42%

profile of v2, /device:TPU:12, one launch (start us, length us, event | category | flops | bytes accessed | tf_op | source)
XLA Modules:
  0.0 125.2 jit_solution(5245024317695255102)
XLA Ops:
  0.6 1.0 fusion.7
  1.6 1.1 fusion.1
  2.7 1.0 fusion.5
  4.5 1.3 %collective-permute-start.1 = (f32[6,4,16,256]{3,2,1,0:T(8,128)}, f32[6,4,16,256]{3,2,1,0:T(8,128)S(1)}, u32[]{:S(2)}, u32[]{:S(2)}) collective-permute-start(f32[6,4,16,256]{3,2,1,0:T(8,128)} %pad_maximum_fusion.4), channel_id=1, source_target_pairs={{8,0},{16,8},{24,16},{9,1},{17,9},{25,17},{10,2},{18,10},{26,18},{... | collective-permute-start | bytes 1179656 | tf_op jit(solution)/shard_map/ppermute | solution.py:499
  6.5 3.0 %collective-permute-start = (f32[6,4,16,256]{3,2,1,0:T(8,128)}, f32[6,4,16,256]{3,2,1,0:T(8,128)S(1)}, u32[]{:S(2)}, u32[]{:S(2)}) collective-permute-start(f32[6,4,16,256]{3,2,1,0:T(8,128)} %pad_maximum_fusion.3), channel_id=1, source_target_pairs={{0,8},{8,16},{16,24},{1,9},{9,17},{17,25},{2,10},{10,18},{18,26},{... | collective-permute-start | bytes 1179656 | tf_op jit(solution)/shard_map/ppermute | solution.py:499
  9.6 6.2 %all-to-all-start = ((s32[8,1,48]{2,1,0:T(1,128)}), s32[8,1,48]{2,1,0:T(1,128)S(1)}, u32[]{:S(2)}, u32[]{:S(2)}) async-start(s32[8,1,48]{2,1,0:T(1,128)} %bitcast.3), calls=%async_computation | async-start | bytes 8192 | tf_op jit(solution)/shard_map/all_to_all | solution.py:515
  15.8 1.0 fusion
  16.8 0.8 fusion.2
  17.6 2.2 %all-to-all-done = s32[8,1,48]{2,1,0:T(1,128)S(1)} async-done(((s32[8,1,48]{2,1,0:T(1,128)}), s32[8,1,48]{2,1,0:T(1,128)S(1)}, u32[]{:S(2)}, u32[]{:S(2)}) %all-to-all-start) | async-done | bytes 1568 | tf_op jit(solution)/shard_map/all_to_all | solution.py:515
  19.9 7.5 %pick_bricks.1 = f32[8,3,48,128]{3,2,1,0:T(8,128)} custom-call(s32[8,48]{1,0:T(8,128)S(1)} %bitcast.11, f32[3,32,16,256]{3,2,1,0:T(8,128)S(1)} %copy-done), custom_call_target="tpu_custom_call" | custom-call | tf_op jit(solution)/shard_map/pick_bricks/pallas_call | solution.py:72
  27.3 6.4 %all-to-all-start.1 = ((f32[8,3,48,128]{3,2,1,0:T(8,128)}), f32[8,3,48,128]{3,2,1,0:T(8,128)}, u32[]{:S(2)}, u32[]{:S(2)}) async-start(f32[8,3,48,128]{3,2,1,0:T(8,128)} %pick_bricks.1), calls=%async_computation.1 | async-start | bytes 1179648 | tf_op jit(solution)/shard_map/all_to_all | solution.py:530
  34.0 0.8 copy-done.10
  34.8 2.2 %pad_maximum_fusion.1 = f32[6,40,4,256]{3,2,1,0:T(4,128)} fusion(f32[6,4,4,256]{3,2,1,0:T(4,128)S(1)} %get-tuple-element.35, f32[1,32,4,256]{3,2,1,0:T(4,128)S(1)} %get-tuple-element.25, f32[1,32,4,256]{3,2,1,0:T(4,128)} %get-tuple-element.40, f32[1,32,4,256]{3,2,1,0:T(4,128)} %get-tuple-element.21, f32[3,32,4,256]{3,2,1,0:T(4,128)S(1)} %copy-done.10, ...), kind=kLoop, calls=%fused_computation.1 | loop fusion | flops 1228800 | bytes 1966080 | tf_op jit(solution)/shard_map/concatenate | solution.py:523
  37.0 2.5 %collective-permute-start.2 = (f32[6,40,4,256]{3,2,1,0:T(4,128)}, f32[6,40,4,256]{3,2,1,0:T(4,128)}, u32[]{:S(2)}, u32[]{:S(2)}) collective-permute-start(f32[6,40,4,256]{3,2,1,0:T(4,128)} %pad_maximum_fusion.1), channel_id=1, source_target_pairs={{1,0},{2,1},{3,2},{4,3},{5,4},{6,5},{7,6},{9,8},{10,9},{11,10},{12... | collective-permute-start | bytes 2949128 | tf_op jit(solution)/shard_map/ppermute | solution.py:499
  39.5 1.2 pad_maximum_fusion.2
  40.7 4.3 %collective-permute-start.3 = (f32[6,40,4,256]{3,2,1,0:T(4,128)}, f32[6,40,4,256]{3,2,1,0:T(4,128)}, u32[]{:S(2)}, u32[]{:S(2)}) collective-permute-start(f32[6,40,4,256]{3,2,1,0:T(4,128)} %pad_maximum_fusion.2), channel_id=1, source_target_pairs={{0,1},{1,2},{2,3},{3,4},{4,5},{5,6},{6,7},{8,9},{9,10},{10,11},{11... | collective-permute-start | bytes 2949128 | tf_op jit(solution)/shard_map/ppermute | solution.py:499
  45.0 1.7 %all-to-all-done.1.brick = f32[8,3,48,128]{3,2,1,0:T(8,128)} async-done(((f32[8,3,48,128]{3,2,1,0:T(8,128)}), f32[8,3,48,128]{3,2,1,0:T(8,128)}, u32[]{:S(2)}, u32[]{:S(2)}) %all-to-all-start.1) | async-done | bytes 589856 | tf_op jit(solution)/shard_map/all_to_all | solution.py:530
  46.7 22.8 %marker_work.1 = (f32[8,48,256]{2,1,0:T(8,128)}, f32[8,3,48,128]{3,2,1,0:T(8,128)}) custom-call(s32[1,8]{1,0:T(1,128)} %counts.1, bf16[2,2,128,256]{3,2,1,0:T(8,128)(2,1)} %constant.4.clone.spread, bf16[512,512]{1,0:T(8,128)(2,1)} %constant.5.clone.gather, f32[8,3,48,256]{3,2,1,0:T(8,128)} %places.1, f32[8,48,256]{2,1,0:T(8,128)} %start.1, ...), custom_call_target="tpu_custom_call" | custom-call | tf_op jit(solution)/shard_map/marker_work/pallas_call | solution.py:271
  69.4 10.7 %all-to-all-start.2 = ((f32[8,3,48,128]{3,2,1,0:T(8,128)}), f32[8,3,48,128]{3,2,1,0:T(8,128)S(1)}, u32[]{:S(2)}, u32[]{:S(2)}) async-start(f32[8,3,48,128]{3,2,1,0:T(8,128)} %get-tuple-element.13), calls=%async_computation.2 | async-start | bytes 1179648 | tf_op jit(solution)/shard_map/all_to_all | solution.py:534
  80.2 7.5 %collective-permute-done.2 = f32[6,40,4,256]{3,2,1,0:T(4,128)} collective-permute-done((f32[6,40,4,256]{3,2,1,0:T(4,128)}, f32[6,40,4,256]{3,2,1,0:T(4,128)}, u32[]{:S(2)}, u32[]{:S(2)}) %collective-permute-start.2) | collective-permute-done | bytes 983072 | tf_op jit(solution)/shard_map/ppermute | solution.py:499
  87.7 5.2 %collective-permute-done.3 = f32[6,40,4,256]{3,2,1,0:T(4,128)} collective-permute-done((f32[6,40,4,256]{3,2,1,0:T(4,128)}, f32[6,40,4,256]{3,2,1,0:T(4,128)}, u32[]{:S(2)}, u32[]{:S(2)}) %collective-permute-start.3) | collective-permute-done | bytes 983072 | tf_op jit(solution)/shard_map/ppermute | solution.py:499
  92.9 1.9 %pad_maximum_fusion.side_y = f32[6,40,8,256]{3,2,1,0:T(8,128)S(1)} fusion(f32[6,40,4,256]{3,2,1,0:T(4,128)} %collective-permute-done.3, f32[6,40,4,256]{3,2,1,0:T(4,128)} %collective-permute-done.2), kind=kLoop, calls=%fused_computation | loop fusion | flops 491520 | bytes 3932160 | tf_op jit(solution)/shard_map/concatenate | solution.py:527
  94.9 22.1 %all_sweeps.1 = (f32[3,32,16,256]{3,2,1,0:T(8,128)}, f32[32,16,256]{2,1,0:T(8,128)}) custom-call(f32[3,32,16,256]{3,2,1,0:T(8,128)S(1)} %copy-done, f32[32,16,256]{2,1,0:T(8,128)S(1)} %copy-done.4, f32[32,16,256]{2,1,0:T(8,128)S(1)} %copy-done.2, f32[32,16,256]{2,1,0:T(8,128)S(1)} %copy-done.1, f32[6,4,16,256]{3,2,1,0:T(8,128)S(1)} %copy-done.8, ...), custom_call_target="tpu_custom_call" | custom-call | tf_op jit(solution)/shard_map/all_sweeps/pallas_call | solution.py:476
  117.0 8.2 %settle.1 = (f32[32,16,256]{2,1,0:T(8,128)}, f32[32,16,256]{2,1,0:T(8,128)}) custom-call(s32[8,48]{1,0:T(8,128)S(1)} %bitcast.12, f32[8,3,48,128]{3,2,1,0:T(8,128)S(1)} %all-to-all-done.2.moments, f32[32,16,256]{2,1,0:T(8,128)S(1)} %copy-done.2, f32[32,16,256]{2,1,0:T(8,128)S(1)} %copy-done.1), custom_call_target="tpu_custom_call" | custom-call | tf_op jit(solution)/shard_map/settle/pallas_call | solution.py:353
  (31 shorter events, 1.7 us)
Async XLA Ops:
  0.6 15.2 %copy-start = (f32[3,32,16,256]{3,2,1,0:T(8,128)S(1)}, f32[3,32,16,256]{3,2,1,0:T(8,128)}, u32[]{:S(2)}) copy-start(f32[3,32,16,256]{3,2,1,0:T(8,128)} %vel.3) | copy-start | bytes 4718596
  3.7 13.2 %copy-start.2 = (f32[32,16,256]{2,1,0:T(8,128)S(1)}, f32[32,16,256]{2,1,0:T(8,128)}, u32[]{:S(2)}) copy-start(f32[32,16,256]{2,1,0:T(8,128)} %visc.3) | copy-start | bytes 1572868
  3.7 13.2 %copy-start.3 = (f32[32,16,256]{2,1,0:T(8,128)S(1)}, f32[32,16,256]{2,1,0:T(8,128)}, u32[]{:S(2)}) copy-start(f32[32,16,256]{2,1,0:T(8,128)} %pres.1) | copy-start | bytes 1572868
  4.5 29.4 %collective-permute-start.1 = (f32[6,4,16,256]{3,2,1,0:T(8,128)}, f32[6,4,16,256]{3,2,1,0:T(8,128)S(1)}, u32[]{:S(2)}, u32[]{:S(2)}) collective-permute-start(f32[6,4,16,256]{3,2,1,0:T(8,128)} %pad_maximum_fusion.4), channel_id=1, source_target_pairs={{8,0},{16,8},{24,16},{9,1},{17,9},{25,17},{10,2},{18,10},{26,18},{... | collective-permute-start | bytes 1179656 | tf_op jit(solution)/shard_map/ppermute | solution.py:499
  6.5 27.4 %collective-permute-start = (f32[6,4,16,256]{3,2,1,0:T(8,128)}, f32[6,4,16,256]{3,2,1,0:T(8,128)S(1)}, u32[]{:S(2)}, u32[]{:S(2)}) collective-permute-start(f32[6,4,16,256]{3,2,1,0:T(8,128)} %pad_maximum_fusion.3), channel_id=1, source_target_pairs={{0,8},{8,16},{16,24},{1,9},{9,17},{17,25},{2,10},{10,18},{18,26},{... | collective-permute-start | bytes 1179656 | tf_op jit(solution)/shard_map/ppermute | solution.py:499
  9.6 10.3 %all-to-all-start = ((s32[8,1,48]{2,1,0:T(1,128)}), s32[8,1,48]{2,1,0:T(1,128)S(1)}, u32[]{:S(2)}, u32[]{:S(2)}) async-start(s32[8,1,48]{2,1,0:T(1,128)} %bitcast.3), calls=%async_computation | async-start | bytes 8192 | tf_op jit(solution)/shard_map/all_to_all | solution.py:515
  19.8 13.9 %copy-start.1 = (f32[32,16,256]{2,1,0:T(8,128)S(1)}, f32[32,16,256]{2,1,0:T(8,128)}, u32[]{:S(2)}) copy-start(f32[32,16,256]{2,1,0:T(8,128)} %dens.5) | copy-start | bytes 1572868
  27.3 19.3 %all-to-all-start.1 = ((f32[8,3,48,128]{3,2,1,0:T(8,128)}), f32[8,3,48,128]{3,2,1,0:T(8,128)}, u32[]{:S(2)}, u32[]{:S(2)}) async-start(f32[8,3,48,128]{3,2,1,0:T(8,128)} %pick_bricks.1), calls=%async_computation.1 | async-start | bytes 1179648 | tf_op jit(solution)/shard_map/all_to_all | solution.py:530
  33.8 1.0 copy-start.10
  33.8 5.7 %copy-start.9 = (f32[3,32,4,256]{3,2,1,0:T(4,128)S(1)}, f32[3,32,4,256]{3,2,1,0:T(4,128)}, u32[]{:S(2)}) copy-start(f32[3,32,4,256]{3,2,1,0:T(4,128)} %get-tuple-element.18) | copy-start | bytes 1179652
  33.8 5.7 %copy-start.11 = (f32[1,32,4,256]{3,2,1,0:T(4,128)S(1)}, f32[1,32,4,256]{3,2,1,0:T(4,128)}, u32[]{:S(2)}) copy-start(f32[1,32,4,256]{3,2,1,0:T(4,128)} %get-tuple-element.39) | copy-start | bytes 393220
  33.9 6.8 %copy-start.5 = (f32[6,4,16,256]{3,2,1,0:T(8,128)}, f32[6,4,16,256]{3,2,1,0:T(8,128)S(1)}, u32[]{:S(2)}) copy-start(f32[6,4,16,256]{3,2,1,0:T(8,128)S(1)} %collective-permute-done.1.high_x) | copy-start | bytes 1179652
  33.9 6.7 %copy-start.7 = (f32[6,4,16,256]{3,2,1,0:T(8,128)}, f32[6,4,16,256]{3,2,1,0:T(8,128)S(1)}, u32[]{:S(2)}) copy-start(f32[6,4,16,256]{3,2,1,0:T(8,128)S(1)} %collective-permute-done.low_x) | copy-start | bytes 1179652
  37.0 50.7 %collective-permute-start.2 = (f32[6,40,4,256]{3,2,1,0:T(4,128)}, f32[6,40,4,256]{3,2,1,0:T(4,128)}, u32[]{:S(2)}, u32[]{:S(2)}) collective-permute-start(f32[6,40,4,256]{3,2,1,0:T(4,128)} %pad_maximum_fusion.1), channel_id=1, source_target_pairs={{1,0},{2,1},{3,2},{4,3},{5,4},{6,5},{7,6},{9,8},{10,9},{11,10},{12... | collective-permute-start | bytes 2949128 | tf_op jit(solution)/shard_map/ppermute | solution.py:499
  40.7 52.3 %collective-permute-start.3 = (f32[6,40,4,256]{3,2,1,0:T(4,128)}, f32[6,40,4,256]{3,2,1,0:T(4,128)}, u32[]{:S(2)}, u32[]{:S(2)}) collective-permute-start(f32[6,40,4,256]{3,2,1,0:T(4,128)} %pad_maximum_fusion.2), channel_id=1, source_target_pairs={{0,1},{1,2},{2,3},{3,4},{4,5},{5,6},{6,7},{8,9},{9,10},{10,11},{11... | collective-permute-start | bytes 2949128 | tf_op jit(solution)/shard_map/ppermute | solution.py:499
  69.4 47.6 %all-to-all-start.2 = ((f32[8,3,48,128]{3,2,1,0:T(8,128)}), f32[8,3,48,128]{3,2,1,0:T(8,128)S(1)}, u32[]{:S(2)}, u32[]{:S(2)}) async-start(f32[8,3,48,128]{3,2,1,0:T(8,128)} %get-tuple-element.13), calls=%async_computation.2 | async-start | bytes 1179648 | tf_op jit(solution)/shard_map/all_to_all | solution.py:534
  80.2 14.7 %copy-start.4 = (f32[32,16,256]{2,1,0:T(8,128)S(1)}, f32[32,16,256]{2,1,0:T(8,128)}, u32[]{:S(2)}) copy-start(f32[32,16,256]{2,1,0:T(8,128)} %pres.1) | copy-start | bytes 1572868
  80.2 14.7 %copy-start.6 = (f32[6,4,16,256]{3,2,1,0:T(8,128)S(1)}, f32[6,4,16,256]{3,2,1,0:T(8,128)}, u32[]{:S(2)}) copy-start(f32[6,4,16,256]{3,2,1,0:T(8,128)} %copy-done.5) | copy-start | bytes 1179652
  80.2 14.7 %copy-start.8 = (f32[6,4,16,256]{3,2,1,0:T(8,128)S(1)}, f32[6,4,16,256]{3,2,1,0:T(8,128)}, u32[]{:S(2)}) copy-start(f32[6,4,16,256]{3,2,1,0:T(8,128)} %copy-done.7) | copy-start | bytes 1179652

commit v3 on v2

--- a/solution.py
+++ b/solution.py
@@ -231,8 +231,9 @@
         sums[16 : 16 + 3 * BX, columns] = low.astype(f32)
 
 
-def marker_body(counts, spread, gather, places, start, dens, brick, visc_out, moments_out, *work):
-    owner, group = pl.program_id(0), pl.program_id(1)
+def marker_body(first_owner, aliased, counts, spread, gather, places, start, dens, brick, *rest):
+    visc_out, moments_out, *work = rest[aliased:]
+    owner, group = first_owner + pl.program_id(0), pl.program_id(1)
     live_count = counts[0, owner] - group * GROUP
     sums = work[-1]
 
@@ -263,14 +264,16 @@
         run((0, 1))
 
 
-def marker_work(counts, positions, start_visc, marker_dens, bricks):
+def marker_work(counts, positions, start_visc, marker_dens, bricks, begin, end, earlier=()):
     owners, _, slots, markers = positions.shape
     groups = slots // GROUP
     spread, gather = permutations()
     width = 4 * BZ * HALF
+    operands = (counts, spread, gather, positions, start_visc, marker_dens, bricks)
+    visits = (end - begin) * slots * markers
     return pl.pallas_call(
-        marker_body,
-        grid=(owners, groups),
+        functools.partial(marker_body, begin, len(earlier)),
+        grid=(end - begin, groups),
         out_shape=(
             jax.ShapeDtypeStruct((owners, slots, markers), f32),
             jax.ShapeDtypeStruct((owners, groups, ROWS, LANES), f32),
@@ -279,15 +282,17 @@
             pl.BlockSpec(memory_space=pltpu.SMEM),
             pl.BlockSpec(spread.shape, lambda q, g: (0, 0, 0, 0)),
             pl.BlockSpec(gather.shape, lambda q, g: (0, 0)),
-            pl.BlockSpec((1, 3, GROUP, markers), lambda q, g: (q, 0, g, 0)),
-            pl.BlockSpec((1, GROUP, markers), lambda q, g: (q, g, 0)),
-            pl.BlockSpec((1, GROUP, markers), lambda q, g: (q, g, 0)),
-            pl.BlockSpec((1, 1, ROWS, LANES), lambda q, g: (q, g, 0, 0)),
-        ],
+            pl.BlockSpec((1, 3, GROUP, markers), lambda q, g: (q + begin, 0, g, 0)),
+            pl.BlockSpec((1, GROUP, markers), lambda q, g: (q + begin, g, 0)),
+            pl.BlockSpec((1, GROUP, markers), lambda q, g: (q + begin, g, 0)),
+            pl.BlockSpec((1, 1, ROWS, LANES), lambda q, g: (q + begin, g, 0, 0)),
+        ]
+        + [pl.BlockSpec(memory_space=pl.ANY)] * len(earlier),
         out_specs=(
-            pl.BlockSpec((1, GROUP, markers), lambda q, g: (q, g, 0)),
-            pl.BlockSpec((1, 1, ROWS, LANES), lambda q, g: (q, g, 0, 0)),
+            pl.BlockSpec((1, GROUP, markers), lambda q, g: (q + begin, g, 0)),
+            pl.BlockSpec((1, 1, ROWS, LANES), lambda q, g: (q + begin, g, 0, 0)),
         ),
+        input_output_aliases={len(operands) + n: n for n in range(len(earlier))},
         scratch_shapes=[
             pltpu.VMEM((2, ROWS, width), f32),
             pltpu.VMEM((2, ROWS * HALF, width), bf16),
@@ -299,8 +304,11 @@
             pltpu.VMEM((32, 2 * BY * BZ * HALF), f32),
         ],
         compiler_params=vmem_limit(60),
+        cost_estimate=pl.CostEstimate(
+            flops=visits * 100000, bytes_accessed=visits * 32, transcendentals=visits * 8
+        ),
         name="marker_work",
-    )(counts, spread, gather, positions, start_visc, marker_dens, bricks)
+    )(*operands, *earlier)
 
 
 def settle_body(asked, moments, visc, dens, visc_out, dens_out, table):
@@ -361,7 +369,97 @@
     )(asked, moments, cell_visc, cell_dens)
 
 
-def sweep_body(vel, pres, visc, dens, low_x, high_x, side_y, vel_out, pres_out, *work):
+def pack_y_body(vel, pres, visc, dens, upward, downward):
+    size_y = pres.shape[1]
+    width = SWEEPS
+    for f in range(6):
+        field = vel.at[f] if f < 3 else (pres, visc, dens)[f - 3]
+        rows = slice(f * width, (f + 1) * width)
+        upward[:, rows, :] = field[:, size_y - width :, :]
+        downward[:, rows, :] = field[:, :width, :]
+
+
+def pack_y(velocity, pressure, cell_visc, cell_dens):
+    size_x, size_y, size_z = cell_visc.shape
+    step = 8
+    block = pl.BlockSpec((step, size_y, size_z), lambda i: (i, 0, 0))
+    face = pl.BlockSpec((step, 6 * SWEEPS, size_z), lambda i: (i, 0, 0))
+    shape = jax.ShapeDtypeStruct((size_x, 6 * SWEEPS, size_z), f32)
+    return pl.pallas_call(
+        pack_y_body,
+        grid=(size_x // step,),
+        out_shape=(shape, shape),
+        in_specs=[
+            pl.BlockSpec((3, step, size_y, size_z), lambda i: (0, i, 0, 0)),
+            block,
+            block,
+            block,
+        ],
+        out_specs=(face, face),
+        compiler_params=vmem_limit(60),
+        name="pack_y",
+    )(velocity, pressure, cell_visc, cell_dens)
+
+
+def pack_x_body(vels, press, viscs, denss, low_ys, high_ys, *outs):
+    width = SWEEPS
+    for side in range(2):
+        vel, pres, visc, dens = vels[side], press[side], viscs[side], denss[side]
+        size_y = pres.shape[1]
+        for f in range(6):
+            field = vel.at[f] if f < 3 else (pres, visc, dens)[f - 3]
+            rows = slice(f * width, (f + 1) * width)
+            outs[side][f, :, :size_y, :] = field[...]
+            outs[side][f, :, size_y : size_y + width, :] = high_ys[side][:, rows, :]
+            outs[side][f, :, size_y + width :, :] = low_ys[side][:, rows, :]
+
+
+def pack_x(velocity, pressure, cell_visc, cell_dens, low_y, high_y, after):
+    size_x, size_y, size_z = cell_visc.shape
+    width = SWEEPS
+    ends = (0, size_x // width - 1)
+    ring = size_y + 2 * width
+
+    def body(*refs):
+        pairs = [refs[2 * n : 2 * n + 2] for n in range(6)]
+        pack_x_body(*pairs, *refs[12 + len(after) :])
+
+    def block(rows):
+        return [pl.BlockSpec((width, rows, size_z), lambda i, e=e: (e, 0, 0)) for e in ends]
+
+    whole = pl.BlockSpec((6, width, ring, size_z), lambda i: (0, 0, 0, 0))
+    shape = jax.ShapeDtypeStruct((6, width, ring, size_z), f32)
+    return pl.pallas_call(
+        body,
+        grid=(1,),
+        out_shape=(shape, shape),
+        in_specs=[
+            pl.BlockSpec((3, width, size_y, size_z), lambda i, e=e: (0, e, 0, 0)) for e in ends
+        ]
+        + block(size_y) * 3
+        + block(6 * width) * 2
+        + [pl.BlockSpec(memory_space=pl.ANY)] * len(after),
+        out_specs=(whole, whole),
+        compiler_params=vmem_limit(60),
+        name="pack_x",
+    )(
+        velocity,
+        velocity,
+        pressure,
+        pressure,
+        cell_visc,
+        cell_visc,
+        cell_dens,
+        cell_dens,
+        low_y,
+        low_y,
+        high_y,
+        high_y,
+        *after,
+    )
+
+
+def sweep_body(vel, pres, visc, dens, low_x, high_x, low_y, high_y, vel_out, pres_out, *work):
     fields, coefs, rate, relax, forcing = work
     size_x, size_y, size_z = visc.shape
     width = low_x.shape[1]
@@ -376,9 +474,11 @@
     fields[1, 1, inner, own, :] = dens[...]
     for f in range(6):
         slot = (0, f) if f < 4 else (1, f - 4)
-        fields[slot[0], slot[1], :width, own, :] = low_x[f]
-        fields[slot[0], slot[1], width + size_x :, own, :] = high_x[f]
-        fields[slot[0], slot[1], :, size_y:, :] = side_y[f]
+        rows = slice(f * width, (f + 1) * width)
+        fields[slot[0], slot[1], :width] = low_x[f]
+        fields[slot[0], slot[1], width + size_x :] = high_x[f]
+        fields[slot[0], slot[1], inner, size_y : size_y + width, :] = high_y[:, rows, :]
+        fields[slot[0], slot[1], inner, size_y + width :, :] = low_y[:, rows, :]
 
     lane = lax.broadcasted_iota(jnp.int32, (ring, size_z), 1)
     not_last = (lane < size_z - 1).astype(f32)
@@ -467,10 +567,10 @@
         lax.fori_loop(1 + sweep, long_x - 1 - sweep, one_plane, 0)
 
 
-def all_sweeps(velocity, pressure, cell_visc, cell_dens, low_x, high_x, side_y):
+def all_sweeps(velocity, pressure, cell_visc, cell_dens, low_x, high_x, low_y, high_y):
     size_x, size_y, size_z = cell_visc.shape
-    width = low_x.shape[1]
-    long_x, ring = size_x + 2 * width, size_y + side_y.shape[2]
+    _, width, ring, _ = low_x.shape
+    long_x = size_x + 2 * width
     whole = pl.BlockSpec(memory_space=pltpu.VMEM)
     block = (long_x, ring, size_z)
     return pl.pallas_call(
@@ -479,7 +579,7 @@
             jax.ShapeDtypeStruct(velocity.shape, f32),
             jax.ShapeDtypeStruct(pressure.shape, f32),
         ),
-        in_specs=[whole] * 7,
+        in_specs=[whole] * 8,
         out_specs=(whole, whole),
         scratch_shapes=[
             pltpu.VMEM((2, 4) + block, f32),
@@ -490,7 +590,7 @@
         ],
         compiler_params=vmem_limit(48),
         name="all_sweeps",
-    )(velocity, pressure, cell_visc, cell_dens, low_x, high_x, side_y)
+    )(velocity, pressure, cell_visc, cell_dens, low_x, high_x, low_y, high_y)
 
 
 def shift(value, axis, step):
@@ -510,31 +610,23 @@
     start_visc,
     marker_dens,
 ):
-    width = SWEEPS
-    size_x, size_y, _ = cell_visc.shape
     asked = lax.all_to_all(block_brick, "mark", 0, 0, tiled=True)
-
-    fields = (velocity, pressure[None], cell_visc[None], cell_dens[None])
-    low_x = shift(jnp.concatenate([f[:, size_x - width :] for f in fields]), "grid", 1)
-    high_x = shift(jnp.concatenate([f[:, :width] for f in fields]), "grid", -1)
-
-    def face_y(rows):
-        own = jnp.concatenate([f[:, :, rows] for f in fields])
-        return jnp.concatenate([low_x[:, :, rows], own, high_x[:, :, rows]], axis=1)
-
-    low_y = shift(face_y(slice(size_y - width, size_y)), "mark", 1)
-    high_y = shift(face_y(slice(0, width)), "mark", -1)
-    side_y = jnp.concatenate([high_y, low_y], axis=2)
+    fields = (velocity, pressure, cell_visc, cell_dens)
+    upward, downward = pack_y(*fields)
+    low_y, high_y = shift(upward, "mark", 1), shift(downward, "mark", -1)
 
     picked = pick_bricks(asked, velocity)
     bricks = lax.all_to_all(picked, "mark", 0, 0, tiled=True)
-    marker_visc, moments = marker_work(
-        block_counts, positions, start_visc, marker_dens, bricks
-    )
+    owners = positions.shape[0]
+    middle = owners // 2
+    marker_data = (block_counts, positions, start_visc, marker_dens, bricks)
+    earlier = marker_work(*marker_data, 0, middle)
+    to_low, to_high = pack_x(*fields, low_y, high_y, earlier[1:])
+    low_x, high_x = shift(to_high, "grid", 1), shift(to_low, "grid", -1)
+    earlier, to_low, to_high = lax.optimization_barrier((earlier, to_low, to_high))
+    marker_visc, moments = marker_work(*marker_data, middle, owners, earlier)
     gathered = lax.all_to_all(moments, "mark", 0, 0, tiled=True)
-    velocity_next, pressure_next = all_sweeps(
-        velocity, pressure, cell_visc, cell_dens, low_x, high_x, side_y
-    )
+    velocity_next, pressure_next = all_sweeps(*fields, low_x, high_x, low_y, high_y)
     visc_next, dens_next = settle(asked, gathered, cell_visc, cell_dens)
     return velocity_next, pressure_next, visc_next, dens_next, marker_visc
 

time: 127 us -> 140 us (1.10)
  the two profiles are of different devices: /device:TPU:12 before, /device:TPU:1 now
where the time goes in v3:
time: 140 us; the launch traced here: 139 us
  Pallas kernels  67.8 us (48%)
  waiting for transfers between devices  29.7 us (21%)
  starting transfers between devices  23.1 us (16%)
  blocking collectives  11.6 us (8%)
  local copies, waits for them, and re-layouts  5.68 us (4%)
    ppermute x4, waiting for transfers between devices, shift(): return lax.ppermute(value, axis, pairs)  24 us
    pallas_call x2, Pallas kernels, marker_work(): pl.pallas_call(functools.partial(marker_body, begin, len(earlier)), grid=...  22.8 us
    pallas_call x1, Pallas kernels, all_sweeps(): pl.pallas_call(sweep_body, out_shape=(jax.ShapeDtypeStruct(velocity.shape...  22.5 us
    all_to_all x1, blocking collectives, per_device(): asked = lax.all_to_all(block_brick, 'mark', 0, 0, tiled=True)  11.6 us
    ppermute x4, starting transfers between devices, shift(): return lax.ppermute(value, axis, pairs)  10.5 us
    all_to_all x1, starting transfers between devices, per_device(): gathered = lax.all_to_all(moments, 'mark', 0, 0, tiled=True)  9.1 us
    pallas_call x1, Pallas kernels, settle(): pl.pallas_call(settle_body, out_shape=(shape, shape), in_specs=[pl.BlockS...  8.63 us
    pallas_call x1, Pallas kernels, pick_bricks(): pl.pallas_call(pick_body, out_shape=jax.ShapeDtypeStruct((devices, slots...  7.53 us
  transfers between devices with their start and end apart: 6, of which 4 were waited for; matrix products, arithmetic and copies ran while one was open for 0% of the time, Pallas kernels for 28%

profile of v3, /device:TPU:1, one launch (start us, length us, event | category | flops | bytes accessed | tf_op | source)
XLA Modules:
  0.0 138.6 jit_solution(12875009819140129545)
XLA Ops:
  0.6 11.6 %all_to_all.21 = s32[8,1,48]{2,1,0:T(1,128)S(1)} all-to-all(s32[8,1,48]{2,1,0:T(1,128)} %bitcast.4), channel_id=1, replica_groups=mesh['grid'=4,'mark'=8] {'mark'}, dimensions={0} | all-to-all | bytes 3072 | tf_op jit(solution)/shard_map/all_to_all | solution.py:613
  12.3 1.4 %copy-done = f32[3,32,16,256]{3,2,1,0:T(8,128)S(1)} copy-done((f32[3,32,16,256]{3,2,1,0:T(8,128)S(1)}, f32[3,32,16,256]{3,2,1,0:T(8,128)}, u32[]{:S(2)}) %copy-start) | copy-done | bytes 1572888
  13.7 7.5 %pick_bricks.1 = f32[8,3,48,128]{3,2,1,0:T(8,128)} custom-call(s32[8,48]{1,0:T(8,128)S(1)} %bitcast.2, f32[3,32,16,256]{3,2,1,0:T(8,128)S(1)} %copy-done), custom_call_target="tpu_custom_call" | custom-call | tf_op jit(solution)/shard_map/pick_bricks/pallas_call | solution.py:72
  21.2 3.5 %all-to-all-start.1 = ((f32[8,3,48,128]{3,2,1,0:T(8,128)}), f32[8,3,48,128]{3,2,1,0:T(8,128)S(1)}, u32[]{:S(2)}, u32[]{:S(2)}) async-start(f32[8,3,48,128]{3,2,1,0:T(8,128)} %pick_bricks.1), calls=%async_computation.1 | async-start | bytes 1179648 | tf_op jit(solution)/shard_map/all_to_all | solution.py:619
  24.7 3.9 %pack_y.1 = (f32[32,24,256]{2,1,0:T(8,128)}, f32[32,24,256]{2,1,0:T(8,128)}) custom-call(f32[3,32,16,256]{3,2,1,0:T(8,128)} %vel.5, f32[32,16,256]{2,1,0:T(8,128)} %pres.3, f32[32,16,256]{2,1,0:T(8,128)} %visc.5, f32[32,16,256]{2,1,0:T(8,128)} %dens.9), custom_call_target="tpu_custom_call" | custom-call | tf_op jit(solution)/shard_map/pack_y/pallas_call | solution.py:388
  28.7 3.3 %collective-permute-start = (f32[32,24,256]{2,1,0:T(8,128)}, f32[32,24,256]{2,1,0:T(8,128)S(1)}, u32[]{:S(2)}, u32[]{:S(2)}) collective-permute-start(f32[32,24,256]{2,1,0:T(8,128)} %get-tuple-element.19), channel_id=1, source_target_pairs={{0,1},{1,2},{2,3},{3,4},{4,5},{5,6},{6,7},{8,9},{9,10},{10,11},{11... | collective-permute-start | bytes 2359304 | tf_op jit(solution)/shard_map/ppermute | solution.py:599
  32.0 1.3 collective-permute-start.1
  33.3 5.7 %all-to-all-done.1.brick = f32[8,3,48,128]{3,2,1,0:T(8,128)S(1)} async-done(((f32[8,3,48,128]{3,2,1,0:T(8,128)}), f32[8,3,48,128]{3,2,1,0:T(8,128)S(1)}, u32[]{:S(2)}, u32[]{:S(2)}) %all-to-all-start.1) | async-done | bytes 589856 | tf_op jit(solution)/shard_map/all_to_all | solution.py:619
  39.0 0.8 copy-done.9
  39.8 11.9 %marker_work.2 = (f32[8,48,256]{2,1,0:T(8,128)}, f32[8,3,48,128]{3,2,1,0:T(8,128)}) custom-call(s32[1,8]{1,0:T(1,128)} %counts.3, bf16[2,2,128,256]{3,2,1,0:T(8,128)(2,1)} %constant.4.clone.spread, bf16[512,512]{1,0:T(8,128)(2,1)} %constant.5.clone.gather, f32[8,3,48,256]{3,2,1,0:T(8,128)} %places.3, f32[8,48,256]{2,1,0:T(8,128)} %start.3, ...), custom_call_target="tpu_custom_call" | custom-call | flops 4915200000 | bytes 1572864 | tf_op jit(solution)/shard_map/marker_work/pallas_call | solution.py:274
  51.7 14.1 %collective-permute-done.refs_8_.refs_9_.low_y = f32[32,24,256]{2,1,0:T(8,128)S(1)} collective-permute-done((f32[32,24,256]{2,1,0:T(8,128)}, f32[32,24,256]{2,1,0:T(8,128)S(1)}, u32[]{:S(2)}, u32[]{:S(2)}) %collective-permute-start) | collective-permute-done | bytes 786464 | tf_op jit(solution)/shard_map/ppermute | solution.py:599
  65.9 0.9 copy-done.5
  66.7 0.3 copy-done.7
  67.0 2.4 %pack_x.1 = (f32[6,4,24,256]{3,2,1,0:T(8,128)}, f32[6,4,24,256]{3,2,1,0:T(8,128)}) custom-call(f32[3,32,16,256]{3,2,1,0:T(8,128)} %vel.5, f32[3,32,16,256]{3,2,1,0:T(8,128)} %vel.5, f32[32,16,256]{2,1,0:T(8,128)} %pres.3, f32[32,16,256]{2,1,0:T(8,128)} %pres.3, f32[32,16,256]{2,1,0:T(8,128)} %visc.5, f32[32,16,256]{2,1,0:T(8,128)} %visc.5, ...), custom_call_target="tpu_custom_call" | custom-call | tf_op jit(solution)/shard_map/pack_x/pallas_call | solution.py:432
  69.4 10.9 %marker_work.3 = (f32[8,48,256]{2,1,0:T(8,128)}, f32[8,3,48,128]{3,2,1,0:T(8,128)}) custom-call(s32[1,8]{1,0:T(1,128)} %counts.3, bf16[2,2,128,256]{3,2,1,0:T(8,128)(2,1)} %constant.4.clone.spread, bf16[512,512]{1,0:T(8,128)(2,1)} %constant.5.clone.gather, f32[8,3,48,256]{3,2,1,0:T(8,128)} %places.3, ...), custom_call_target="tpu_custom_call", output_to_operand_aliasing={{0}: (7, {}), {1}: (8, {})} | custom-call | flops 4915200000 | bytes 1572864 | tf_op jit(solution)/shard_map/marker_work/pallas_call | solution.py:274
  80.3 9.1 %all-to-all-start.2 = ((f32[8,3,48,128]{3,2,1,0:T(8,128)}), f32[8,3,48,128]{3,2,1,0:T(8,128)}, u32[]{:S(2)}, u32[]{:S(2)}) async-start(f32[8,3,48,128]{3,2,1,0:T(8,128)} %get-tuple-element.29), calls=%async_computation.2 | async-start | bytes 1179648 | tf_op jit(solution)/shard_map/all_to_all | solution.py:628
  89.4 4.0 %collective-permute-start.2 = (f32[6,4,24,256]{3,2,1,0:T(8,128)}, f32[6,4,24,256]{3,2,1,0:T(8,128)S(1)}, u32[]{:S(2)}, u32[]{:S(2)}) collective-permute-start(f32[6,4,24,256]{3,2,1,0:T(8,128)} %get-tuple-element.22), channel_id=1, source_target_pairs={{0,8},{8,16},{16,24},{1,9},{9,17},{17,25},{2,10},{10,18},{18,26},{... | collective-permute-start | bytes 1769480 | tf_op jit(solution)/shard_map/ppermute | solution.py:599
  93.4 1.9 %collective-permute-start.3 = (f32[6,4,24,256]{3,2,1,0:T(8,128)}, f32[6,4,24,256]{3,2,1,0:T(8,128)S(1)}, u32[]{:S(2)}, u32[]{:S(2)}) collective-permute-start(f32[6,4,24,256]{3,2,1,0:T(8,128)} %get-tuple-element.23), channel_id=1, source_target_pairs={{8,0},{16,8},{24,16},{9,1},{17,9},{25,17},{10,2},{18,10},{26,18},{... | collective-permute-start | bytes 1769480 | tf_op jit(solution)/shard_map/ppermute | solution.py:599
  95.3 5.2 %collective-permute-done.2.low_x = f32[6,4,24,256]{3,2,1,0:T(8,128)S(1)} collective-permute-done((f32[6,4,24,256]{3,2,1,0:T(8,128)}, f32[6,4,24,256]{3,2,1,0:T(8,128)S(1)}, u32[]{:S(2)}, u32[]{:S(2)}) %collective-permute-start.2) | collective-permute-done | bytes 589856 | tf_op jit(solution)/shard_map/ppermute | solution.py:599
  100.5 4.7 %collective-permute-done.3.high_x = f32[6,4,24,256]{3,2,1,0:T(8,128)S(1)} collective-permute-done((f32[6,4,24,256]{3,2,1,0:T(8,128)}, f32[6,4,24,256]{3,2,1,0:T(8,128)S(1)}, u32[]{:S(2)}, u32[]{:S(2)}) %collective-permute-start.3) | collective-permute-done | bytes 589856 | tf_op jit(solution)/shard_map/ppermute | solution.py:599
  105.2 1.1 copy-done.6
  106.3 1.1 copy-done.8
  107.5 22.5 %all_sweeps.1 = (f32[3,32,16,256]{3,2,1,0:T(8,128)}, f32[32,16,256]{2,1,0:T(8,128)}) custom-call(f32[3,32,16,256]{3,2,1,0:T(8,128)S(1)} %copy-done.1, f32[32,16,256]{2,1,0:T(8,128)S(1)} %copy-done.4, f32[32,16,256]{2,1,0:T(8,128)S(1)} %copy-done.2, f32[32,16,256]{2,1,0:T(8,128)S(1)} %copy-done.3, f32[6,4,24,256]{3,2,1,0:T(8,128)S(1)} %collective-permute-done.2.low_x, ...), custom_call_target="tpu_custom_call" | custom-call | tf_op jit(solution)/shard_map/all_sweeps/pallas_call | solution.py:576
  130.0 8.6 %settle.1 = (f32[32,16,256]{2,1,0:T(8,128)}, f32[32,16,256]{2,1,0:T(8,128)}) custom-call(s32[8,48]{1,0:T(8,128)S(1)} %bitcast.3, f32[8,3,48,128]{3,2,1,0:T(8,128)} %all-to-all-done.2.moments, f32[32,16,256]{2,1,0:T(8,128)S(1)} %copy-done.2, f32[32,16,256]{2,1,0:T(8,128)S(1)} %copy-done.3), custom_call_target="tpu_custom_call" | custom-call | tf_op jit(solution)/shard_map/settle/pallas_call | solution.py:361
  (16 shorter events, 0.0 us)
Async XLA Ops:
  12.3 1.4 %copy-start = (f32[3,32,16,256]{3,2,1,0:T(8,128)S(1)}, f32[3,32,16,256]{3,2,1,0:T(8,128)}, u32[]{:S(2)}) copy-start(f32[3,32,16,256]{3,2,1,0:T(8,128)} %vel.5) | copy-start | bytes 4718596
  21.2 17.8 %all-to-all-start.1 = ((f32[8,3,48,128]{3,2,1,0:T(8,128)}), f32[8,3,48,128]{3,2,1,0:T(8,128)S(1)}, u32[]{:S(2)}, u32[]{:S(2)}) async-start(f32[8,3,48,128]{3,2,1,0:T(8,128)} %pick_bricks.1), calls=%async_computation.1 | async-start | bytes 1179648 | tf_op jit(solution)/shard_map/all_to_all | solution.py:619
  28.7 37.2 %collective-permute-start = (f32[32,24,256]{2,1,0:T(8,128)}, f32[32,24,256]{2,1,0:T(8,128)S(1)}, u32[]{:S(2)}, u32[]{:S(2)}) collective-permute-start(f32[32,24,256]{2,1,0:T(8,128)} %get-tuple-element.19), channel_id=1, source_target_pairs={{0,1},{1,2},{2,3},{3,4},{4,5},{5,6},{6,7},{8,9},{9,10},{10,11},{11... | collective-permute-start | bytes 2359304 | tf_op jit(solution)/shard_map/ppermute | solution.py:599
  32.0 33.9 %collective-permute-start.1 = (f32[32,24,256]{2,1,0:T(8,128)}, f32[32,24,256]{2,1,0:T(8,128)S(1)}, u32[]{:S(2)}, u32[]{:S(2)}) collective-permute-start(f32[32,24,256]{2,1,0:T(8,128)} %get-tuple-element.20), channel_id=1, source_target_pairs={{1,0},{2,1},{3,2},{4,3},{5,4},{6,5},{7,6},{9,8},{10,9},{11,10},{12... | collective-permute-start | bytes 2359304 | tf_op jit(solution)/shard_map/ppermute | solution.py:599
  39.0 0.8 copy-start.9
  65.9 0.9 copy-start.5
  65.9 1.1 copy-start.7
  69.4 35.8 %copy-start.1 = (f32[3,32,16,256]{3,2,1,0:T(8,128)S(1)}, f32[3,32,16,256]{3,2,1,0:T(8,128)}, u32[]{:S(2)}) copy-start(f32[3,32,16,256]{3,2,1,0:T(8,128)} %vel.5) | copy-start | bytes 4718596
  69.4 35.8 %copy-start.2 = (f32[32,16,256]{2,1,0:T(8,128)S(1)}, f32[32,16,256]{2,1,0:T(8,128)}, u32[]{:S(2)}) copy-start(f32[32,16,256]{2,1,0:T(8,128)} %visc.5) | copy-start | bytes 1572868
  69.4 35.8 %copy-start.3 = (f32[32,16,256]{2,1,0:T(8,128)S(1)}, f32[32,16,256]{2,1,0:T(8,128)}, u32[]{:S(2)}) copy-start(f32[32,16,256]{2,1,0:T(8,128)} %dens.9) | copy-start | bytes 1572868
  69.4 35.8 %copy-start.4 = (f32[32,16,256]{2,1,0:T(8,128)S(1)}, f32[32,16,256]{2,1,0:T(8,128)}, u32[]{:S(2)}) copy-start(f32[32,16,256]{2,1,0:T(8,128)} %pres.3) | copy-start | bytes 1572868
  80.3 49.7 %all-to-all-start.2 = ((f32[8,3,48,128]{3,2,1,0:T(8,128)}), f32[8,3,48,128]{3,2,1,0:T(8,128)}, u32[]{:S(2)}, u32[]{:S(2)}) async-start(f32[8,3,48,128]{3,2,1,0:T(8,128)} %get-tuple-element.29), calls=%async_computation.2 | async-start | bytes 1179648 | tf_op jit(solution)/shard_map/all_to_all | solution.py:628
  89.4 11.1 %collective-permute-start.2 = (f32[6,4,24,256]{3,2,1,0:T(8,128)}, f32[6,4,24,256]{3,2,1,0:T(8,128)S(1)}, u32[]{:S(2)}, u32[]{:S(2)}) collective-permute-start(f32[6,4,24,256]{3,2,1,0:T(8,128)} %get-tuple-element.22), channel_id=1, source_target_pairs={{0,8},{8,16},{16,24},{1,9},{9,17},{17,25},{2,10},{10,18},{18,26},{... | collective-permute-start | bytes 1769480 | tf_op jit(solution)/shard_map/ppermute | solution.py:599
  93.4 11.8 %collective-permute-start.3 = (f32[6,4,24,256]{3,2,1,0:T(8,128)}, f32[6,4,24,256]{3,2,1,0:T(8,128)S(1)}, u32[]{:S(2)}, u32[]{:S(2)}) collective-permute-start(f32[6,4,24,256]{3,2,1,0:T(8,128)} %get-tuple-element.23), channel_id=1, source_target_pairs={{8,0},{16,8},{24,16},{9,1},{17,9},{25,17},{10,2},{18,10},{26,18},{... | collective-permute-start | bytes 1769480 | tf_op jit(solution)/shard_map/ppermute | solution.py:599
  105.2 1.1 copy-start.6
  106.3 1.1 copy-start.8

commit v4 on v2

--- a/solution.py
+++ b/solution.py
@@ -26,6 +26,12 @@
 
 def vmem_limit(mib):
     return pltpu.CompilerParams(vmem_limit_bytes=mib * 1024 * 1024)
+
+
+def cost(microseconds):
+    return pl.CostEstimate(
+        flops=int(microseconds * 1.15e9), bytes_accessed=0, transcendentals=0
+    )
 
 
 def pick_body(asked, vel, out, table):
@@ -78,7 +84,8 @@
         ],
         out_specs=pl.BlockSpec(memory_space=pltpu.VMEM),
         scratch_shapes=[pltpu.VMEM((places, ROWS, LANES), f32)],
-        compiler_params=vmem_limit(32),
+        compiler_params=vmem_limit(60),
+        cost_estimate=cost(7),
         name="pick_bricks",
     )(asked, velocity)
 
@@ -231,7 +238,9 @@
         sums[16 : 16 + 3 * BX, columns] = low.astype(f32)
 
 
-def marker_body(counts, spread, gather, places, start, dens, brick, visc_out, moments_out, *work):
+def marker_body(
+    counts, spread, gather, places, start, dens, brick, _, visc_out, moments_out, *work
+):
     owner, group = pl.program_id(0), pl.program_id(1)
     live_count = counts[0, owner] - group * GROUP
     sums = work[-1]
@@ -263,7 +272,7 @@
         run((0, 1))
 
 
-def marker_work(counts, positions, start_visc, marker_dens, bricks):
+def marker_work(counts, positions, start_visc, marker_dens, bricks, after):
     owners, _, slots, markers = positions.shape
     groups = slots // GROUP
     spread, gather = permutations()
@@ -283,6 +292,7 @@
             pl.BlockSpec((1, GROUP, markers), lambda q, g: (q, g, 0)),
             pl.BlockSpec((1, GROUP, markers), lambda q, g: (q, g, 0)),
             pl.BlockSpec((1, 1, ROWS, LANES), lambda q, g: (q, g, 0, 0)),
+            pl.BlockSpec(memory_space=pl.ANY),
         ],
         out_specs=(
             pl.BlockSpec((1, GROUP, markers), lambda q, g: (q, g, 0)),
@@ -299,14 +309,16 @@
             pltpu.VMEM((32, 2 * BY * BZ * HALF), f32),
         ],
         compiler_params=vmem_limit(60),
+        cost_estimate=cost(25),
         name="marker_work",
-    )(counts, spread, gather, positions, start_visc, marker_dens, bricks)
-
-
-def settle_body(asked, moments, visc, dens, visc_out, dens_out, table):
+    )(counts, spread, gather, positions, start_visc, marker_dens, bricks, after)
+
+
+def settle_body(asked, moments, visc, dens, visc_out, dens_out, *tables):
     size_x, size_y, size_z = visc.shape
     bricks_y, halves = size_y // BY, size_z // LANES
-    table[...] = jnp.zeros_like(table)
+    for table in tables:
+        table[...] = jnp.zeros_like(table)
     groups = moments.shape[1]
     lane_slot = lax.broadcasted_iota(jnp.int32, (ROWS, LANES), 1) // BZ
 
@@ -314,6 +326,7 @@
         device, group = step // groups, step % groups
         packed = moments[device, group]
         for slot in range(GROUP):
+            table = tables[slot % len(tables)]
             brick = asked[device, group * GROUP + slot]
             shift = (BZ * (brick % GROUP) - BZ * slot + LANES) % LANES
             piece = pltpu.roll(jnp.where(lane_slot == slot, packed, 0.0), shift, 1)
@@ -324,19 +337,25 @@
     lax.fori_loop(0, moments.shape[0] * groups, one_group, 0)
 
     def finish(block_x, carry):
-        for block_y in range(bricks_y):
+        for block_y in range(0, bricks_y, 2):
             for half in range(halves):
-                place = (block_x * bricks_y + block_y) * halves + half
                 for i in range(BX):
                     here = (
                         block_x * BX + i,
-                        slice(block_y * BY, (block_y + 1) * BY),
+                        slice(block_y * BY, (block_y + 2) * BY),
                         slice(half * LANES, (half + 1) * LANES),
                     )
-                    sums = [
-                        table[place, (c * BX + i) * BY : (c * BX + i + 1) * BY, :]
-                        for c in range(3)
-                    ]
+                    sums = []
+                    for c in range(3):
+                        rows = slice((c * BX + i) * BY, (c * BX + i + 1) * BY)
+                        places = [
+                            (block_x * bricks_y + block_y + k) * halves + half for k in range(2)
+                        ]
+                        sums.append(
+                            jnp.concatenate(
+                                [add_all([t[place, rows, :] for t in tables]) for place in places]
+                            )
+                        )
                     scale = 1.0 / (sums[0] + 1.0)
                     visc_out[here] = jnp.exp((sums[1] + jnp.log(visc[here])) * scale)
                     dens_out[here] = (sums[2] + dens[here]) * scale
@@ -355,13 +374,106 @@
         out_shape=(shape, shape),
         in_specs=[pl.BlockSpec(memory_space=pltpu.SMEM), whole, whole, whole],
         out_specs=(whole, whole),
-        scratch_shapes=[pltpu.VMEM((places, ROWS, LANES), f32)],
-        compiler_params=vmem_limit(32),
+        scratch_shapes=[pltpu.VMEM((places, ROWS, LANES), f32)] * 2,
+        compiler_params=vmem_limit(60),
+        cost_estimate=cost(7),
         name="settle",
     )(asked, moments, cell_visc, cell_dens)
 
 
-def sweep_body(vel, pres, visc, dens, low_x, high_x, side_y, vel_out, pres_out, *work):
+def field_of(fields, index):
+    return fields[0].at[index] if index < 3 else fields[index - 2]
+
+
+def pack_x_body(*refs):
+    ends, outs = refs[:8], refs[8:]
+    for side in range(2):
+        for f in range(6):
+            outs[side][f] = field_of(ends[side::2], f)[...]
+
+
+def pack_x(velocity, pressure, cell_visc, cell_dens):
+    size_x, size_y, size_z = cell_visc.shape
+    width = SWEEPS
+    ends = (0, size_x // width - 1)
+    vel = [
+        pl.BlockSpec((3, width, size_y, size_z), lambda i, e=e: (0, e, 0, 0)) for e in ends
+    ]
+    block = [pl.BlockSpec((width, size_y, size_z), lambda i, e=e: (e, 0, 0)) for e in ends]
+    whole = pl.BlockSpec((6, width, size_y, size_z), lambda i: (0, 0, 0, 0))
+    shape = jax.ShapeDtypeStruct((6, width, size_y, size_z), f32)
+    return pl.pallas_call(
+        pack_x_body,
+        grid=(1,),
+        out_shape=(shape, shape),
+        in_specs=vel + block * 3,
+        out_specs=(whole, whole),
+        compiler_params=vmem_limit(60),
+        cost_estimate=cost(2),
+        name="pack_x",
+    )(velocity, velocity, pressure, pressure, cell_visc, cell_visc, cell_dens, cell_dens)
+
+
+def corner_rows(field):
+    found, width = [], SWEEPS
+    per_field = width * (width - 1)
+    for side in range(2):
+        for far_x in range(1, width):
+            for far_y in range(1, width - far_x + 1):
+                flat = field * per_field + len(found)
+                found.append((side, far_x, far_y, *divmod(flat, 6 * width)))
+    return found
+
+
+def pack_y_body(vel, pres, visc, dens, low_x, high_x, upward, downward):
+    step_x, size_y, _ = pres.shape
+    width = SWEEPS
+    step = pl.program_id(0)
+    planes = pl.ds(pl.multiple_of(step * step_x, step_x), step_x)
+    for f in range(6):
+        field = field_of((vel, pres, visc, dens), f)
+        rows = slice(f * width, (f + 1) * width)
+        upward[planes, rows, :] = field[:, size_y - width :, :]
+        downward[planes, rows, :] = field[:, :width, :]
+
+    @pl.when(step == 0)
+    def _():
+        size_x = pl.num_programs(0) * step_x
+        for f in range(6):
+            for side, far_x, far_y, plane, row in corner_rows(f):
+                halo, at = (high_x, far_x - 1) if side else (low_x, width - far_x)
+                upward[size_x + plane, row] = halo[f, at, size_y - far_y]
+                downward[size_x + plane, row] = halo[f, at, far_y - 1]
+
+
+def pack_y(velocity, pressure, cell_visc, cell_dens, low_x, high_x):
+    size_x, size_y, size_z = cell_visc.shape
+    step, width = 8, SWEEPS
+    long_x = size_x + width - 1
+    block = pl.BlockSpec((step, size_y, size_z), lambda i: (i, 0, 0))
+    halo = pl.BlockSpec(low_x.shape, lambda i: (0, 0, 0, 0))
+    face = pl.BlockSpec((long_x, 6 * width, size_z), lambda i: (0, 0, 0))
+    shape = jax.ShapeDtypeStruct((long_x, 6 * width, size_z), f32)
+    return pl.pallas_call(
+        pack_y_body,
+        grid=(size_x // step,),
+        out_shape=(shape, shape),
+        in_specs=[
+            pl.BlockSpec((3, step, size_y, size_z), lambda i: (0, i, 0, 0)),
+            block,
+            block,
+            block,
+            halo,
+            halo,
+        ],
+        out_specs=(face, face),
+        compiler_params=vmem_limit(60),
+        cost_estimate=cost(3),
+        name="pack_y",
+    )(velocity, pressure, cell_visc, cell_dens, low_x, high_x)
+
+
+def sweep_body(vel, pres, visc, dens, low_x, high_x, low_y, high_y, vel_out, pres_out, *work):
     fields, coefs, rate, relax, forcing = work
     size_x, size_y, size_z = visc.shape
     width = low_x.shape[1]
@@ -375,10 +487,17 @@
     fields[1, 0, inner, own, :] = visc[...]
     fields[1, 1, inner, own, :] = dens[...]
     for f in range(6):
-        slot = (0, f) if f < 4 else (1, f - 4)
-        fields[slot[0], slot[1], :width, own, :] = low_x[f]
-        fields[slot[0], slot[1], width + size_x :, own, :] = high_x[f]
-        fields[slot[0], slot[1], :, size_y:, :] = side_y[f]
+        field = fields.at[0, f] if f < 4 else fields.at[1, f - 4]
+        rows = slice(f * width, (f + 1) * width)
+        for at, halo in ((0, low_x), (width + size_x, high_x)):
+            field[at : at + width, own, :] = halo[f]
+            field[at : at + width, size_y:, :] = jnp.zeros((width, 2 * width, size_z), f32)
+        field[inner, size_y : size_y + width, :] = high_y[:size_x, rows, :]
+        field[inner, size_y + width :, :] = low_y[:size_x, rows, :]
+        for side, far_x, far_y, plane, row in corner_rows(f):
+            at = width + size_x - 1 + far_x if side else width - far_x
+            field[at, size_y + far_y - 1] = high_y[size_x + plane, row]
+            field[at, ring - far_y] = low_y[size_x + plane, row]
 
     lane = lax.broadcasted_iota(jnp.int32, (ring, size_z), 1)
     not_last = (lane < size_z - 1).astype(f32)
@@ -418,7 +537,7 @@
         rate[i] = PRESSURE_RATE * here
         return carry
 
-    lax.fori_loop(1, long_x - 1, prepare, 0)
+    lax.fori_loop(1, long_x - 1, prepare, 0, unroll=2)
 
     for sweep in range(SWEEPS):
         old, new = sweep % 2, (sweep + 1) % 2
@@ -426,7 +545,6 @@
 
         def one_plane(i, carry, old=old, new=new, last=last):
             pressure = fields[old, 3, i]
-            links = [coefs[n, i] for n in range(6)]
             scale = relax[i]
             before = (
                 fields[old, 3, i - 1],
@@ -445,8 +563,8 @@
                     down_z(here),
                 ]
                 total = (1.0 - RELAX) * here - scale * (pressure - before[c])
-                for link, other in zip(links, near):
-                    total = total + link * other
+                for n, other in enumerate(near):
+                    total = total + coefs[n, i] * other
                 ahead = near[2 * c]
                 if c == 2:
                     total = total + forcing[i]
@@ -464,13 +582,13 @@
                 fields[new, 3, i] = pressed
             return carry
 
-        lax.fori_loop(1 + sweep, long_x - 1 - sweep, one_plane, 0)
-
-
-def all_sweeps(velocity, pressure, cell_visc, cell_dens, low_x, high_x, side_y):
+        lax.fori_loop(1 + sweep, long_x - 1 - sweep, one_plane, 0, unroll=2)
+
+
+def all_sweeps(velocity, pressure, cell_visc, cell_dens, low_x, high_x, low_y, high_y):
     size_x, size_y, size_z = cell_visc.shape
     width = low_x.shape[1]
-    long_x, ring = size_x + 2 * width, size_y + side_y.shape[2]
+    long_x, ring = size_x + 2 * width, size_y + 2 * width
     whole = pl.BlockSpec(memory_space=pltpu.VMEM)
     block = (long_x, ring, size_z)
     return pl.pallas_call(
@@ -479,7 +597,7 @@
             jax.ShapeDtypeStruct(velocity.shape, f32),
             jax.ShapeDtypeStruct(pressure.shape, f32),
         ),
-        in_specs=[whole] * 7,
+        in_specs=[whole] * 8,
         out_specs=(whole, whole),
         scratch_shapes=[
             pltpu.VMEM((2, 4) + block, f32),
@@ -488,9 +606,10 @@
             pltpu.VMEM(block, f32),
             pltpu.VMEM(block, f32),
         ],
-        compiler_params=vmem_limit(48),
+        compiler_params=vmem_limit(60),
+        cost_estimate=cost(20),
         name="all_sweeps",
-    )(velocity, pressure, cell_visc, cell_dens, low_x, high_x, side_y)
+    )(velocity, pressure, cell_visc, cell_dens, low_x, high_x, low_y, high_y)
 
 
 def shift(value, axis, step):
@@ -510,31 +629,21 @@
     start_visc,
     marker_dens,
 ):
-    width = SWEEPS
-    size_x, size_y, _ = cell_visc.shape
-    asked = lax.all_to_all(block_brick, "mark", 0, 0, tiled=True)
-
-    fields = (velocity, pressure[None], cell_visc[None], cell_dens[None])
-    low_x = shift(jnp.concatenate([f[:, size_x - width :] for f in fields]), "grid", 1)
-    high_x = shift(jnp.concatenate([f[:, :width] for f in fields]), "grid", -1)
-
-    def face_y(rows):
-        own = jnp.concatenate([f[:, :, rows] for f in fields])
-        return jnp.concatenate([low_x[:, :, rows], own, high_x[:, :, rows]], axis=1)
-
-    low_y = shift(face_y(slice(size_y - width, size_y)), "mark", 1)
-    high_y = shift(face_y(slice(0, width)), "mark", -1)
-    side_y = jnp.concatenate([high_y, low_y], axis=2)
+    every = lax.all_gather(block_brick, "mark", axis=0)
+    asked = lax.dynamic_index_in_dim(every, lax.axis_index("mark"), axis=1, keepdims=False)
+    fields = (velocity, pressure, cell_visc, cell_dens)
+    to_low, to_high = pack_x(*fields)
+    low_x, high_x = shift(to_high, "grid", 1), shift(to_low, "grid", -1)
+    upward, downward = pack_y(*fields, low_x, high_x)
+    low_y, high_y = shift(upward, "mark", 1), shift(downward, "mark", -1)
 
     picked = pick_bricks(asked, velocity)
     bricks = lax.all_to_all(picked, "mark", 0, 0, tiled=True)
     marker_visc, moments = marker_work(
-        block_counts, positions, start_visc, marker_dens, bricks
+        block_counts, positions, start_visc, marker_dens, bricks, upward
     )
     gathered = lax.all_to_all(moments, "mark", 0, 0, tiled=True)
-    velocity_next, pressure_next = all_sweeps(
-        velocity, pressure, cell_visc, cell_dens, low_x, high_x, side_y
-    )
+    velocity_next, pressure_next = all_sweeps(*fields, low_x, high_x, low_y, high_y)
     visc_next, dens_next = settle(asked, gathered, cell_visc, cell_dens)
     return velocity_next, pressure_next, visc_next, dens_next, marker_visc
 

time: 127 us -> 139 us (1.094)
  the two profiles are of different devices: /device:TPU:12 before, /device:TPU:21 now
where the time goes in v4:
time: 139 us; the launch traced here: 137 us
  Pallas kernels  65.7 us (47%)
  starting transfers between devices  33.3 us (24%)
  blocking collectives  22.5 us (16%)
  waiting for transfers between devices  10 us (7%)
  local copies, waits for them, and re-layouts  4.88 us (4%)
    pallas_call x1, Pallas kernels, marker_work(): pl.pallas_call(marker_body, grid=(owners, groups), out_shape=(jax.ShapeDt...  22.8 us
    all_gather x1, blocking collectives, per_device(): every = lax.all_gather(block_brick, 'mark', axis=0)  22.5 us
    pallas_call x1, Pallas kernels, all_sweeps(): pl.pallas_call(sweep_body, out_shape=(jax.ShapeDtypeStruct(velocity.shape...  19.3 us
    ppermute x4, starting transfers between devices, shift(): return lax.ppermute(value, axis, pairs)  17.8 us
    ppermute x4, waiting for transfers between devices, shift(): return lax.ppermute(value, axis, pairs)  10 us
    pallas_call x1, Pallas kernels, settle(): pl.pallas_call(settle_body, out_shape=(shape, shape), in_specs=[pl.BlockS...  8.98 us
    pallas_call x1, Pallas kernels, pick_bricks(): pl.pallas_call(pick_body, out_shape=jax.ShapeDtypeStruct((devices, slots...  8.35 us
    all_to_all x1, starting transfers between devices, per_device(): gathered = lax.all_to_all(moments, 'mark', 0, 0, tiled=True)  8.24 us
  transfers between devices with their start and end apart: 6, of which 3 were waited for; matrix products, arithmetic and copies ran while one was open for 0% of the time, Pallas kernels for 35%

profile of v4, /device:TPU:21, one launch (start us, length us, event | category | flops | bytes accessed | tf_op | source)
XLA Modules:
  0.0 137.0 jit_solution(10085776270019725269)
XLA Ops:
  0.6 22.5 %all-gather = s32[64,48]{1,0:T(8,128)S(1)} all-gather(s32[8,48]{1,0:T(8,128)} %param.15), channel_id=2, replica_groups=mesh['grid'=4,'mark'=8] {'mark'}, dimensions={0}, use_global_device_ids=true | all-gather | bytes 13824 | tf_op jit(solution)/shard_map/all_gather | solution.py:632
  23.1 0.6 constant_dynamic-slice_fusion
  23.7 8.3 %pick_bricks.1 = f32[8,3,48,128]{3,2,1,0:T(8,128)} custom-call(s32[8,48]{1,0:T(8,128)} %bitcast.5, f32[3,32,16,256]{3,2,1,0:T(8,128)} %vel.5), custom_call_target="tpu_custom_call" | custom-call | flops 8049999872 | tf_op jit(solution)/shard_map/pick_bricks/pallas_call | solution.py:78
  32.1 7.2 %all-to-all-start = ((f32[8,3,48,128]{3,2,1,0:T(8,128)}), f32[8,3,48,128]{3,2,1,0:T(8,128)S(1)}, u32[]{:S(2)}, u32[]{:S(2)}) async-start(f32[8,3,48,128]{3,2,1,0:T(8,128)} %pick_bricks.1), calls=%async_computation | async-start | bytes 1179648 | tf_op jit(solution)/shard_map/all_to_all | solution.py:641
  39.3 2.1 %pack_x.1 = (f32[6,4,16,256]{3,2,1,0:T(8,128)}, f32[6,4,16,256]{3,2,1,0:T(8,128)}) custom-call(f32[3,32,16,256]{3,2,1,0:T(8,128)} %vel.5, f32[3,32,16,256]{3,2,1,0:T(8,128)} %vel.5, f32[32,16,256]{2,1,0:T(8,128)} %pres.3, f32[32,16,256]{2,1,0:T(8,128)} %pres.3, f32[32,16,256]{2,1,0:T(8,128)} %visc.5, f32[32,16,256]{2,1,0:T(8,128)} %visc.5, ...), custom_call_target="tpu_custom_call" | custom-call | flops 2300000000 | tf_op jit(solution)/shard_map/pack_x/pallas_call | solution.py:405
  41.4 10.6 %collective-permute-start = (f32[6,4,16,256]{3,2,1,0:T(8,128)}, f32[6,4,16,256]{3,2,1,0:T(8,128)S(1)}, u32[]{:S(2)}, u32[]{:S(2)}) collective-permute-start(f32[6,4,16,256]{3,2,1,0:T(8,128)} %get-tuple-element.15), channel_id=1, source_target_pairs={{0,8},{8,16},{16,24},{1,9},{9,17},{17,25},{2,10},{10,18},{18,26},{... | collective-permute-start | bytes 1179656 | tf_op jit(solution)/shard_map/ppermute | solution.py:618
  52.0 1.9 %collective-permute-start.1 = (f32[6,4,16,256]{3,2,1,0:T(8,128)}, f32[6,4,16,256]{3,2,1,0:T(8,128)S(1)}, u32[]{:S(2)}, u32[]{:S(2)}) collective-permute-start(f32[6,4,16,256]{3,2,1,0:T(8,128)} %get-tuple-element.16), channel_id=1, source_target_pairs={{8,0},{16,8},{24,16},{9,1},{17,9},{25,17},{10,2},{18,10},{26,18},{... | collective-permute-start | bytes 1179656 | tf_op jit(solution)/shard_map/ppermute | solution.py:618
  53.9 3.1 %collective-permute-done.low_x = f32[6,4,16,256]{3,2,1,0:T(8,128)S(1)} collective-permute-done((f32[6,4,16,256]{3,2,1,0:T(8,128)}, f32[6,4,16,256]{3,2,1,0:T(8,128)S(1)}, u32[]{:S(2)}, u32[]{:S(2)}) %collective-permute-start) | collective-permute-done | bytes 393248 | tf_op jit(solution)/shard_map/ppermute | solution.py:618
  57.0 4.3 %collective-permute-done.1.high_x = f32[6,4,16,256]{3,2,1,0:T(8,128)S(1)} collective-permute-done((f32[6,4,16,256]{3,2,1,0:T(8,128)}, f32[6,4,16,256]{3,2,1,0:T(8,128)S(1)}, u32[]{:S(2)}, u32[]{:S(2)}) %collective-permute-start.1) | collective-permute-done | bytes 393248 | tf_op jit(solution)/shard_map/ppermute | solution.py:618
  61.3 0.7 copy-done.5
  62.0 4.2 %pack_y.1 = (f32[35,24,256]{2,1,0:T(8,128)}, f32[35,24,256]{2,1,0:T(8,128)}) custom-call(f32[3,32,16,256]{3,2,1,0:T(8,128)} %vel.5, f32[32,16,256]{2,1,0:T(8,128)} %pres.3, f32[32,16,256]{2,1,0:T(8,128)} %visc.5, f32[32,16,256]{2,1,0:T(8,128)} %dens.7, f32[6,4,16,256]{3,2,1,0:T(8,128)} %copy-done.4, f32[6,4,16,256]{3,2,1,0:T(8,128)} %copy-done.5), custom_call_target="tpu_custom_call" | custom-call | flops 3449999872 | tf_op jit(solution)/shard_map/pack_y/pallas_call | solution.py:457
  66.2 3.1 %collective-permute-start.2 = (f32[35,24,256]{2,1,0:T(8,128)}, f32[35,24,256]{2,1,0:T(8,128)S(1)}, u32[]{:S(2)}, u32[]{:S(2)}) collective-permute-start(f32[35,24,256]{2,1,0:T(8,128)} %get-tuple-element.17._), channel_id=1, source_target_pairs={{0,1},{1,2},{2,3},{3,4},{4,5},{5,6},{6,7},{8,9},{9,10},{10,11},{11... | collective-permute-start | bytes 2580488 | tf_op jit(solution)/shard_map/ppermute | solution.py:618
  69.3 2.2 %collective-permute-start.3 = (f32[35,24,256]{2,1,0:T(8,128)}, f32[35,24,256]{2,1,0:T(8,128)S(1)}, u32[]{:S(2)}, u32[]{:S(2)}) collective-permute-start(f32[35,24,256]{2,1,0:T(8,128)} %get-tuple-element.18), channel_id=1, source_target_pairs={{1,0},{2,1},{3,2},{4,3},{5,4},{6,5},{7,6},{9,8},{10,9},{11,10},{12... | collective-permute-start | bytes 2580488 | tf_op jit(solution)/shard_map/ppermute | solution.py:618
  71.5 0.0 all-to-all-done.brick
  71.5 0.8 copy-done
  72.4 22.8 %marker_work.1 = (f32[8,48,256]{2,1,0:T(8,128)}, f32[8,3,48,128]{3,2,1,0:T(8,128)}) custom-call(s32[1,8]{1,0:T(1,128)} %counts.1, bf16[2,2,128,256]{3,2,1,0:T(8,128)(2,1)} %constant.14.clone.spread, bf16[512,512]{1,0:T(8,128)(2,1)} %constant.15.clone.gather, f32[8,3,48,256]{3,2,1,0:T(8,128)} %places.1, f32[8,48,256]{2,1,0:T(8,128)} %start.1, ...), custom_call_target="tpu_custom_call" | custom-call | flops 28750000128 | tf_op jit(solution)/shard_map/marker_work/pallas_call | solution.py:280
  95.1 8.2 %all-to-all-start.1 = ((f32[8,3,48,128]{3,2,1,0:T(8,128)}), f32[8,3,48,128]{3,2,1,0:T(8,128)S(1)}, u32[]{:S(2)}, u32[]{:S(2)}) async-start(f32[8,3,48,128]{3,2,1,0:T(8,128)} %get-tuple-element.21), calls=%async_computation.1 | async-start | bytes 1179648 | tf_op jit(solution)/shard_map/all_to_all | solution.py:645
  103.4 2.7 %collective-permute-done.2.low_y = f32[35,24,256]{2,1,0:T(8,128)S(1)} collective-permute-done((f32[35,24,256]{2,1,0:T(8,128)}, f32[35,24,256]{2,1,0:T(8,128)S(1)}, u32[]{:S(2)}, u32[]{:S(2)}) %collective-permute-start.2) | collective-permute-done | bytes 860192 | tf_op jit(solution)/shard_map/ppermute | solution.py:618
  106.0 0.0 collective-permute-done.3.high_y
  106.0 1.0 copy-done.2
  107.0 0.9 copy-done.3
  107.9 19.3 %all_sweeps.1 = (f32[3,32,16,256]{3,2,1,0:T(8,128)}, f32[32,16,256]{2,1,0:T(8,128)}) custom-call(f32[3,32,16,256]{3,2,1,0:T(8,128)} %vel.5, f32[32,16,256]{2,1,0:T(8,128)} %pres.3, f32[32,16,256]{2,1,0:T(8,128)} %visc.5, f32[32,16,256]{2,1,0:T(8,128)} %dens.7, f32[6,4,16,256]{3,2,1,0:T(8,128)} %copy-done.4, f32[6,4,16,256]{3,2,1,0:T(8,128)} %copy-done.5, ...), custom_call_target="tpu_custom_call" | custom-call | flops 23000000512 | tf_op jit(solution)/shard_map/all_sweeps/pallas_call | solution.py:594
  127.2 0.8 copy-done.1
  128.1 9.0 %settle.1 = (f32[32,16,256]{2,1,0:T(8,128)}, f32[32,16,256]{2,1,0:T(8,128)}) custom-call(s32[8,48]{1,0:T(8,128)} %bitcast.6, f32[8,3,48,128]{3,2,1,0:T(8,128)} %copy-done.1, f32[32,16,256]{2,1,0:T(8,128)} %visc.5, f32[32,16,256]{2,1,0:T(8,128)} %dens.7), custom_call_target="tpu_custom_call" | custom-call | flops 8049999872 | tf_op jit(solution)/shard_map/settle/pallas_call | solution.py:372
  (8 shorter events, 0.0 us)
Async XLA Ops:
  32.1 39.4 %all-to-all-start = ((f32[8,3,48,128]{3,2,1,0:T(8,128)}), f32[8,3,48,128]{3,2,1,0:T(8,128)S(1)}, u32[]{:S(2)}, u32[]{:S(2)}) async-start(f32[8,3,48,128]{3,2,1,0:T(8,128)} %pick_bricks.1), calls=%async_computation | async-start | bytes 1179648 | tf_op jit(solution)/shard_map/all_to_all | solution.py:641
  41.4 15.6 %collective-permute-start = (f32[6,4,16,256]{3,2,1,0:T(8,128)}, f32[6,4,16,256]{3,2,1,0:T(8,128)S(1)}, u32[]{:S(2)}, u32[]{:S(2)}) collective-permute-start(f32[6,4,16,256]{3,2,1,0:T(8,128)} %get-tuple-element.15), channel_id=1, source_target_pairs={{0,8},{8,16},{16,24},{1,9},{9,17},{17,25},{2,10},{10,18},{18,26},{... | collective-permute-start | bytes 1179656 | tf_op jit(solution)/shard_map/ppermute | solution.py:618
  52.0 9.3 %collective-permute-start.1 = (f32[6,4,16,256]{3,2,1,0:T(8,128)}, f32[6,4,16,256]{3,2,1,0:T(8,128)S(1)}, u32[]{:S(2)}, u32[]{:S(2)}) collective-permute-start(f32[6,4,16,256]{3,2,1,0:T(8,128)} %get-tuple-element.16), channel_id=1, source_target_pairs={{8,0},{16,8},{24,16},{9,1},{17,9},{25,17},{10,2},{18,10},{26,18},{... | collective-permute-start | bytes 1179656 | tf_op jit(solution)/shard_map/ppermute | solution.py:618
  57.0 4.3 %copy-start.4 = (f32[6,4,16,256]{3,2,1,0:T(8,128)}, f32[6,4,16,256]{3,2,1,0:T(8,128)S(1)}, u32[]{:S(2)}) copy-start(f32[6,4,16,256]{3,2,1,0:T(8,128)S(1)} %collective-permute-done.low_x) | copy-start | bytes 1179652
  61.3 0.7 copy-start.5
  66.2 39.8 %collective-permute-start.2 = (f32[35,24,256]{2,1,0:T(8,128)}, f32[35,24,256]{2,1,0:T(8,128)S(1)}, u32[]{:S(2)}, u32[]{:S(2)}) collective-permute-start(f32[35,24,256]{2,1,0:T(8,128)} %get-tuple-element.17._), channel_id=1, source_target_pairs={{0,1},{1,2},{2,3},{3,4},{4,5},{5,6},{6,7},{8,9},{9,10},{10,11},{11... | collective-permute-start | bytes 2580488 | tf_op jit(solution)/shard_map/ppermute | solution.py:618
  69.3 36.7 %collective-permute-start.3 = (f32[35,24,256]{2,1,0:T(8,128)}, f32[35,24,256]{2,1,0:T(8,128)S(1)}, u32[]{:S(2)}, u32[]{:S(2)}) collective-permute-start(f32[35,24,256]{2,1,0:T(8,128)} %get-tuple-element.18), channel_id=1, source_target_pairs={{1,0},{2,1},{3,2},{4,3},{5,4},{6,5},{7,6},{9,8},{10,9},{11,10},{12... | collective-permute-start | bytes 2580488 | tf_op jit(solution)/shard_map/ppermute | solution.py:618
  71.5 0.8 copy-start
  95.1 32.1 %all-to-all-start.1 = ((f32[8,3,48,128]{3,2,1,0:T(8,128)}), f32[8,3,48,128]{3,2,1,0:T(8,128)S(1)}, u32[]{:S(2)}, u32[]{:S(2)}) async-start(f32[8,3,48,128]{3,2,1,0:T(8,128)} %get-tuple-element.21), calls=%async_computation.1 | async-start | bytes 1179648 | tf_op jit(solution)/shard_map/all_to_all | solution.py:645
  106.0 1.0 copy-start.2
  107.0 0.9 copy-start.3
  127.2 0.8 copy-start.1

commit v5 on v4

--- a/solution.py
+++ b/solution.py
@@ -32,6 +32,10 @@
     return pl.CostEstimate(
         flops=int(microseconds * 1.15e9), bytes_accessed=0, transcendentals=0
     )
+
+
+def place_of(brick):
+    return lax.shift_right_logical(brick, GROUP.bit_length() - 1), (brick & (GROUP - 1)) * BZ
 
 
 def pick_body(asked, vel, out, table):
@@ -61,9 +65,8 @@
         device, group = step // groups, step % groups
         packed = jnp.zeros((ROWS, LANES), f32)
         for slot in range(GROUP):
-            brick = asked[device, group * GROUP + slot]
-            shift = (BZ * slot - BZ * (brick % GROUP) + LANES) % LANES
-            rolled = pltpu.roll(table[brick // GROUP], shift, 1)
+            place, lane = place_of(asked[device, group * GROUP + slot])
+            rolled = pltpu.roll(table[place], (BZ * slot - lane) & (LANES - 1), 1)
             packed = jnp.where(lane_slot == slot, rolled, packed)
         out[device, group] = packed
         return carry
@@ -84,8 +87,8 @@
         ],
         out_specs=pl.BlockSpec(memory_space=pltpu.VMEM),
         scratch_shapes=[pltpu.VMEM((places, ROWS, LANES), f32)],
-        compiler_params=vmem_limit(60),
-        cost_estimate=cost(7),
+        compiler_params=vmem_limit(24),
+        cost_estimate=cost(3),
         name="pick_bricks",
     )(asked, velocity)
 
@@ -327,10 +330,9 @@
         packed = moments[device, group]
         for slot in range(GROUP):
             table = tables[slot % len(tables)]
-            brick = asked[device, group * GROUP + slot]
-            shift = (BZ * (brick % GROUP) - BZ * slot + LANES) % LANES
-            piece = pltpu.roll(jnp.where(lane_slot == slot, packed, 0.0), shift, 1)
-            place = brick // GROUP
+            place, lane = place_of(asked[device, group * GROUP + slot])
+            piece = jnp.where(lane_slot == slot, packed, 0.0)
+            piece = pltpu.roll(piece, (lane - BZ * slot) & (LANES - 1), 1)
             table[place] = table[place] + piece
         return carry
 
@@ -375,7 +377,7 @@
         in_specs=[pl.BlockSpec(memory_space=pltpu.SMEM), whole, whole, whole],
         out_specs=(whole, whole),
         scratch_shapes=[pltpu.VMEM((places, ROWS, LANES), f32)] * 2,
-        compiler_params=vmem_limit(60),
+        compiler_params=vmem_limit(24),
         cost_estimate=cost(7),
         name="settle",
     )(asked, moments, cell_visc, cell_dens)
@@ -408,7 +410,7 @@
         out_shape=(shape, shape),
         in_specs=vel + block * 3,
         out_specs=(whole, whole),
-        compiler_params=vmem_limit(60),
+        compiler_params=vmem_limit(24),
         cost_estimate=cost(2),
         name="pack_x",
     )(velocity, velocity, pressure, pressure, cell_visc, cell_visc, cell_dens, cell_dens)
@@ -467,8 +469,8 @@
             halo,
         ],
         out_specs=(face, face),
-        compiler_params=vmem_limit(60),
-        cost_estimate=cost(3),
+        compiler_params=vmem_limit(24),
+        cost_estimate=cost(15),
         name="pack_y",
     )(velocity, pressure, cell_visc, cell_dens, low_x, high_x)
 
@@ -606,7 +608,7 @@
             pltpu.VMEM(block, f32),
             pltpu.VMEM(block, f32),
         ],
-        compiler_params=vmem_limit(60),
+        compiler_params=vmem_limit(40),
         cost_estimate=cost(20),
         name="all_sweeps",
     )(velocity, pressure, cell_visc, cell_dens, low_x, high_x, low_y, high_y)
@@ -629,8 +631,7 @@
     start_visc,
     marker_dens,
 ):
-    every = lax.all_gather(block_brick, "mark", axis=0)
-    asked = lax.dynamic_index_in_dim(every, lax.axis_index("mark"), axis=1, keepdims=False)
+    asked = lax.all_to_all(block_brick, "mark", 0, 0, tiled=True)
     fields = (velocity, pressure, cell_visc, cell_dens)
     to_low, to_high = pack_x(*fields)
     low_x, high_x = shift(to_high, "grid", 1), shift(to_low, "grid", -1)

time: 139 us -> 116 us (0.83)
  the two profiles are of different devices: /device:TPU:21 before, /device:TPU:18 now
where the time goes in v5:
time: 116 us; the launch traced here: 115 us
  Pallas kernels  60 us (52%)
  starting transfers between devices  23.4 us (20%)
  waiting for transfers between devices  12.4 us (11%)
  blocking collectives  10.1 us (9%)
  local copies, waits for them, and re-layouts  8.71 us (8%)
    pallas_call x1, Pallas kernels, marker_work(): pl.pallas_call(marker_body, grid=(owners, groups), out_shape=(jax.ShapeDt...  25.2 us
    pallas_call x1, Pallas kernels, all_sweeps(): pl.pallas_call(sweep_body, out_shape=(jax.ShapeDtypeStruct(velocity.shape...  18.4 us
    ppermute x4, starting transfers between devices, shift(): return lax.ppermute(value, axis, pairs)  12.3 us
    all_to_all x1, blocking collectives, per_device(): asked = lax.all_to_all(block_brick, 'mark', 0, 0, tiled=True)  10.1 us
    ppermute x4, waiting for transfers between devices, shift(): return lax.ppermute(value, axis, pairs)  8.91 us
    unnamed x26, local copies, waits for them, and re-layouts  8.71 us
    pallas_call x1, Pallas kernels, settle(): pl.pallas_call(settle_body, out_shape=(shape, shape), in_specs=[pl.BlockS...  6.6 us
    all_to_all x1, starting transfers between devices, per_device(): bricks = lax.all_to_all(picked, 'mark', 0, 0, tiled=True)  6.46 us
  transfers between devices with their start and end apart: 6, of which 3 were waited for; matrix products, arithmetic and copies ran while one was open for 0% of the time, Pallas kernels for 45%

profile of v5, /device:TPU:18, one launch (start us, length us, event | category | flops | bytes accessed | tf_op | source)
XLA Modules:
  0.0 115.4 jit_solution(2162605838948314023)
XLA Ops:
  0.6 1.4 %copy-done = f32[3,32,16,256]{3,2,1,0:T(8,128)S(1)} copy-done((f32[3,32,16,256]{3,2,1,0:T(8,128)S(1)}, f32[3,32,16,256]{3,2,1,0:T(8,128)}, u32[]{:S(2)}) %copy-start) | copy-done | bytes 1572888
  2.0 1.0 copy-done.2
  3.1 1.0 copy-done.4
  4.1 1.0 copy-done.8
  5.2 0.9 pack_x.1
  6.1 1.9 %collective-permute-start = (f32[6,4,16,256]{3,2,1,0:T(8,128)}, f32[6,4,16,256]{3,2,1,0:T(8,128)}, u32[]{:S(2)}, u32[]{:S(2)}) collective-permute-start(f32[6,4,16,256]{3,2,1,0:T(8,128)} %get-tuple-element.15), channel_id=1, source_target_pairs={{0,8},{8,16},{16,24},{1,9},{9,17},{17,25},{2,10},{10,18},{18,26},{... | collective-permute-start | bytes 1179656 | tf_op jit(solution)/shard_map/ppermute | solution.py:620
  8.0 3.6 %collective-permute-start.1 = (f32[6,4,16,256]{3,2,1,0:T(8,128)}, f32[6,4,16,256]{3,2,1,0:T(8,128)}, u32[]{:S(2)}, u32[]{:S(2)}) collective-permute-start(f32[6,4,16,256]{3,2,1,0:T(8,128)} %get-tuple-element.16), channel_id=1, source_target_pairs={{8,0},{16,8},{24,16},{9,1},{17,9},{25,17},{10,2},{18,10},{26,18},{... | collective-permute-start | bytes 1179656 | tf_op jit(solution)/shard_map/ppermute | solution.py:620
  11.7 10.1 %all_to_all.21 = s32[8,1,48]{2,1,0:T(1,128)S(1)} all-to-all(s32[8,1,48]{2,1,0:T(1,128)S(1)} %bitcast.4), channel_id=1, replica_groups=mesh['grid'=4,'mark'=8] {'mark'}, dimensions={0} | all-to-all | bytes 3072 | tf_op jit(solution)/shard_map/all_to_all | solution.py:634
  21.8 5.9 %pick_bricks.1 = f32[8,3,48,128]{3,2,1,0:T(8,128)} custom-call(s32[8,48]{1,0:T(8,128)S(1)} %bitcast.2, f32[3,32,16,256]{3,2,1,0:T(8,128)S(1)} %copy-done), custom_call_target="tpu_custom_call" | custom-call | flops 3449999872 | tf_op jit(solution)/shard_map/pick_bricks/pallas_call | solution.py:81
  27.7 6.5 %all-to-all-start.1 = ((f32[8,3,48,128]{3,2,1,0:T(8,128)}), f32[8,3,48,128]{3,2,1,0:T(8,128)}, u32[]{:S(2)}, u32[]{:S(2)}) async-start(f32[8,3,48,128]{3,2,1,0:T(8,128)} %pick_bricks.1), calls=%async_computation.1 | async-start | bytes 1179648 | tf_op jit(solution)/shard_map/all_to_all | solution.py:642
  34.2 2.9 %pack_y.1 = (f32[35,24,256]{2,1,0:T(8,128)}, f32[35,24,256]{2,1,0:T(8,128)}) custom-call(f32[3,32,16,256]{3,2,1,0:T(8,128)S(1)} %copy-done.1, f32[32,16,256]{2,1,0:T(8,128)S(1)} %copy-done.3, f32[32,16,256]{2,1,0:T(8,128)S(1)} %copy-done.5, f32[32,16,256]{2,1,0:T(8,128)S(1)} %copy-done.9, f32[6,4,16,256]{3,2,1,0:T(8,128)} %collective-permute-done.low_x, ...), custom_call_target="tpu_custom_call" | custom-call | flops 17250000896 | tf_op jit(solution)/shard_map/pack_y/pallas_call | solution.py:459
  37.1 3.4 %collective-permute-start.2 = (f32[35,24,256]{2,1,0:T(8,128)}, f32[35,24,256]{2,1,0:T(8,128)S(1)}, u32[]{:S(2)}, u32[]{:S(2)}) collective-permute-start(f32[35,24,256]{2,1,0:T(8,128)} %get-tuple-element.17._), channel_id=1, source_target_pairs={{0,1},{1,2},{2,3},{3,4},{4,5},{5,6},{6,7},{8,9},{9,10},{10,11},{11... | collective-permute-start | bytes 2580488 | tf_op jit(solution)/shard_map/ppermute | solution.py:620
  40.5 3.4 %collective-permute-start.3 = (f32[35,24,256]{2,1,0:T(8,128)}, f32[35,24,256]{2,1,0:T(8,128)}, u32[]{:S(2)}, u32[]{:S(2)}) collective-permute-start(f32[35,24,256]{2,1,0:T(8,128)} %get-tuple-element.18), channel_id=1, source_target_pairs={{1,0},{2,1},{3,2},{4,3},{5,4},{6,5},{7,6},{9,8},{10,9},{11,10},{12... | collective-permute-start | bytes 2580488 | tf_op jit(solution)/shard_map/ppermute | solution.py:620
  43.9 3.5 %all-to-all-done.1.brick = f32[8,3,48,128]{3,2,1,0:T(8,128)} async-done(((f32[8,3,48,128]{3,2,1,0:T(8,128)}), f32[8,3,48,128]{3,2,1,0:T(8,128)}, u32[]{:S(2)}, u32[]{:S(2)}) %all-to-all-start.1) | async-done | bytes 589856 | tf_op jit(solution)/shard_map/all_to_all | solution.py:642
  47.4 25.2 %marker_work.1 = (f32[8,48,256]{2,1,0:T(8,128)}, f32[8,3,48,128]{3,2,1,0:T(8,128)}) custom-call(s32[1,8]{1,0:T(1,128)} %counts.1, bf16[2,2,128,256]{3,2,1,0:T(8,128)(2,1)} %constant.4.clone.spread, bf16[512,512]{1,0:T(8,128)(2,1)} %constant.5.clone.gather, f32[8,3,48,256]{3,2,1,0:T(8,128)} %places.1, f32[8,48,256]{2,1,0:T(8,128)} %start.1, ...), custom_call_target="tpu_custom_call" | custom-call | flops 28750000128 | tf_op jit(solution)/shard_map/marker_work/pallas_call | solution.py:283
  72.6 4.7 %all-to-all-start.2 = ((f32[8,3,48,128]{3,2,1,0:T(8,128)}), f32[8,3,48,128]{3,2,1,0:T(8,128)S(1)}, u32[]{:S(2)}, u32[]{:S(2)}) async-start(f32[8,3,48,128]{3,2,1,0:T(8,128)} %get-tuple-element.21), calls=%async_computation.2 | async-start | bytes 1179648 | tf_op jit(solution)/shard_map/all_to_all | solution.py:646
  77.3 4.0 %collective-permute-done.2.low_y = f32[35,24,256]{2,1,0:T(8,128)S(1)} collective-permute-done((f32[35,24,256]{2,1,0:T(8,128)}, f32[35,24,256]{2,1,0:T(8,128)S(1)}, u32[]{:S(2)}, u32[]{:S(2)}) %collective-permute-start.2) | collective-permute-done | bytes 860192 | tf_op jit(solution)/shard_map/ppermute | solution.py:620
  81.3 4.9 %collective-permute-done.3.high_y = f32[35,24,256]{2,1,0:T(8,128)} collective-permute-done((f32[35,24,256]{2,1,0:T(8,128)}, f32[35,24,256]{2,1,0:T(8,128)}, u32[]{:S(2)}, u32[]{:S(2)}) %collective-permute-start.3) | collective-permute-done | bytes 860192 | tf_op jit(solution)/shard_map/ppermute | solution.py:620
  86.2 1.0 copy-done.6
  87.2 1.0 copy-done.10
  88.3 18.4 %all_sweeps.1 = (f32[3,32,16,256]{3,2,1,0:T(8,128)}, f32[32,16,256]{2,1,0:T(8,128)}) custom-call(f32[3,32,16,256]{3,2,1,0:T(8,128)S(1)} %copy-done.1, f32[32,16,256]{2,1,0:T(8,128)S(1)} %copy-done.3, f32[32,16,256]{2,1,0:T(8,128)S(1)} %copy-done.6, f32[32,16,256]{2,1,0:T(8,128)S(1)} %copy-done.10, f32[6,4,16,256]{3,2,1,0:T(8,128)} %collective-permute-done.low_x, ...), custom_call_target="tpu_custom_call" | custom-call | flops 23000000512 | tf_op jit(solution)/shard_map/all_sweeps/pallas_call | solution.py:596
  106.7 1.0 copy-done.7
  107.7 1.0 copy-done.11
  108.8 6.6 %settle.1 = (f32[32,16,256]{2,1,0:T(8,128)}, f32[32,16,256]{2,1,0:T(8,128)}) custom-call(s32[8,48]{1,0:T(8,128)S(1)} %bitcast.3, f32[8,3,48,128]{3,2,1,0:T(8,128)S(1)} %all-to-all-done.2.moments, f32[32,16,256]{2,1,0:T(8,128)S(1)} %copy-done.7, f32[32,16,256]{2,1,0:T(8,128)S(1)} %copy-done.11), custom_call_target="tpu_custom_call" | custom-call | flops 8049999872 | tf_op jit(solution)/shard_map/settle/pallas_call | solution.py:374
  (21 shorter events, 0.0 us)
Async XLA Ops:
  0.6 1.4 %copy-start = (f32[3,32,16,256]{3,2,1,0:T(8,128)S(1)}, f32[3,32,16,256]{3,2,1,0:T(8,128)}, u32[]{:S(2)}) copy-start(f32[3,32,16,256]{3,2,1,0:T(8,128)} %vel.5) | copy-start | bytes 4718596
  2.0 1.0 copy-start.2
  3.1 1.0 copy-start.4
  4.1 1.0 copy-start.8
  5.2 6.5 %copy-start.12 = (s32[8,48]{1,0:T(8,128)S(1)}, s32[8,48]{1,0:T(8,128)}, u32[]{:S(2)}) copy-start(s32[8,48]{1,0:T(8,128)} %param.15) | copy-start | bytes 4612
  6.1 28.1 %collective-permute-start = (f32[6,4,16,256]{3,2,1,0:T(8,128)}, f32[6,4,16,256]{3,2,1,0:T(8,128)}, u32[]{:S(2)}, u32[]{:S(2)}) collective-permute-start(f32[6,4,16,256]{3,2,1,0:T(8,128)} %get-tuple-element.15), channel_id=1, source_target_pairs={{0,8},{8,16},{16,24},{1,9},{9,17},{17,25},{2,10},{10,18},{18,26},{... | collective-permute-start | bytes 1179656 | tf_op jit(solution)/shard_map/ppermute | solution.py:620
  8.0 26.1 %collective-permute-start.1 = (f32[6,4,16,256]{3,2,1,0:T(8,128)}, f32[6,4,16,256]{3,2,1,0:T(8,128)}, u32[]{:S(2)}, u32[]{:S(2)}) collective-permute-start(f32[6,4,16,256]{3,2,1,0:T(8,128)} %get-tuple-element.16), channel_id=1, source_target_pairs={{8,0},{16,8},{24,16},{9,1},{17,9},{25,17},{10,2},{18,10},{26,18},{... | collective-permute-start | bytes 1179656 | tf_op jit(solution)/shard_map/ppermute | solution.py:620
  21.7 12.4 %copy-start.1 = (f32[3,32,16,256]{3,2,1,0:T(8,128)S(1)}, f32[3,32,16,256]{3,2,1,0:T(8,128)}, u32[]{:S(2)}) copy-start(f32[3,32,16,256]{3,2,1,0:T(8,128)} %vel.5) | copy-start | bytes 4718596
  21.7 12.4 %copy-start.3 = (f32[32,16,256]{2,1,0:T(8,128)S(1)}, f32[32,16,256]{2,1,0:T(8,128)}, u32[]{:S(2)}) copy-start(f32[32,16,256]{2,1,0:T(8,128)} %pres.3) | copy-start | bytes 1572868
  21.7 12.4 %copy-start.5 = (f32[32,16,256]{2,1,0:T(8,128)S(1)}, f32[32,16,256]{2,1,0:T(8,128)}, u32[]{:S(2)}) copy-start(f32[32,16,256]{2,1,0:T(8,128)} %visc.5) | copy-start | bytes 1572868
  21.7 12.4 %copy-start.9 = (f32[32,16,256]{2,1,0:T(8,128)S(1)}, f32[32,16,256]{2,1,0:T(8,128)}, u32[]{:S(2)}) copy-start(f32[32,16,256]{2,1,0:T(8,128)} %dens.7) | copy-start | bytes 1572868
  27.7 19.7 %all-to-all-start.1 = ((f32[8,3,48,128]{3,2,1,0:T(8,128)}), f32[8,3,48,128]{3,2,1,0:T(8,128)}, u32[]{:S(2)}, u32[]{:S(2)}) async-start(f32[8,3,48,128]{3,2,1,0:T(8,128)} %pick_bricks.1), calls=%async_computation.1 | async-start | bytes 1179648 | tf_op jit(solution)/shard_map/all_to_all | solution.py:642
  37.1 44.2 %collective-permute-start.2 = (f32[35,24,256]{2,1,0:T(8,128)}, f32[35,24,256]{2,1,0:T(8,128)S(1)}, u32[]{:S(2)}, u32[]{:S(2)}) collective-permute-start(f32[35,24,256]{2,1,0:T(8,128)} %get-tuple-element.17._), channel_id=1, source_target_pairs={{0,1},{1,2},{2,3},{3,4},{4,5},{5,6},{6,7},{8,9},{9,10},{10,11},{11... | collective-permute-start | bytes 2580488 | tf_op jit(solution)/shard_map/ppermute | solution.py:620
  40.5 45.7 %collective-permute-start.3 = (f32[35,24,256]{2,1,0:T(8,128)}, f32[35,24,256]{2,1,0:T(8,128)}, u32[]{:S(2)}, u32[]{:S(2)}) collective-permute-start(f32[35,24,256]{2,1,0:T(8,128)} %get-tuple-element.18), channel_id=1, source_target_pairs={{1,0},{2,1},{3,2},{4,3},{5,4},{6,5},{7,6},{9,8},{10,9},{11,10},{12... | collective-permute-start | bytes 2580488 | tf_op jit(solution)/shard_map/ppermute | solution.py:620
  72.6 34.1 %all-to-all-start.2 = ((f32[8,3,48,128]{3,2,1,0:T(8,128)}), f32[8,3,48,128]{3,2,1,0:T(8,128)S(1)}, u32[]{:S(2)}, u32[]{:S(2)}) async-start(f32[8,3,48,128]{3,2,1,0:T(8,128)} %get-tuple-element.21), calls=%async_computation.2 | async-start | bytes 1179648 | tf_op jit(solution)/shard_map/all_to_all | solution.py:646
  86.2 1.0 copy-start.6
  87.2 1.0 copy-start.10
  106.7 1.0 copy-start.7
  107.7 1.0 copy-start.11

commit v6 on v5

--- a/solution.py
+++ b/solution.py
@@ -88,7 +88,7 @@
         out_specs=pl.BlockSpec(memory_space=pltpu.VMEM),
         scratch_shapes=[pltpu.VMEM((places, ROWS, LANES), f32)],
         compiler_params=vmem_limit(24),
-        cost_estimate=cost(3),
+        cost_estimate=cost(25),
         name="pick_bricks",
     )(asked, velocity)
 
@@ -96,7 +96,7 @@
 def permutations():
     inside = BZ * HALF
     spread = np.zeros((2, 2, LANES, 4 * inside), np.float32)
-    gather = np.zeros((2 * BY * inside, BY * LANES), np.float32)
+    gather = np.zeros((2, BY * inside, BY * LANES), np.float32)
     for half in range(2):
         for slot in range(HALF):
             for z in range(BZ):
@@ -104,7 +104,7 @@
                 for part in range(4):
                     spread[half, part // 2, outer, part * inside + inner] = 1
                 for j in range(BY):
-                    gather[(half * BY + j) * inside + inner, j * LANES + outer] = 1
+                    gather[half, j * inside + inner, j * LANES + outer] = 1
     return jnp.asarray(spread, bf16), jnp.asarray(gather, bf16)
 
 
@@ -141,8 +141,8 @@
     return jnp.dot(a, b, preferred_element_type=f32)
 
 
-def gradients(products, weights_x, weights_y, markers):
-    (weight_x, slope_x), (weight_y, slope_y) = weights_x, weights_y
+def gradients(products, weights, markers):
+    weight_x, slope_x, weight_y, slope_y = ([weights[4 * n + i] for i in range(4)] for n in range(4))
     grads = []
     for c in range(3):
         lines = [[], [], []]
@@ -157,164 +157,198 @@
     return grads
 
 
-def marker_halves(halves, live_count, spread, gather, places, start, dens, brick, visc_out, work):
-    permuted, left, right, products, factors, planes_high, planes_low, sums = work
+def own_lanes():
+    shape = (HALF, 4 * BZ * HALF)
+    lane = lax.broadcasted_iota(jnp.int32, shape, 1)
+    return (lane % HALF == lax.broadcasted_iota(jnp.int32, shape, 0)).astype(f32)
+
+
+def first_stage(unit, ins, buffers):
+    spread, _, places, _, _, brick = ins
+    permuted, left, right, products, weights, _, planes_high, planes_low = buffers
+    owner, part = unit
     markers = places.shape[-1]
     inside = BZ * HALF
-    lane = lax.broadcasted_iota(jnp.int32, (HALF, 4 * inside), 1)
-    sub = lax.broadcasted_iota(jnp.int32, (HALF, 4 * inside), 0)
-    own = (lane % HALF == sub).astype(f32)
-    parts = split(brick)
-    weights = {}
-    for half in halves:
-        permuted[half] = dot(parts[0], spread[half, 0]) + dot(parts[1], spread[half, 1])
-        lo, hi = half * HALF, (half + 1) * HALF
-        weight_z, slope_z = axis_weights(places[0, 2, lo:hi, :], BZ)
+    own = own_lanes()
+    half = part & 1
+    parts = split(brick[owner, lax.shift_right_logical(part, 1)])
+    permuted[...] = dot(parts[0], spread[half, 0]) + dot(parts[1], spread[half, 1])
+    weight_z, slope_z = axis_weights(places[owner, 2, part], BZ)
+    for z in range(0, BZ, 2):
+        for column, values in ((0, weight_z), (1, slope_z)):
+            high, low = split(jnp.concatenate(values[z : z + 2], axis=0))
+            columns = slice(column * markers, (column + 1) * markers)
+            for n in range(4):
+                begin = n * inside + z * HALF
+                right[begin : begin + 2 * HALF, columns] = low if n % 2 else high
+    for row in range(0, ROWS, 2):
+        pair = [jnp.broadcast_to(permuted[r : r + 1, :], own.shape) * own for r in (row, row + 1)]
+        left[row * HALF : (row + 2) * HALF, :] = jnp.concatenate(pair, axis=0).astype(bf16)
+    products[...] = dot(left[...], right[...])
+    weights_x = axis_weights(places[owner, 0, part], BX)
+    weights_y = axis_weights(places[owner, 1, part], BY)
+    for n, values in enumerate((*weights_x, *weights_y)):
+        for i, value in enumerate(values):
+            weights[4 * n + i] = value
+    for j in range(BY):
         for z in range(0, BZ, 2):
-            for column, values in ((0, weight_z), (1, slope_z)):
-                high, low = split(jnp.concatenate(values[z : z + 2], axis=0))
-                columns = slice(column * markers, (column + 1) * markers)
-                for part in range(4):
-                    begin = part * inside + z * HALF
-                    right[half, begin : begin + 2 * HALF, columns] = low if part % 2 else high
-        for row in range(0, ROWS, 2):
-            pair = [
-                jnp.broadcast_to(permuted[half, r : r + 1, :], own.shape) * own
-                for r in (row, row + 1)
-            ]
-            left[half, row * HALF : (row + 2) * HALF, :] = jnp.concatenate(pair, axis=0).astype(
-                bf16
-            )
-        products[half] = dot(left[half], right[half])
-
-        weights_x = axis_weights(places[0, 0, lo:hi, :], BX)
-        weights_y = axis_weights(places[0, 1, lo:hi, :], BY)
-        weights[half] = (weights_x, weights_y)
-        for j in range(BY):
-            for z in range(0, BZ, 2):
-                pair = [weights_y[0][j] * weight_z[z + k] for k in range(2)]
-                rows = slice((j * BZ + z) * HALF, (j * BZ + z + 2) * HALF)
-                high, low = split(jnp.concatenate(pair, axis=0))
-                planes_high[half, rows, :] = high
-                planes_low[half, rows, :] = low
-
+            pair = [weights_y[0][j] * weight_z[z + k] for k in range(2)]
+            rows = slice((j * BZ + z) * HALF, (j * BZ + z + 2) * HALF)
+            high, low = split(jnp.concatenate(pair, axis=0))
+            planes_high[rows, :] = high
+            planes_low[rows, :] = low
+
+
+def second_stage(unit, counts, ins, buffers, outs, sums):
+    _, gather, places, start, dens, _ = ins
+    visc_out, moments_out = outs
+    _, _, _, products, weights, factors, planes_high, planes_low = buffers
+    owner, part = unit
+    markers = places.shape[-1]
+    inside = BZ * HALF
+    grads = gradients(products, weights, markers)
+    normal = grads[0][0] ** 2 + grads[1][1] ** 2 + grads[2][2] ** 2
+    shear_xy = 0.5 * (grads[0][1] + grads[1][0])
+    shear_xz = 0.5 * (grads[0][2] + grads[2][0])
+    shear_yz = 0.5 * (grads[1][2] + grads[2][1])
+    invariant = 0.5 * normal + shear_xy**2 + shear_xz**2 + shear_yz**2
+    third = jnp.log(1.0 + invariant * (1.0 / (STRAIN_SCALE * STRAIN_SCALE))) * (1.0 / 3.0)
+    first = start[owner, part]
+    slot = lax.broadcasted_iota(jnp.int32, first.shape, 0) + part * HALF
+    live = slot < counts[0, owner]
+    visc_out[owner, part] = jnp.where(live, first * jnp.exp(-third), 0.0)
+    carried = (
+        live.astype(f32),
+        jnp.where(live, jnp.log(first) - third, 0.0),
+        jnp.where(live, dens[owner, part], 0.0),
+    )
+    count = 3 * BX * HALF
+    for c in range(3):
+        for i in range(0, BX, 2):
+            pair = [carried[c] * weights[i + k] for k in range(2)]
+            row = (c * BX + i) * HALF
+            high, low = split(jnp.concatenate(pair, axis=0))
+            factors[row : row + 2 * HALF, :] = high
+            factors[count + row : count + row + 2 * HALF, :] = low
     contract = (((1,), (1,)), ((), ()))
-    for half in halves:
-        lo, hi = half * HALF, (half + 1) * HALF
-        weights_x, weights_y = weights[half]
-        grads = gradients(products.at[half], weights_x, weights_y, markers)
-        normal = grads[0][0] ** 2 + grads[1][1] ** 2 + grads[2][2] ** 2
-        shear_xy = 0.5 * (grads[0][1] + grads[1][0])
-        shear_xz = 0.5 * (grads[0][2] + grads[2][0])
-        shear_yz = 0.5 * (grads[1][2] + grads[2][1])
-        invariant = 0.5 * normal + shear_xy**2 + shear_xz**2 + shear_yz**2
-        third = jnp.log(1.0 + invariant * (1.0 / (STRAIN_SCALE * STRAIN_SCALE))) * (1.0 / 3.0)
-        first = start[0, lo:hi, :]
-        slot = lax.broadcasted_iota(jnp.int32, first.shape, 0) + lo
-        live = slot < live_count
-        visc_out[0, lo:hi, :] = jnp.where(live, first * jnp.exp(-third), 0.0)
-        carried = (
-            live.astype(f32),
-            jnp.where(live, jnp.log(first) - third, 0.0),
-            jnp.where(live, dens[0, lo:hi, :], 0.0),
-        )
-        count = 3 * BX * HALF
-        for c in range(3):
-            for i in range(0, BX, 2):
-                pair = [carried[c] * weights_x[0][i + k] for k in range(2)]
-                row = (c * BX + i) * HALF
-                high, low = split(jnp.concatenate(pair, axis=0))
-                factors[half, row : row + 2 * HALF, :] = high
-                factors[half, count + row : count + row + 2 * HALF, :] = low
-        both = lax.dot_general(
-            factors[half], planes_high[half], contract, preferred_element_type=f32
-        )
-        rest = lax.dot_general(
-            factors[half, :count], planes_low[half], contract, preferred_element_type=f32
-        )
-        total = both[:count] + both[count:] + rest
-        chosen = total.reshape(3 * BX, HALF, BY * inside) * own[None]
-        packed = jnp.sum(chosen, axis=1)
-        high, low = split(packed)
-        columns = slice(half * BY * inside, (half + 1) * BY * inside)
-        sums[: 3 * BX, columns] = high.astype(f32)
-        sums[16 : 16 + 3 * BX, columns] = low.astype(f32)
-
-
-def marker_body(
-    counts, spread, gather, places, start, dens, brick, _, visc_out, moments_out, *work
-):
-    owner, group = pl.program_id(0), pl.program_id(1)
-    live_count = counts[0, owner] - group * GROUP
-    sums = work[-1]
-
-    def run(halves):
-        marker_halves(
-            halves, live_count, spread, gather, places, start, dens, brick[0, 0], visc_out, work
-        )
-        moved = dot(sums[...].astype(bf16), gather[...])
-        moved = moved[: 3 * BX] + moved[16 : 16 + 3 * BX]
-        for j in range(BY):
-            rows = pl.ds(j, 3 * BX, stride=BY)
-            moments_out[0, 0, rows, :] = moved[:, j * LANES : (j + 1) * LANES]
-
-    @pl.when(live_count <= 0)
+    both = lax.dot_general(factors[...], planes_high[...], contract, preferred_element_type=f32)
+    rest = lax.dot_general(factors[:count], planes_low[...], contract, preferred_element_type=f32)
+    total = both[:count] + both[count:] + rest
+    chosen = total.reshape(3 * BX, HALF, BY * inside) * own_lanes()[None]
+    high, low = split(jnp.sum(chosen, axis=1))
+    sums[: 3 * BX, :] = high.astype(f32)
+    sums[16 : 16 + 3 * BX, :] = low.astype(f32)
+    moved = dot(sums[...].astype(bf16), gather[part & 1])
+    moved = moved[: 3 * BX] + moved[16 : 16 + 3 * BX]
+    group = lax.shift_right_logical(part, 1)
+    for j in range(BY):
+        rows = pl.ds(j, 3 * BX, stride=BY)
+        before = moments_out[owner, group, rows, :]
+        moments_out[owner, group, rows, :] = before + moved[:, j * LANES : (j + 1) * LANES]
+
+
+def marker_body(counts, *refs):
+    ins, outs, scratch = refs[:6], refs[7:9], refs[9:]
+    units, sums, *buffers = scratch
+    buffers = (buffers[0::2], buffers[1::2])
+    visc_out, moments_out = outs
+    owners, parts = visc_out.shape[:2]
+    visc_out[...] = jnp.zeros_like(visc_out)
+    moments_out[...] = jnp.zeros_like(moments_out)
+    sums[...] = jnp.zeros_like(sums)
+
+    def list_units(index, found):
+        number, dead = found
+        owner, part = index // parts, index % parts
+        live = part * HALF < counts[0, owner]
+
+        @pl.when(live)
+        def _():
+            units[2 * number] = owner
+            units[2 * number + 1] = part
+
+        return jnp.where(live, number + 1, number), jnp.where(live, dead, index)
+
+    number, dead = lax.fori_loop(0, owners * parts, list_units, (0, 0))
+
+    @pl.when(number % 2 == 1)
     def _():
-        visc_out[...] = jnp.zeros_like(visc_out)
-        moments_out[...] = jnp.zeros_like(moments_out)
-
-    @pl.when(jnp.logical_and(live_count > 0, live_count <= HALF))
+        units[2 * number] = dead // parts
+        units[2 * number + 1] = dead % parts
+
+    pairs = (number + 1) // 2
+
+    def unit(index):
+        return units[2 * index], units[2 * index + 1]
+
+    def first(index, buffer):
+        first_stage(unit(index), ins, buffers[buffer])
+
+    def second(index, buffer):
+        second_stage(unit(index), counts, ins, buffers[buffer], outs, sums)
+
+    @pl.when(pairs > 0)
     def _():
-        sums[...] = jnp.zeros_like(sums)
-        visc_out[:, HALF:, :] = jnp.zeros((1, HALF, visc_out.shape[-1]), f32)
-        run((0,))
-
-    @pl.when(live_count > HALF)
-    def _():
-        sums[...] = jnp.zeros_like(sums)
-        run((0, 1))
+        first(0, 0)
+
+        def both(pair, carry):
+            first(2 * pair + 1, 1)
+            second(2 * pair, 0)
+            first(2 * pair + 2, 0)
+            second(2 * pair + 1, 1)
+            return carry
+
+        lax.fori_loop(0, pairs - 1, both, 0)
+        first(2 * pairs - 1, 1)
+        second(2 * pairs - 2, 0)
+        second(2 * pairs - 1, 1)
 
 
 def marker_work(counts, positions, start_visc, marker_dens, bricks, after):
     owners, _, slots, markers = positions.shape
-    groups = slots // GROUP
+    groups, parts = slots // GROUP, slots // HALF
     spread, gather = permutations()
     width = 4 * BZ * HALF
-    return pl.pallas_call(
+    whole = pl.BlockSpec(memory_space=pltpu.VMEM)
+    buffers = (
+        pltpu.VMEM((ROWS, width), f32),
+        pltpu.VMEM((ROWS * HALF, width), bf16),
+        pltpu.VMEM((width, 2 * markers), bf16),
+        pltpu.VMEM((ROWS * HALF, 2 * markers), f32),
+        pltpu.VMEM((4 * 4, HALF, markers), f32),
+        pltpu.VMEM((2 * 3 * BX * HALF, markers), bf16),
+        pltpu.VMEM((BY * BZ * HALF, markers), bf16),
+        pltpu.VMEM((BY * BZ * HALF, markers), bf16),
+    )
+    visc, moments = pl.pallas_call(
         marker_body,
-        grid=(owners, groups),
         out_shape=(
-            jax.ShapeDtypeStruct((owners, slots, markers), f32),
+            jax.ShapeDtypeStruct((owners, parts, HALF, markers), f32),
             jax.ShapeDtypeStruct((owners, groups, ROWS, LANES), f32),
         ),
-        in_specs=[
-            pl.BlockSpec(memory_space=pltpu.SMEM),
-            pl.BlockSpec(spread.shape, lambda q, g: (0, 0, 0, 0)),
-            pl.BlockSpec(gather.shape, lambda q, g: (0, 0)),
-            pl.BlockSpec((1, 3, GROUP, markers), lambda q, g: (q, 0, g, 0)),
-            pl.BlockSpec((1, GROUP, markers), lambda q, g: (q, g, 0)),
-            pl.BlockSpec((1, GROUP, markers), lambda q, g: (q, g, 0)),
-            pl.BlockSpec((1, 1, ROWS, LANES), lambda q, g: (q, g, 0, 0)),
-            pl.BlockSpec(memory_space=pl.ANY),
-        ],
-        out_specs=(
-            pl.BlockSpec((1, GROUP, markers), lambda q, g: (q, g, 0)),
-            pl.BlockSpec((1, 1, ROWS, LANES), lambda q, g: (q, g, 0, 0)),
-        ),
+        in_specs=[pl.BlockSpec(memory_space=pltpu.SMEM)]
+        + [whole] * 6
+        + [pl.BlockSpec(memory_space=pl.ANY)],
+        out_specs=(whole, whole),
         scratch_shapes=[
-            pltpu.VMEM((2, ROWS, width), f32),
-            pltpu.VMEM((2, ROWS * HALF, width), bf16),
-            pltpu.VMEM((2, width, 2 * markers), bf16),
-            pltpu.VMEM((2, ROWS * HALF, 2 * markers), f32),
-            pltpu.VMEM((2, 2 * 3 * BX * HALF, markers), bf16),
-            pltpu.VMEM((2, BY * BZ * HALF, markers), bf16),
-            pltpu.VMEM((2, BY * BZ * HALF, markers), bf16),
-            pltpu.VMEM((32, 2 * BY * BZ * HALF), f32),
-        ],
+            pltpu.SMEM((2 * (owners * parts + 1),), jnp.int32),
+            pltpu.VMEM((32, BY * BZ * HALF), f32),
+        ]
+        + [buffer for buffer in buffers for _ in range(2)],
         compiler_params=vmem_limit(60),
         cost_estimate=cost(25),
         name="marker_work",
-    )(counts, spread, gather, positions, start_visc, marker_dens, bricks, after)
+    )(
+        counts,
+        spread,
+        gather,
+        positions.reshape(owners, 3, parts, HALF, markers),
+        start_visc.reshape(owners, parts, HALF, markers),
+        marker_dens.reshape(owners, parts, HALF, markers),
+        bricks,
+        after,
+    )
+    return visc.reshape(owners, slots, markers), moments
 
 
 def settle_body(asked, moments, visc, dens, visc_out, dens_out, *tables):
@@ -410,7 +444,7 @@
         out_shape=(shape, shape),
         in_specs=vel + block * 3,
         out_specs=(whole, whole),
-        compiler_params=vmem_limit(24),
+        compiler_params=vmem_limit(60),
         cost_estimate=cost(2),
         name="pack_x",
     )(velocity, velocity, pressure, pressure, cell_visc, cell_visc, cell_dens, cell_dens)

time: 116 us -> 109 us (0.940)
  starting transfers between devices: 23.4 us -> 40.7 us
  blocking collectives: 10.1 us -> 0 us
  waiting for transfers between devices: 12.4 us -> 4.43 us
  local copies, waits for them, and re-layouts: 8.71 us -> 4.18 us
  Pallas kernels: 60 us -> 57.6 us
    all_to_all x1, starting transfers between devices: 4.67 us -> 16.3 us  [per_device(): gathered = lax.all_to_all(moments, 'mark', 0, 0, tiled=True)]
    all_to_all x1 -> x0, blocking collectives: 10.1 us -> none  [per_device(): asked = lax.all_to_all(block_brick, 'mark', 0, 0, tiled=True)]
    ppermute x4, waiting for transfers between devices: 8.91 us -> 0.01 us  [shift(): return lax.ppermute(value, axis, pairs)]
    all_to_all x0 -> x1, starting transfers between devices: none -> 6.18 us  [per_device(): asked = lax.all_to_all(block_brick, 'mark', 0, 0, tiled=True)]
    unnamed x26 -> x16, local copies, waits for them, and re-layouts: 8.71 us -> 4.18 us
    pallas_call x1, Pallas kernels: 25.2 us -> 21.6 us  [marker_work(): pl.pallas_call(marker_body, out_shape=(jax.ShapeDtypeStruct((owners, part...]
    pallas_call x1, Pallas kernels: 0.93 us -> 2.17 us  [pack_x(): pl.pallas_call(pack_x_body, grid=(1,), out_shape=(shape, shape), in_specs...]
  transfers between devices with their start and end apart: 6 -> 7, of which waited for: 3 -> 1; matrix products, arithmetic and copies ran while one was open for 0% -> 0% of each run, Pallas kernels for 45% -> 47%
where the time goes in v6:
time: 109 us; the launch traced here: 108 us
  Pallas kernels  57.6 us (53%)
  starting transfers between devices  40.7 us (37%)
  waiting for transfers between devices  4.43 us (4%)
  local copies, waits for them, and re-layouts  4.18 us (4%)
    pallas_call x1, Pallas kernels, marker_work(): pl.pallas_call(marker_body, out_shape=(jax.ShapeDtypeStruct((owners, part...  21.6 us
    pallas_call x1, Pallas kernels, all_sweeps(): pl.pallas_call(sweep_body, out_shape=(jax.ShapeDtypeStruct(velocity.shape...  18.4 us
    all_to_all x1, starting transfers between devices, per_device(): gathered = lax.all_to_all(moments, 'mark', 0, 0, tiled=True)  16.3 us
    ppermute x4, starting transfers between devices, shift(): return lax.ppermute(value, axis, pairs)  12.3 us
    pallas_call x1, Pallas kernels, settle(): pl.pallas_call(settle_body, out_shape=(shape, shape), in_specs=[pl.BlockS...  6.59 us
    all_to_all x1, starting transfers between devices, per_device(): asked = lax.all_to_all(block_brick, 'mark', 0, 0, tiled=True)  6.18 us
    all_to_all x1, starting transfers between devices, per_device(): bricks = lax.all_to_all(picked, 'mark', 0, 0, tiled=True)  6 us
    pallas_call x1, Pallas kernels, pick_bricks(): pl.pallas_call(pick_body, out_shape=jax.ShapeDtypeStruct((devices, slots...  5.94 us
  transfers between devices with their start and end apart: 7, of which 1 were waited for; matrix products, arithmetic and copies ran while one was open for 0% of the time, Pallas kernels for 47%

profile of v6, /device:TPU:18, one launch (start us, length us, event | category | flops | bytes accessed | tf_op | source)
XLA Modules:
  0.0 107.7 jit_solution(3968440021850275037)
XLA Ops:
  0.6 6.2 %all-to-all-start = ((s32[8,1,48]{2,1,0:T(1,128)}), s32[8,1,48]{2,1,0:T(1,128)S(1)}, u32[]{:S(2)}, u32[]{:S(2)}) async-start(s32[8,1,48]{2,1,0:T(1,128)} %bitcast.8), calls=%async_computation | async-start | bytes 8192 | tf_op jit(solution)/shard_map/all_to_all | solution.py:668
  6.8 2.2 %pack_x.1 = (f32[6,4,16,256]{3,2,1,0:T(8,128)}, f32[6,4,16,256]{3,2,1,0:T(8,128)}) custom-call(f32[3,32,16,256]{3,2,1,0:T(8,128)} %vel.5, f32[3,32,16,256]{3,2,1,0:T(8,128)} %vel.5, f32[32,16,256]{2,1,0:T(8,128)} %pres.3, f32[32,16,256]{2,1,0:T(8,128)} %pres.3, f32[32,16,256]{2,1,0:T(8,128)} %visc.5, f32[32,16,256]{2,1,0:T(8,128)} %visc.5, ...), custom_call_target="tpu_custom_call" | custom-call | flops 2300000000 | tf_op jit(solution)/shard_map/pack_x/pallas_call | solution.py:441
  9.0 1.9 %collective-permute-start = (f32[6,4,16,256]{3,2,1,0:T(8,128)}, f32[6,4,16,256]{3,2,1,0:T(8,128)}, u32[]{:S(2)}, u32[]{:S(2)}) collective-permute-start(f32[6,4,16,256]{3,2,1,0:T(8,128)} %get-tuple-element.15), channel_id=1, source_target_pairs={{0,8},{8,16},{16,24},{1,9},{9,17},{17,25},{2,10},{10,18},{18,26},{... | collective-permute-start | bytes 1179656 | tf_op jit(solution)/shard_map/ppermute | solution.py:654
  10.9 3.6 %collective-permute-start.1 = (f32[6,4,16,256]{3,2,1,0:T(8,128)}, f32[6,4,16,256]{3,2,1,0:T(8,128)}, u32[]{:S(2)}, u32[]{:S(2)}) collective-permute-start(f32[6,4,16,256]{3,2,1,0:T(8,128)} %get-tuple-element.16), channel_id=1, source_target_pairs={{8,0},{16,8},{24,16},{9,1},{17,9},{25,17},{10,2},{18,10},{26,18},{... | collective-permute-start | bytes 1179656 | tf_op jit(solution)/shard_map/ppermute | solution.py:654
  14.6 0.0 all-to-all-done
  14.6 0.0 copy-start.1
  14.6 0.0 copy-start.2
  14.6 0.0 copy-start.5
  14.6 5.9 %pick_bricks.1 = f32[8,3,48,128]{3,2,1,0:T(8,128)} custom-call(s32[8,48]{1,0:T(8,128)S(1)} %bitcast.6, f32[3,32,16,256]{3,2,1,0:T(8,128)S(1)} %copy-done), custom_call_target="tpu_custom_call" | custom-call | flops 28750000128 | tf_op jit(solution)/shard_map/pick_bricks/pallas_call | solution.py:81
  20.5 6.0 %all-to-all-start.1 = ((f32[8,3,48,128]{3,2,1,0:T(8,128)}), f32[8,3,48,128]{3,2,1,0:T(8,128)}, u32[]{:S(2)}, u32[]{:S(2)}) async-start(f32[8,3,48,128]{3,2,1,0:T(8,128)} %pick_bricks.1), calls=%async_computation.1 | async-start | bytes 1179648 | tf_op jit(solution)/shard_map/all_to_all | solution.py:676
  26.6 2.9 %pack_y.1 = (f32[35,24,256]{2,1,0:T(8,128)}, f32[35,24,256]{2,1,0:T(8,128)}) custom-call(f32[3,32,16,256]{3,2,1,0:T(8,128)S(1)} %copy-done, f32[32,16,256]{2,1,0:T(8,128)S(1)} %copy-done.1, f32[32,16,256]{2,1,0:T(8,128)S(1)} %copy-done.2, f32[32,16,256]{2,1,0:T(8,128)S(1)} %copy-done.5, f32[6,4,16,256]{3,2,1,0:T(8,128)} %collective-permute-done.low_x, ...), custom_call_target="tpu_custom_call" | custom-call | flops 17250000896 | tf_op jit(solution)/shard_map/pack_y/pallas_call | solution.py:493
  29.5 3.4 %collective-permute-start.2 = (f32[35,24,256]{2,1,0:T(8,128)}, f32[35,24,256]{2,1,0:T(8,128)S(1)}, u32[]{:S(2)}, u32[]{:S(2)}) collective-permute-start(f32[35,24,256]{2,1,0:T(8,128)} %get-tuple-element.17.refs_6_), channel_id=1, source_target_pairs={{0,1},{1,2},{2,3},{3,4},{4,5},{5,6},{6,7},{8,9},{9,10},{10,11},{11... | collective-permute-start | bytes 2580488 | tf_op jit(solution)/shard_map/ppermute | solution.py:654
  32.9 3.4 %collective-permute-start.3 = (f32[35,24,256]{2,1,0:T(8,128)}, f32[35,24,256]{2,1,0:T(8,128)}, u32[]{:S(2)}, u32[]{:S(2)}) collective-permute-start(f32[35,24,256]{2,1,0:T(8,128)} %get-tuple-element.18), channel_id=1, source_target_pairs={{1,0},{2,1},{3,2},{4,3},{5,4},{6,5},{7,6},{9,8},{10,9},{11,10},{12... | collective-permute-start | bytes 2580488 | tf_op jit(solution)/shard_map/ppermute | solution.py:654
  36.3 4.4 %all-to-all-done.1.refs_5_ = f32[8,3,48,128]{3,2,1,0:T(8,128)} async-done(((f32[8,3,48,128]{3,2,1,0:T(8,128)}), f32[8,3,48,128]{3,2,1,0:T(8,128)}, u32[]{:S(2)}, u32[]{:S(2)}) %all-to-all-start.1) | async-done | bytes 589856 | tf_op jit(solution)/shard_map/all_to_all | solution.py:676
  40.7 21.6 %marker_work.1 = (f32[8,6,8,256]{3,2,1,0:T(8,128)}, f32[8,3,48,128]{3,2,1,0:T(8,128)}) custom-call(s32[1,8]{1,0:T(1,128)} %counts.1, bf16[2,2,128,256]{3,2,1,0:T(8,128)(2,1)} %constant.4.clone.refs_0_, bf16[2,256,512]{2,1,0:T(8,128)(2,1)} %constant.5.clone.refs_1_, f32[8,3,6,8,256]{4,3,2,1,0:T(8,128)} %bitcast.9, f32[8,6,8,256]{3,2,1,0:T(8,128)} %bitcast.10, ...), custom_call_target="tpu_custom_call" | custom-call | flops 28750000128 | tf_op jit(solution)/shard_map/marker_work/pallas_call | solution.py:323
  62.3 16.3 %all-to-all-start.2 = ((f32[8,3,48,128]{3,2,1,0:T(8,128)}), f32[8,3,48,128]{3,2,1,0:T(8,128)S(1)}, u32[]{:S(2)}, u32[]{:S(2)}) async-start(f32[8,3,48,128]{3,2,1,0:T(8,128)} %get-tuple-element.21), calls=%async_computation.2 | async-start | bytes 1179648 | tf_op jit(solution)/shard_map/all_to_all | solution.py:680
  78.5 0.0 copy-start.3
  78.5 1.0 copy-done.3
  79.6 1.0 copy-done.6
  80.6 18.4 %all_sweeps.1 = (f32[3,32,16,256]{3,2,1,0:T(8,128)}, f32[32,16,256]{2,1,0:T(8,128)}) custom-call(f32[3,32,16,256]{3,2,1,0:T(8,128)S(1)} %copy-done, f32[32,16,256]{2,1,0:T(8,128)S(1)} %copy-done.1, f32[32,16,256]{2,1,0:T(8,128)S(1)} %copy-done.3, f32[32,16,256]{2,1,0:T(8,128)S(1)} %copy-done.6, f32[6,4,16,256]{3,2,1,0:T(8,128)} %collective-permute-done.low_x, ...), custom_call_target="tpu_custom_call" | custom-call | flops 23000000512 | tf_op jit(solution)/shard_map/all_sweeps/pallas_call | solution.py:630
  99.0 0.0 all-to-all-done.2.moments
  99.0 1.0 copy-done.4
  100.1 1.0 copy-done.7
  101.1 6.6 %settle.1 = (f32[32,16,256]{2,1,0:T(8,128)}, f32[32,16,256]{2,1,0:T(8,128)}) custom-call(s32[8,48]{1,0:T(8,128)S(1)} %bitcast.7, f32[8,3,48,128]{3,2,1,0:T(8,128)S(1)} %all-to-all-done.2.moments, f32[32,16,256]{2,1,0:T(8,128)S(1)} %copy-done.4, f32[32,16,256]{2,1,0:T(8,128)S(1)} %copy-done.7), custom_call_target="tpu_custom_call" | custom-call | flops 8049999872 | tf_op jit(solution)/shard_map/settle/pallas_call | solution.py:408
  (12 shorter events, 0.0 us)
Async XLA Ops:
  0.6 13.9 %all-to-all-start = ((s32[8,1,48]{2,1,0:T(1,128)}), s32[8,1,48]{2,1,0:T(1,128)S(1)}, u32[]{:S(2)}, u32[]{:S(2)}) async-start(s32[8,1,48]{2,1,0:T(1,128)} %bitcast.8), calls=%async_computation | async-start | bytes 8192 | tf_op jit(solution)/shard_map/all_to_all | solution.py:668
  6.8 7.8 %copy-start = (f32[3,32,16,256]{3,2,1,0:T(8,128)S(1)}, f32[3,32,16,256]{3,2,1,0:T(8,128)}, u32[]{:S(2)}) copy-start(f32[3,32,16,256]{3,2,1,0:T(8,128)} %vel.5) | copy-start | bytes 4718596
  9.0 17.6 %collective-permute-start = (f32[6,4,16,256]{3,2,1,0:T(8,128)}, f32[6,4,16,256]{3,2,1,0:T(8,128)}, u32[]{:S(2)}, u32[]{:S(2)}) collective-permute-start(f32[6,4,16,256]{3,2,1,0:T(8,128)} %get-tuple-element.15), channel_id=1, source_target_pairs={{0,8},{8,16},{16,24},{1,9},{9,17},{17,25},{2,10},{10,18},{18,26},{... | collective-permute-start | bytes 1179656 | tf_op jit(solution)/shard_map/ppermute | solution.py:654
  10.9 15.7 %collective-permute-start.1 = (f32[6,4,16,256]{3,2,1,0:T(8,128)}, f32[6,4,16,256]{3,2,1,0:T(8,128)}, u32[]{:S(2)}, u32[]{:S(2)}) collective-permute-start(f32[6,4,16,256]{3,2,1,0:T(8,128)} %get-tuple-element.16), channel_id=1, source_target_pairs={{8,0},{16,8},{24,16},{9,1},{17,9},{25,17},{10,2},{18,10},{26,18},{... | collective-permute-start | bytes 1179656 | tf_op jit(solution)/shard_map/ppermute | solution.py:654
  14.6 12.0 %copy-start.1 = (f32[32,16,256]{2,1,0:T(8,128)S(1)}, f32[32,16,256]{2,1,0:T(8,128)}, u32[]{:S(2)}) copy-start(f32[32,16,256]{2,1,0:T(8,128)} %pres.3) | copy-start | bytes 1572868
  14.6 12.0 %copy-start.2 = (f32[32,16,256]{2,1,0:T(8,128)S(1)}, f32[32,16,256]{2,1,0:T(8,128)}, u32[]{:S(2)}) copy-start(f32[32,16,256]{2,1,0:T(8,128)} %visc.5) | copy-start | bytes 1572868
  14.6 12.0 %copy-start.5 = (f32[32,16,256]{2,1,0:T(8,128)S(1)}, f32[32,16,256]{2,1,0:T(8,128)}, u32[]{:S(2)}) copy-start(f32[32,16,256]{2,1,0:T(8,128)} %dens.5) | copy-start | bytes 1572868
  20.5 20.1 %all-to-all-start.1 = ((f32[8,3,48,128]{3,2,1,0:T(8,128)}), f32[8,3,48,128]{3,2,1,0:T(8,128)}, u32[]{:S(2)}, u32[]{:S(2)}) async-start(f32[8,3,48,128]{3,2,1,0:T(8,128)} %pick_bricks.1), calls=%async_computation.1 | async-start | bytes 1179648 | tf_op jit(solution)/shard_map/all_to_all | solution.py:676
  29.5 49.0 %collective-permute-start.2 = (f32[35,24,256]{2,1,0:T(8,128)}, f32[35,24,256]{2,1,0:T(8,128)S(1)}, u32[]{:S(2)}, u32[]{:S(2)}) collective-permute-start(f32[35,24,256]{2,1,0:T(8,128)} %get-tuple-element.17.refs_6_), channel_id=1, source_target_pairs={{0,1},{1,2},{2,3},{3,4},{4,5},{5,6},{6,7},{8,9},{9,10},{10,11},{11... | collective-permute-start | bytes 2580488 | tf_op jit(solution)/shard_map/ppermute | solution.py:654
  32.9 45.6 %collective-permute-start.3 = (f32[35,24,256]{2,1,0:T(8,128)}, f32[35,24,256]{2,1,0:T(8,128)}, u32[]{:S(2)}, u32[]{:S(2)}) collective-permute-start(f32[35,24,256]{2,1,0:T(8,128)} %get-tuple-element.18), channel_id=1, source_target_pairs={{1,0},{2,1},{3,2},{4,3},{5,4},{6,5},{7,6},{9,8},{10,9},{11,10},{12... | collective-permute-start | bytes 2580488 | tf_op jit(solution)/shard_map/ppermute | solution.py:654
  62.3 36.8 %all-to-all-start.2 = ((f32[8,3,48,128]{3,2,1,0:T(8,128)}), f32[8,3,48,128]{3,2,1,0:T(8,128)S(1)}, u32[]{:S(2)}, u32[]{:S(2)}) async-start(f32[8,3,48,128]{3,2,1,0:T(8,128)} %get-tuple-element.21), calls=%async_computation.2 | async-start | bytes 1179648 | tf_op jit(solution)/shard_map/all_to_all | solution.py:680
  78.5 1.0 copy-start.3
  79.6 1.0 copy-start.6
  99.0 1.0 copy-start.4
  100.1 1.0 copy-start.7

commit v7 on v6

--- a/solution.py
+++ b/solution.py
@@ -20,6 +20,7 @@
 LANES = 128
 GROUP = LANES // BZ
 HALF = 8
+SUBLANES = 8
 
 f32, bf16 = jnp.float32, jnp.bfloat16
 
@@ -287,21 +288,14 @@
     def second(index, buffer):
         second_stage(unit(index), counts, ins, buffers[buffer], outs, sums)
 
-    @pl.when(pairs > 0)
-    def _():
-        first(0, 0)
-
-        def both(pair, carry):
-            first(2 * pair + 1, 1)
-            second(2 * pair, 0)
-            first(2 * pair + 2, 0)
-            second(2 * pair + 1, 1)
-            return carry
-
-        lax.fori_loop(0, pairs - 1, both, 0)
-        first(2 * pairs - 1, 1)
-        second(2 * pairs - 2, 0)
-        second(2 * pairs - 1, 1)
+    def both(pair, carry):
+        first(2 * pair, 0)
+        first(2 * pair + 1, 1)
+        second(2 * pair, 0)
+        second(2 * pair + 1, 1)
+        return carry
+
+    lax.fori_loop(0, pairs, both, 0)
 
 
 def marker_work(counts, positions, start_visc, marker_dens, bricks, after):
@@ -351,11 +345,21 @@
     return visc.reshape(owners, slots, markers), moments
 
 
-def settle_body(asked, moments, visc, dens, visc_out, dens_out, *tables):
+def settle_body(asked, moments_in, visc_in, dens_in, visc_out, dens_out, *scratch):
+    moments, visc, dens, done, *tables = scratch
     size_x, size_y, size_z = visc.shape
+    copies = [
+        pltpu.make_async_copy(there, here, done.at[n])
+        for n, (there, here) in enumerate(
+            ((moments_in, moments), (visc_in, visc), (dens_in, dens))
+        )
+    ]
+    for copy in copies:
+        copy.start()
     bricks_y, halves = size_y // BY, size_z // LANES
     for table in tables:
         table[...] = jnp.zeros_like(table)
+    copies[0].wait()
     groups = moments.shape[1]
     lane_slot = lax.broadcasted_iota(jnp.int32, (ROWS, LANES), 1) // BZ
 
@@ -371,6 +375,8 @@
         return carry
 
     lax.fori_loop(0, moments.shape[0] * groups, one_group, 0)
+    copies[1].wait()
+    copies[2].wait()
 
     def finish(block_x, carry):
         for block_y in range(0, bricks_y, 2):
@@ -408,9 +414,16 @@
     return pl.pallas_call(
         settle_body,
         out_shape=(shape, shape),
-        in_specs=[pl.BlockSpec(memory_space=pltpu.SMEM), whole, whole, whole],
+        in_specs=[pl.BlockSpec(memory_space=pltpu.SMEM)]
+        + [pl.BlockSpec(memory_space=pl.ANY)] * 3,
         out_specs=(whole, whole),
-        scratch_shapes=[pltpu.VMEM((places, ROWS, LANES), f32)] * 2,
+        scratch_shapes=[
+            pltpu.VMEM(moments.shape, f32),
+            pltpu.VMEM(cell_visc.shape, f32),
+            pltpu.VMEM(cell_visc.shape, f32),
+            pltpu.SemaphoreType.DMA((3,)),
+        ]
+        + [pltpu.VMEM((places, ROWS, LANES), f32)] * 2,
         compiler_params=vmem_limit(24),
         cost_estimate=cost(7),
         name="settle",
@@ -510,40 +523,93 @@
 
 
 def sweep_body(vel, pres, visc, dens, low_x, high_x, low_y, high_y, vel_out, pres_out, *work):
-    fields, coefs, rate, relax, forcing = work
-    size_x, size_y, size_z = visc.shape
-    width = low_x.shape[1]
-    long_x = size_x + 2 * width
-    ring = fields.shape[3]
-    inner = slice(width, width + size_x)
-    own = slice(0, size_y)
-    for c in range(3):
-        fields[0, c, inner, own, :] = vel[c]
-    fields[0, 3, inner, own, :] = pres[...]
-    fields[1, 0, inner, own, :] = visc[...]
-    fields[1, 1, inner, own, :] = dens[...]
-    for f in range(6):
-        field = fields.at[0, f] if f < 4 else fields.at[1, f - 4]
-        rows = slice(f * width, (f + 1) * width)
-        for at, halo in ((0, low_x), (width + size_x, high_x)):
-            field[at : at + width, own, :] = halo[f]
-            field[at : at + width, size_y:, :] = jnp.zeros((width, 2 * width, size_z), f32)
-        field[inner, size_y : size_y + width, :] = high_y[:size_x, rows, :]
-        field[inner, size_y + width :, :] = low_y[:size_x, rows, :]
-        for side, far_x, far_y, plane, row in corner_rows(f):
-            at = width + size_x - 1 + far_x if side else width - far_x
-            field[at, size_y + far_y - 1] = high_y[size_x + plane, row]
-            field[at, ring - far_y] = low_y[size_x + plane, row]
-
-    lane = lax.broadcasted_iota(jnp.int32, (ring, size_z), 1)
+    blocks, sides_x, sides_y, results, fields, coefs, relax, forcing, rate, done = work
+    size_x, size_y, size_z = blocks.shape[1:]
+    width = SWEEPS
+    per, halves = fields.shape[1:3]
+    long_y = size_y + 2 * width
+    inputs = (
+        (visc, blocks.at[4]),
+        (vel, blocks.at[0:3]),
+        (pres, blocks.at[3]),
+        (dens, blocks.at[5]),
+        (low_x, sides_x.at[0]),
+        (high_x, sides_x.at[1]),
+        (low_y, sides_y.at[0]),
+        (high_y, sides_y.at[1]),
+    )
+    copies = [
+        pltpu.make_async_copy(there, here, done.at[n]) for n, (there, here) in enumerate(inputs)
+    ]
+    for copy in copies:
+        copy.start()
+
+    def place(x, y, rows):
+        return x % per, pl.ds(y * SUBLANES + x // per, rows, stride=SUBLANES)
+
+    def put(field, x, y, rows, value):
+        plane, lines = place(x, y, rows)
+        for half in range(halves):
+            fields[field, plane, half, lines, :] = value[:, half * LANES : (half + 1) * LANES]
+
+    def own_planes(field, carry):
+        for i in range(size_x):
+            for y in range(0, size_y, SUBLANES):
+                put(field, i + width, y + width, SUBLANES, blocks[field, i, y : y + SUBLANES, :])
+        return carry
+
+    def side_planes(field):
+        rows = slice(field * width, (field + 1) * width)
+        for side, begin in enumerate((0, width + size_x)):
+            for i in range(width):
+                for y in range(0, size_y, SUBLANES):
+                    value = sides_x[side, field, i, y : y + SUBLANES, :]
+                    put(field, begin + i, y + width, SUBLANES, value)
+                for y in (0, width + size_y):
+                    put(field, begin + i, y, width, jnp.zeros((width, size_z), f32))
+        for side, begin in enumerate((0, width + size_y)):
+            for i in range(size_x):
+                put(field, i + width, begin, width, sides_y[side, i, rows, :])
+
+    for copy in copies[:4]:
+        copy.wait()
+    lax.fori_loop(0, 6, own_planes, 0)
+    for copy in copies[4:]:
+        copy.wait()
+    for field in range(6):
+        side_planes(field)
+        for side, far_x, far_y, plane, row in corner_rows(field):
+            x = width + size_x - 1 + far_x if side else width - far_x
+            for end, y in enumerate((width - far_y, width + size_y - 1 + far_y)):
+                line = sides_y[end, size_x + plane, pl.ds(row, 1), :]
+                put(field, x, y, 1, line)
+
+    lane = lax.broadcasted_iota(jnp.int32, (SUBLANES, size_z), 1)
     not_last = (lane < size_z - 1).astype(f32)
     not_first = (lane > 0).astype(f32)
 
-    def up_y(a):
-        return pltpu.roll(a, ring - 1, 0)
-
-    def down_y(a):
-        return pltpu.roll(a, 1, 0)
+    def tile(y):
+        return pl.ds(pl.multiple_of(y * SUBLANES, SUBLANES), SUBLANES)
+
+    def take(field, plane, y):
+        return jnp.concatenate(
+            [fields[field, plane, half, tile(y), :] for half in range(halves)], axis=1
+        )
+
+    def store(field, plane, y, value):
+        for half in range(halves):
+            part = value[:, half * LANES : (half + 1) * LANES]
+            fields[field, plane, half, tile(y), :] = part
+
+    def up_x(field, plane, y):
+        if plane < per - 1:
+            return take(field, plane + 1, y)
+        return pltpu.roll(take(field, 0, y), SUBLANES - 1, 0)
+
+    def down_x(field, plane, y):
+        if plane > 0:
+            return take(field, plane - 1, y)
+        return pltpu.roll(take(field, per - 1, y), 1, 0)
 
     def up_z(a):
         return pltpu.roll(a, size_z - 1, 1)
@@ -551,98 +617,114 @@
     def down_z(a):
         return pltpu.roll(a, 1, 1)
 
-    def prepare(i, carry):
-        here = fields[1, 0, i]
-        near = [
-            fields[1, 0, i + 1],
-            fields[1, 0, i - 1],
-            up_y(here),
-            down_y(here),
-            up_z(here) * not_last,
-            down_z(here) * not_first,
-        ]
-        links = [0.5 * (here + other) for other in near]
-        diagonal = functools.reduce(jnp.add, links)
-        scale = jnp.where(here > 0.0, RELAX / diagonal, 0.0)
-        links[4] = links[4] * not_last
-        links[5] = links[5] * not_first
-        for n in range(6):
-            coefs[n, i] = links[n] * scale
-        relax[i] = scale
-        forcing[i] = fields[1, 1, i] * (-GRAVITY * scale)
-        rate[i] = PRESSURE_RATE * here
+    def prepare(y, carry):
+        for plane in range(per):
+            here = take(4, plane, y)
+            near = [
+                up_x(4, plane, y),
+                down_x(4, plane, y),
+                take(4, plane, y + 1),
+                take(4, plane, y - 1),
+                up_z(here) * not_last,
+                down_z(here) * not_first,
+            ]
+            links = [0.5 * (here + other) for other in near]
+            scale = jnp.where(here > 0.0, RELAX / add_all(links), 0.0)
+            links[4] = links[4] * not_last
+            links[5] = links[5] * not_first
+            for n in range(6):
+                coefs[n, plane, tile(y), :] = links[n] * scale
+            relax[plane, tile(y), :] = scale
+            forcing[plane, tile(y), :] = take(5, plane, y) * (-GRAVITY * scale)
+            rate[plane, tile(y), :] = PRESSURE_RATE * here
         return carry
 
-    lax.fori_loop(1, long_x - 1, prepare, 0, unroll=2)
+    lax.fori_loop(1, long_y - 1, prepare, 0)
 
     for sweep in range(SWEEPS):
-        old, new = sweep % 2, (sweep + 1) % 2
-        last = sweep == SWEEPS - 1
-
-        def one_plane(i, carry, old=old, new=new, last=last):
-            pressure = fields[old, 3, i]
-            scale = relax[i]
-            before = (
-                fields[old, 3, i - 1],
-                down_y(pressure),
-                down_z(pressure) * not_first,
-            )
-            divergence = None
-            for c in range(3):
-                here = fields[old, c, i]
-                near = [
-                    fields[old, c, i + 1],
-                    fields[old, c, i - 1],
-                    up_y(here),
-                    down_y(here),
-                    up_z(here),
-                    down_z(here),
-                ]
-                total = (1.0 - RELAX) * here - scale * (pressure - before[c])
-                for n, other in enumerate(near):
-                    total = total + coefs[n, i] * other
-                ahead = near[2 * c]
-                if c == 2:
-                    total = total + forcing[i]
-                    ahead = ahead * not_last
-                change = ahead - here
-                divergence = change if divergence is None else divergence + change
-                if last:
-                    vel_out[c, i - width] = total[:size_y]
-                else:
-                    fields[new, c, i] = total
-            pressed = pressure - rate[i] * divergence
-            if last:
-                pres_out[i - width] = pressed[:size_y]
-            else:
-                fields[new, 3, i] = pressed
+        old, new = (6, 0) if sweep % 2 else (0, 6)
+
+        def one_row(y, carry, old=old, new=new):
+            for plane in range(per):
+                pressure = take(old + 3, plane, y)
+                scale = relax[plane, tile(y), :]
+                before = (
+                    down_x(old + 3, plane, y),
+                    take(old + 3, plane, y - 1),
+                    down_z(pressure) * not_first,
+                )
+                divergence = None
+                for c in range(3):
+                    here = take(old + c, plane, y)
+                    near = [
+                        up_x(old + c, plane, y),
+                        down_x(old + c, plane, y),
+                        take(old + c, plane, y + 1),
+                        take(old + c, plane, y - 1),
+                        up_z(here),
+                        down_z(here),
+                    ]
+                    total = (1.0 - RELAX) * here - scale * (pressure - before[c])
+                    for n, other in enumerate(near):
+                        total = total + coefs[n, plane, tile(y), :] * other
+                    ahead = near[2 * c]
+                    if c == 2:
+                        total = total + forcing[plane, tile(y), :]
+                        ahead = ahead * not_last
+                    change = ahead - here
+                    divergence = change if divergence is None else divergence + change
+                    store(new + c, plane, y, total)
+                pressed = pressure - rate[plane, tile(y), :] * divergence
+                store(new + 3, plane, y, pressed)
             return carry
 
-        lax.fori_loop(1 + sweep, long_x - 1 - sweep, one_plane, 0, unroll=2)
+        lax.fori_loop(1 + sweep, long_y - 1 - sweep, one_row, 0)
+
+    final = 6 if SWEEPS % 2 else 0
+    outs = [vel_out.at[0], vel_out.at[1], vel_out.at[2], pres_out]
+    sends = [
+        pltpu.make_async_copy(results.at[n], out, done.at[n]) for n, out in enumerate(outs)
+    ]
+    for field, send in enumerate(sends):
+        for i in range(size_x):
+            for y in range(0, size_y, SUBLANES):
+                plane, lines = place(i + width, y + width, SUBLANES)
+                for half in range(halves):
+                    results[
+                        field, i, y : y + SUBLANES, half * LANES : (half + 1) * LANES
+                    ] = fields[final + field, plane, half, lines, :]
+        send.start()
+    for send in sends:
+        send.wait()
 
 
 def all_sweeps(velocity, pressure, cell_visc, cell_dens, low_x, high_x, low_y, high_y):
     size_x, size_y, size_z = cell_visc.shape
     width = low_x.shape[1]
-    long_x, ring = size_x + 2 * width, size_y + 2 * width
-    whole = pl.BlockSpec(memory_space=pltpu.VMEM)
-    block = (long_x, ring, size_z)
+    per, rows = (size_x + 2 * width) // SUBLANES, (size_y + 2 * width) * SUBLANES
+    block = (per, rows, size_z)
+    anywhere = pl.BlockSpec(memory_space=pl.ANY)
     return pl.pallas_call(
         sweep_body,
         out_shape=(
             jax.ShapeDtypeStruct(velocity.shape, f32),
             jax.ShapeDtypeStruct(pressure.shape, f32),
         ),
-        in_specs=[whole] * 8,
-        out_specs=(whole, whole),
+        in_specs=[anywhere] * 8,
+        out_specs=(anywhere, anywhere),
         scratch_shapes=[
-            pltpu.VMEM((2, 4) + block, f32),
+            pltpu.VMEM((6,) + cell_visc.shape, f32),
+            pltpu.VMEM((2,) + low_x.shape, f32),
+            pltpu.VMEM((2,) + low_y.shape, f32),
+            pltpu.VMEM((4,) + cell_visc.shape, f32),
+            pltpu.VMEM((10, per, size_z // LANES, rows, LANES), f32),
             pltpu.VMEM((6,) + block, f32),
             pltpu.VMEM(block, f32),
             pltpu.VMEM(block, f32),
             pltpu.VMEM(block, f32),
+            pltpu.SemaphoreType.DMA((8,)),
         ],
-        compiler_params=vmem_limit(40),
+        compiler_params=vmem_limit(44),
         cost_estimate=cost(20),
         name="all_sweeps",
     )(velocity, pressure, cell_visc, cell_dens, low_x, high_x, low_y, high_y)

time: 109 us -> 112 us (1.028); the launches traced: 108 us -> 112 us
  Pallas kernels: 57.6 us -> 68.8 us
  starting transfers between devices: 40.7 us -> 33.9 us
    pallas_call x1, Pallas kernels: 21.6 us -> 29.5 us  [marker_work(): pl.pallas_call(marker_body, out_shape=(jax.ShapeDtypeStruct((owners, part...]
    all_to_all x1, starting transfers between devices: 16.3 us -> 9.4 us  [per_device(): gathered = lax.all_to_all(moments, 'mark', 0, 0, tiled=True)]
    pallas_call x1, Pallas kernels: 18.4 us -> 21.4 us  [all_sweeps(): pl.pallas_call(sweep_body, out_shape=(jax.ShapeDtypeStruct(velocity.shape...]
  transfers between devices with their start and end apart: 7 -> 7, of which waited for: 1 -> 1; matrix products, arithmetic and copies ran while one was open for 0% -> 0% of each run, Pallas kernels for 47% -> 55%
where the time goes in v7:
time: 112 us
  Pallas kernels  68.8 us (61%)
  starting transfers between devices  33.9 us (30%)
  waiting for transfers between devices  4.43 us (4%)
  local copies, waits for them, and re-layouts  4.18 us (4%)
    pallas_call x1, Pallas kernels, marker_work(): pl.pallas_call(marker_body, out_shape=(jax.ShapeDtypeStruct((owners, part...  29.5 us
    pallas_call x1, Pallas kernels, all_sweeps(): pl.pallas_call(sweep_body, out_shape=(jax.ShapeDtypeStruct(velocity.shape...  21.4 us
    ppermute x4, starting transfers between devices, shift(): return lax.ppermute(value, axis, pairs)  12.3 us
    all_to_all x1, starting transfers between devices, per_device(): gathered = lax.all_to_all(moments, 'mark', 0, 0, tiled=True)  9.4 us
    pallas_call x1, Pallas kernels, settle(): pl.pallas_call(settle_body, out_shape=(shape, shape), in_specs=[pl.BlockS...  6.83 us
    all_to_all x1, starting transfers between devices, per_device(): asked = lax.all_to_all(block_brick, 'mark', 0, 0, tiled=True)  6.18 us
    all_to_all x1, starting transfers between devices, per_device(): bricks = lax.all_to_all(picked, 'mark', 0, 0, tiled=True)  6 us
    pallas_call x1, Pallas kernels, pick_bricks(): pl.pallas_call(pick_body, out_shape=jax.ShapeDtypeStruct((devices, slots...  5.94 us
  transfers between devices with their start and end apart: 7, of which 1 were waited for; matrix products, arithmetic and copies ran while one was open for 0% of the time, Pallas kernels for 55%

profile of v7, /device:TPU:18, one launch (start us, length us, event | category | flops | bytes accessed | tf_op | source)
XLA Modules:
  0.0 112.1 jit_solution(13228127476921252828)
XLA Ops:
  0.6 6.2 %all-to-all-start = ((s32[8,1,48]{2,1,0:T(1,128)}), s32[8,1,48]{2,1,0:T(1,128)S(1)}, u32[]{:S(2)}, u32[]{:S(2)}) async-start(s32[8,1,48]{2,1,0:T(1,128)} %bitcast.8), calls=%async_computation | async-start | bytes 8192 | tf_op jit(solution)/shard_map/all_to_all | solution.py:750
  6.8 2.2 %pack_x.1 = (f32[6,4,16,256]{3,2,1,0:T(8,128)}, f32[6,4,16,256]{3,2,1,0:T(8,128)}) custom-call(f32[3,32,16,256]{3,2,1,0:T(8,128)} %vel.5, f32[3,32,16,256]{3,2,1,0:T(8,128)} %vel.5, f32[32,16,256]{2,1,0:T(8,128)} %pres.3, f32[32,16,256]{2,1,0:T(8,128)} %pres.3, f32[32,16,256]{2,1,0:T(8,128)} %visc_in.1, f32[32,16,256]{2,1,0:T(8,128)} %visc_in.1, ...), custom_call_target="tpu_custom_call" | custom-call | flops 2300000000 | tf_op jit(solution)/shard_map/pack_x/pallas_call | solution.py:454
  9.0 1.9 %collective-permute-start = (f32[6,4,16,256]{3,2,1,0:T(8,128)}, f32[6,4,16,256]{3,2,1,0:T(8,128)}, u32[]{:S(2)}, u32[]{:S(2)}) collective-permute-start(f32[6,4,16,256]{3,2,1,0:T(8,128)} %get-tuple-element.15), channel_id=1, source_target_pairs={{0,8},{8,16},{16,24},{1,9},{9,17},{17,25},{2,10},{10,18},{18,26},{... | collective-permute-start | bytes 1179656 | tf_op jit(solution)/shard_map/ppermute | solution.py:736
  10.9 3.6 %collective-permute-start.1 = (f32[6,4,16,256]{3,2,1,0:T(8,128)}, f32[6,4,16,256]{3,2,1,0:T(8,128)}, u32[]{:S(2)}, u32[]{:S(2)}) collective-permute-start(f32[6,4,16,256]{3,2,1,0:T(8,128)} %get-tuple-element.16), channel_id=1, source_target_pairs={{8,0},{16,8},{24,16},{9,1},{17,9},{25,17},{10,2},{18,10},{26,18},{... | collective-permute-start | bytes 1179656 | tf_op jit(solution)/shard_map/ppermute | solution.py:736
  14.6 0.0 all-to-all-done
  14.6 0.0 copy-start.1
  14.6 0.0 copy-start.2
  14.6 0.0 copy-start.5
  14.6 5.9 %pick_bricks.1 = f32[8,3,48,128]{3,2,1,0:T(8,128)} custom-call(s32[8,48]{1,0:T(8,128)S(1)} %bitcast.6, f32[3,32,16,256]{3,2,1,0:T(8,128)S(1)} %copy-done), custom_call_target="tpu_custom_call" | custom-call | flops 28750000128 | tf_op jit(solution)/shard_map/pick_bricks/pallas_call | solution.py:82
  20.5 6.0 %all-to-all-start.1 = ((f32[8,3,48,128]{3,2,1,0:T(8,128)}), f32[8,3,48,128]{3,2,1,0:T(8,128)}, u32[]{:S(2)}, u32[]{:S(2)}) async-start(f32[8,3,48,128]{3,2,1,0:T(8,128)} %pick_bricks.1), calls=%async_computation.1 | async-start | bytes 1179648 | tf_op jit(solution)/shard_map/all_to_all | solution.py:758
  26.6 2.9 %pack_y.1 = (f32[35,24,256]{2,1,0:T(8,128)}, f32[35,24,256]{2,1,0:T(8,128)}) custom-call(f32[3,32,16,256]{3,2,1,0:T(8,128)S(1)} %copy-done, f32[32,16,256]{2,1,0:T(8,128)S(1)} %copy-done.1, f32[32,16,256]{2,1,0:T(8,128)S(1)} %copy-done.2, f32[32,16,256]{2,1,0:T(8,128)S(1)} %copy-done.5, f32[6,4,16,256]{3,2,1,0:T(8,128)} %collective-permute-done.low_x, ...), custom_call_target="tpu_custom_call" | custom-call | flops 17250000896 | tf_op jit(solution)/shard_map/pack_y/pallas_call | solution.py:506
  29.5 3.4 %collective-permute-start.2 = (f32[35,24,256]{2,1,0:T(8,128)}, f32[35,24,256]{2,1,0:T(8,128)S(1)}, u32[]{:S(2)}, u32[]{:S(2)}) collective-permute-start(f32[35,24,256]{2,1,0:T(8,128)} %get-tuple-element.17.refs_6_), channel_id=1, source_target_pairs={{0,1},{1,2},{2,3},{3,4},{4,5},{5,6},{6,7},{8,9},{9,10},{10,11},{11... | collective-permute-start | bytes 2580488 | tf_op jit(solution)/shard_map/ppermute | solution.py:736
  32.9 3.4 %collective-permute-start.3 = (f32[35,24,256]{2,1,0:T(8,128)}, f32[35,24,256]{2,1,0:T(8,128)}, u32[]{:S(2)}, u32[]{:S(2)}) collective-permute-start(f32[35,24,256]{2,1,0:T(8,128)} %get-tuple-element.18), channel_id=1, source_target_pairs={{1,0},{2,1},{3,2},{4,3},{5,4},{6,5},{7,6},{9,8},{10,9},{11,10},{12... | collective-permute-start | bytes 2580488 | tf_op jit(solution)/shard_map/ppermute | solution.py:736
  36.3 4.4 %all-to-all-done.1.refs_5_ = f32[8,3,48,128]{3,2,1,0:T(8,128)} async-done(((f32[8,3,48,128]{3,2,1,0:T(8,128)}), f32[8,3,48,128]{3,2,1,0:T(8,128)}, u32[]{:S(2)}, u32[]{:S(2)}) %all-to-all-start.1) | async-done | bytes 589856 | tf_op jit(solution)/shard_map/all_to_all | solution.py:758
  40.7 29.5 %marker_work.1 = (f32[8,6,8,256]{3,2,1,0:T(8,128)}, f32[8,3,48,128]{3,2,1,0:T(8,128)}) custom-call(s32[1,8]{1,0:T(1,128)} %counts.1, bf16[2,2,128,256]{3,2,1,0:T(8,128)(2,1)} %constant.4.clone.refs_0_, bf16[2,256,512]{2,1,0:T(8,128)(2,1)} %constant.5.clone.refs_1_, f32[8,3,6,8,256]{4,3,2,1,0:T(8,128)} %bitcast.9, f32[8,6,8,256]{3,2,1,0:T(8,128)} %bitcast.10, ...), custom_call_target="tpu_custom_call" | custom-call | flops 28750000128 | tf_op jit(solution)/shard_map/marker_work/pallas_call | solution.py:317
  70.2 9.4 %all-to-all-start.2 = ((f32[8,3,48,128]{3,2,1,0:T(8,128)}), f32[8,3,48,128]{3,2,1,0:T(8,128)S(1)}, u32[]{:S(2)}, u32[]{:S(2)}) async-start(f32[8,3,48,128]{3,2,1,0:T(8,128)} %get-tuple-element.21), calls=%async_computation.2 | async-start | bytes 1179648 | tf_op jit(solution)/shard_map/all_to_all | solution.py:762
  79.6 0.0 copy-start.3
  79.6 1.0 copy-done.3
  80.7 1.0 copy-done.6
  81.7 21.4 %all_sweeps.1 = (f32[3,32,16,256]{3,2,1,0:T(8,128)}, f32[32,16,256]{2,1,0:T(8,128)}) custom-call(f32[3,32,16,256]{3,2,1,0:T(8,128)S(1)} %copy-done, f32[32,16,256]{2,1,0:T(8,128)S(1)} %copy-done.1, f32[32,16,256]{2,1,0:T(8,128)S(1)} %copy-done.3, f32[32,16,256]{2,1,0:T(8,128)S(1)} %copy-done.6, f32[6,4,16,256]{3,2,1,0:T(8,128)} %collective-permute-done.low_x, ...), custom_call_target="tpu_custom_call" | custom-call | flops 23000000512 | tf_op jit(solution)/shard_map/all_sweeps/pallas_call | solution.py:707
  103.2 0.0 copy-start.4
  103.2 1.0 copy-done.4
  104.2 1.0 copy-done.7
  105.2 6.8 %settle.1 = (f32[32,16,256]{2,1,0:T(8,128)}, f32[32,16,256]{2,1,0:T(8,128)}) custom-call(s32[8,48]{1,0:T(8,128)S(1)} %bitcast.7, f32[8,3,48,128]{3,2,1,0:T(8,128)S(1)} %all-to-all-done.2.moments_in, f32[32,16,256]{2,1,0:T(8,128)S(1)} %copy-done.4, f32[32,16,256]{2,1,0:T(8,128)S(1)} %copy-done.7), custom_call_target="tpu_custom_call" | custom-call | flops 8049999872 | tf_op jit(solution)/shard_map/settle/pallas_call | solution.py:414
  (12 shorter events, 0.0 us)
Async XLA Ops:
  0.6 13.9 %all-to-all-start = ((s32[8,1,48]{2,1,0:T(1,128)}), s32[8,1,48]{2,1,0:T(1,128)S(1)}, u32[]{:S(2)}, u32[]{:S(2)}) async-start(s32[8,1,48]{2,1,0:T(1,128)} %bitcast.8), calls=%async_computation | async-start | bytes 8192 | tf_op jit(solution)/shard_map/all_to_all | solution.py:750
  6.8 7.8 %copy-start = (f32[3,32,16,256]{3,2,1,0:T(8,128)S(1)}, f32[3,32,16,256]{3,2,1,0:T(8,128)}, u32[]{:S(2)}) copy-start(f32[3,32,16,256]{3,2,1,0:T(8,128)} %vel.5) | copy-start | bytes 4718596
  9.0 17.6 %collective-permute-start = (f32[6,4,16,256]{3,2,1,0:T(8,128)}, f32[6,4,16,256]{3,2,1,0:T(8,128)}, u32[]{:S(2)}, u32[]{:S(2)}) collective-permute-start(f32[6,4,16,256]{3,2,1,0:T(8,128)} %get-tuple-element.15), channel_id=1, source_target_pairs={{0,8},{8,16},{16,24},{1,9},{9,17},{17,25},{2,10},{10,18},{18,26},{... | collective-permute-start | bytes 1179656 | tf_op jit(solution)/shard_map/ppermute | solution.py:736
  10.9 15.7 %collective-permute-start.1 = (f32[6,4,16,256]{3,2,1,0:T(8,128)}, f32[6,4,16,256]{3,2,1,0:T(8,128)}, u32[]{:S(2)}, u32[]{:S(2)}) collective-permute-start(f32[6,4,16,256]{3,2,1,0:T(8,128)} %get-tuple-element.16), channel_id=1, source_target_pairs={{8,0},{16,8},{24,16},{9,1},{17,9},{25,17},{10,2},{18,10},{26,18},{... | collective-permute-start | bytes 1179656 | tf_op jit(solution)/shard_map/ppermute | solution.py:736
  14.6 12.0 %copy-start.1 = (f32[32,16,256]{2,1,0:T(8,128)S(1)}, f32[32,16,256]{2,1,0:T(8,128)}, u32[]{:S(2)}) copy-start(f32[32,16,256]{2,1,0:T(8,128)} %pres.3) | copy-start | bytes 1572868
  14.6 12.0 %copy-start.2 = (f32[32,16,256]{2,1,0:T(8,128)S(1)}, f32[32,16,256]{2,1,0:T(8,128)}, u32[]{:S(2)}) copy-start(f32[32,16,256]{2,1,0:T(8,128)} %visc_in.1) | copy-start | bytes 1572868
  14.6 12.0 %copy-start.5 = (f32[32,16,256]{2,1,0:T(8,128)S(1)}, f32[32,16,256]{2,1,0:T(8,128)}, u32[]{:S(2)}) copy-start(f32[32,16,256]{2,1,0:T(8,128)} %dens_in.1) | copy-start | bytes 1572868
  20.5 20.1 %all-to-all-start.1 = ((f32[8,3,48,128]{3,2,1,0:T(8,128)}), f32[8,3,48,128]{3,2,1,0:T(8,128)}, u32[]{:S(2)}, u32[]{:S(2)}) async-start(f32[8,3,48,128]{3,2,1,0:T(8,128)} %pick_bricks.1), calls=%async_computation.1 | async-start | bytes 1179648 | tf_op jit(solution)/shard_map/all_to_all | solution.py:758
  29.5 50.1 %collective-permute-start.2 = (f32[35,24,256]{2,1,0:T(8,128)}, f32[35,24,256]{2,1,0:T(8,128)S(1)}, u32[]{:S(2)}, u32[]{:S(2)}) collective-permute-start(f32[35,24,256]{2,1,0:T(8,128)} %get-tuple-element.17.refs_6_), channel_id=1, source_target_pairs={{0,1},{1,2},{2,3},{3,4},{4,5},{5,6},{6,7},{8,9},{9,10},{10,11},{11... | collective-permute-start | bytes 2580488 | tf_op jit(solution)/shard_map/ppermute | solution.py:736
  32.9 46.7 %collective-permute-start.3 = (f32[35,24,256]{2,1,0:T(8,128)}, f32[35,24,256]{2,1,0:T(8,128)}, u32[]{:S(2)}, u32[]{:S(2)}) collective-permute-start(f32[35,24,256]{2,1,0:T(8,128)} %get-tuple-element.18), channel_id=1, source_target_pairs={{1,0},{2,1},{3,2},{4,3},{5,4},{6,5},{7,6},{9,8},{10,9},{11,10},{12... | collective-permute-start | bytes 2580488 | tf_op jit(solution)/shard_map/ppermute | solution.py:736
  70.2 32.9 %all-to-all-start.2 = ((f32[8,3,48,128]{3,2,1,0:T(8,128)}), f32[8,3,48,128]{3,2,1,0:T(8,128)S(1)}, u32[]{:S(2)}, u32[]{:S(2)}) async-start(f32[8,3,48,128]{3,2,1,0:T(8,128)} %get-tuple-element.21), calls=%async_computation.2 | async-start | bytes 1179648 | tf_op jit(solution)/shard_map/all_to_all | solution.py:762
  79.6 1.0 copy-start.3
  80.7 1.0 copy-start.6
  103.2 1.0 copy-start.4
  104.2 1.0 copy-start.7

commit v8 on v7

--- a/solution.py
+++ b/solution.py
@@ -97,7 +97,7 @@
 def permutations():
     inside = BZ * HALF
     spread = np.zeros((2, 2, LANES, 4 * inside), np.float32)
-    gather = np.zeros((2, BY * inside, BY * LANES), np.float32)
+    gather = np.zeros((2 * BY * inside, BY * LANES), np.float32)
     for half in range(2):
         for slot in range(HALF):
             for z in range(BZ):
@@ -105,7 +105,7 @@
                 for part in range(4):
                     spread[half, part // 2, outer, part * inside + inner] = 1
                 for j in range(BY):
-                    gather[half, j * inside + inner, j * LANES + outer] = 1
+                    gather[(half * BY + j) * inside + inner, j * LANES + outer] = 1
     return jnp.asarray(spread, bf16), jnp.asarray(gather, bf16)
 
 
@@ -164,138 +164,146 @@
     return (lane % HALF == lax.broadcasted_iota(jnp.int32, shape, 0)).astype(f32)
 
 
-def first_stage(unit, ins, buffers):
-    spread, _, places, _, _, brick = ins
-    permuted, left, right, products, weights, _, planes_high, planes_low = buffers
-    owner, part = unit
+def marker_groups(groups, counts, ins, outs, buffers, sums):
+    spread, gather, places, start, dens, brick = ins
+    visc_out, moments_out = outs
+    permuted, left, right, products, weights, factors, planes_high, planes_low = buffers
     markers = places.shape[-1]
     inside = BZ * HALF
     own = own_lanes()
-    half = part & 1
-    parts = split(brick[owner, lax.shift_right_logical(part, 1)])
-    permuted[...] = dot(parts[0], spread[half, 0]) + dot(parts[1], spread[half, 1])
-    weight_z, slope_z = axis_weights(places[owner, 2, part], BZ)
-    for z in range(0, BZ, 2):
-        for column, values in ((0, weight_z), (1, slope_z)):
-            high, low = split(jnp.concatenate(values[z : z + 2], axis=0))
-            columns = slice(column * markers, (column + 1) * markers)
-            for n in range(4):
-                begin = n * inside + z * HALF
-                right[begin : begin + 2 * HALF, columns] = low if n % 2 else high
-    for row in range(0, ROWS, 2):
-        pair = [jnp.broadcast_to(permuted[r : r + 1, :], own.shape) * own for r in (row, row + 1)]
-        left[row * HALF : (row + 2) * HALF, :] = jnp.concatenate(pair, axis=0).astype(bf16)
-    products[...] = dot(left[...], right[...])
-    weights_x = axis_weights(places[owner, 0, part], BX)
-    weights_y = axis_weights(places[owner, 1, part], BY)
-    for n, values in enumerate((*weights_x, *weights_y)):
-        for i, value in enumerate(values):
-            weights[4 * n + i] = value
-    for j in range(BY):
+    halves = [
+        (owner, 2 * group + half, half, 2 * n + half)
+        for n, (owner, group) in enumerate(groups)
+        for half in range(2)
+    ]
+    parts = [split(brick[owner, group]) for owner, group in groups]
+    for _, _, half, n in halves:
+        high, low = parts[n // 2]
+        permuted[n][...] = dot(high, spread[half, 0]) + dot(low, spread[half, 1])
+    heights = []
+    for owner, part, _, n in halves:
+        weight_z, slope_z = axis_weights(places[owner, 2, part], BZ)
+        heights.append(weight_z)
         for z in range(0, BZ, 2):
-            pair = [weights_y[0][j] * weight_z[z + k] for k in range(2)]
-            rows = slice((j * BZ + z) * HALF, (j * BZ + z + 2) * HALF)
-            high, low = split(jnp.concatenate(pair, axis=0))
-            planes_high[rows, :] = high
-            planes_low[rows, :] = low
-
-
-def second_stage(unit, counts, ins, buffers, outs, sums):
-    _, gather, places, start, dens, _ = ins
-    visc_out, moments_out = outs
-    _, _, _, products, weights, factors, planes_high, planes_low = buffers
-    owner, part = unit
-    markers = places.shape[-1]
-    inside = BZ * HALF
-    grads = gradients(products, weights, markers)
-    normal = grads[0][0] ** 2 + grads[1][1] ** 2 + grads[2][2] ** 2
-    shear_xy = 0.5 * (grads[0][1] + grads[1][0])
-    shear_xz = 0.5 * (grads[0][2] + grads[2][0])
-    shear_yz = 0.5 * (grads[1][2] + grads[2][1])
-    invariant = 0.5 * normal + shear_xy**2 + shear_xz**2 + shear_yz**2
-    third = jnp.log(1.0 + invariant * (1.0 / (STRAIN_SCALE * STRAIN_SCALE))) * (1.0 / 3.0)
-    first = start[owner, part]
-    slot = lax.broadcasted_iota(jnp.int32, first.shape, 0) + part * HALF
-    live = slot < counts[0, owner]
-    visc_out[owner, part] = jnp.where(live, first * jnp.exp(-third), 0.0)
-    carried = (
-        live.astype(f32),
-        jnp.where(live, jnp.log(first) - third, 0.0),
-        jnp.where(live, dens[owner, part], 0.0),
-    )
+            for column, values in ((0, weight_z), (1, slope_z)):
+                high, low = split(jnp.concatenate(values[z : z + 2], axis=0))
+                columns = slice(column * markers, (column + 1) * markers)
+                for k in range(4):
+                    begin = k * inside + z * HALF
+                    right[n][begin : begin + 2 * HALF, columns] = low if k % 2 else high
+    for _, _, _, n in halves:
+        for row in range(0, ROWS, 2):
+            pair = [
+                jnp.broadcast_to(permuted[n][r : r + 1, :], own.shape) * own for r in (row, row + 1)
+            ]
+            left[n][row * HALF : (row + 2) * HALF, :] = jnp.concatenate(pair, axis=0).astype(bf16)
+    for _, _, _, n in halves:
+        products[n][...] = dot(left[n][...], right[n][...])
+    for owner, part, _, n in halves:
+        weights_x = axis_weights(places[owner, 0, part], BX)
+        weights_y = axis_weights(places[owner, 1, part], BY)
+        for k, values in enumerate((*weights_x, *weights_y)):
+            for i, value in enumerate(values):
+                weights[n][4 * k + i] = value
+        for j in range(BY):
+            for z in range(0, BZ, 2):
+                pair = [weights_y[0][j] * heights[n][z + k] for k in range(2)]
+                rows = slice((j * BZ + z) * HALF, (j * BZ + z + 2) * HALF)
+                high, low = split(jnp.concatenate(pair, axis=0))
+                planes_high[n][rows, :] = high
+                planes_low[n][rows, :] = low
+
     count = 3 * BX * HALF
-    for c in range(3):
-        for i in range(0, BX, 2):
-            pair = [carried[c] * weights[i + k] for k in range(2)]
-            row = (c * BX + i) * HALF
-            high, low = split(jnp.concatenate(pair, axis=0))
-            factors[row : row + 2 * HALF, :] = high
-            factors[count + row : count + row + 2 * HALF, :] = low
+    for owner, part, _, n in halves:
+        grads = gradients(products[n], weights[n], markers)
+        normal = grads[0][0] ** 2 + grads[1][1] ** 2 + grads[2][2] ** 2
+        shear_xy = 0.5 * (grads[0][1] + grads[1][0])
+        shear_xz = 0.5 * (grads[0][2] + grads[2][0])
+        shear_yz = 0.5 * (grads[1][2] + grads[2][1])
+        invariant = 0.5 * normal + shear_xy**2 + shear_xz**2 + shear_yz**2
+        scaled = invariant * (1.0 / (STRAIN_SCALE * STRAIN_SCALE))
+        third = jnp.log(1.0 + scaled) * (1.0 / 3.0)
+        first = start[owner, part]
+        slot = lax.broadcasted_iota(jnp.int32, first.shape, 0) + part * HALF
+        live = slot < counts[0, owner]
+        visc_out[owner, part] = jnp.where(live, first * jnp.exp(-third), 0.0)
+        carried = (
+            live.astype(f32),
+            jnp.where(live, jnp.log(first) - third, 0.0),
+            jnp.where(live, dens[owner, part], 0.0),
+        )
+        for c in range(3):
+            for i in range(0, BX, 2):
+                pair = [carried[c] * weights[n][i + k] for k in range(2)]
+                row = (c * BX + i) * HALF
+                high, low = split(jnp.concatenate(pair, axis=0))
+                factors[n][row : row + 2 * HALF, :] = high
+                factors[n][count + row : count + row + 2 * HALF, :] = low
+
     contract = (((1,), (1,)), ((), ()))
-    both = lax.dot_general(factors[...], planes_high[...], contract, preferred_element_type=f32)
-    rest = lax.dot_general(factors[:count], planes_low[...], contract, preferred_element_type=f32)
-    total = both[:count] + both[count:] + rest
-    chosen = total.reshape(3 * BX, HALF, BY * inside) * own_lanes()[None]
-    high, low = split(jnp.sum(chosen, axis=1))
-    sums[: 3 * BX, :] = high.astype(f32)
-    sums[16 : 16 + 3 * BX, :] = low.astype(f32)
-    moved = dot(sums[...].astype(bf16), gather[part & 1])
-    moved = moved[: 3 * BX] + moved[16 : 16 + 3 * BX]
-    group = lax.shift_right_logical(part, 1)
-    for j in range(BY):
-        rows = pl.ds(j, 3 * BX, stride=BY)
-        before = moments_out[owner, group, rows, :]
-        moments_out[owner, group, rows, :] = before + moved[:, j * LANES : (j + 1) * LANES]
+    found = []
+    for _, _, _, n in halves:
+        both = lax.dot_general(
+            factors[n][...], planes_high[n][...], contract, preferred_element_type=f32
+        )
+        rest = lax.dot_general(
+            factors[n][:count], planes_low[n][...], contract, preferred_element_type=f32
+        )
+        found.append((both, rest))
+    for _, _, half, n in halves:
+        both, rest = found[n]
+        total = both[:count] + both[count:] + rest
+        chosen = total.reshape(3 * BX, HALF, BY * inside) * own[None]
+        high, low = split(jnp.sum(chosen, axis=1))
+        columns = slice(half * BY * inside, (half + 1) * BY * inside)
+        row = (n // 2) * 32
+        sums[row : row + 3 * BX, columns] = high.astype(f32)
+        sums[row + 16 : row + 16 + 3 * BX, columns] = low.astype(f32)
+    moved = dot(sums[...].astype(bf16), gather[...])
+    for n, (owner, group) in enumerate(groups):
+        mine = moved[32 * n : 32 * n + 3 * BX] + moved[32 * n + 16 : 32 * n + 16 + 3 * BX]
+        for j in range(BY):
+            rows = pl.ds(j, 3 * BX, stride=BY)
+            moments_out[owner, group, rows, :] = mine[:, j * LANES : (j + 1) * LANES]
+
+
+TOGETHER = 2
 
 
 def marker_body(counts, *refs):
     ins, outs, scratch = refs[:6], refs[7:9], refs[9:]
-    units, sums, *buffers = scratch
-    buffers = (buffers[0::2], buffers[1::2])
+    listed, sums, *flat = scratch
+    held = 2 * TOGETHER
+    buffers = [flat[n * held : (n + 1) * held] for n in range(len(flat) // held)]
     visc_out, moments_out = outs
-    owners, parts = visc_out.shape[:2]
+    owners, groups = moments_out.shape[:2]
     visc_out[...] = jnp.zeros_like(visc_out)
     moments_out[...] = jnp.zeros_like(moments_out)
     sums[...] = jnp.zeros_like(sums)
 
-    def list_units(index, found):
-        number, dead = found
-        owner, part = index // parts, index % parts
-        live = part * HALF < counts[0, owner]
+    def list_groups(index, number):
+        owner, group = index // groups, index % groups
+        live = group * GROUP < counts[0, owner]
 
         @pl.when(live)
         def _():
-            units[2 * number] = owner
-            units[2 * number + 1] = part
-
-        return jnp.where(live, number + 1, number), jnp.where(live, dead, index)
-
-    number, dead = lax.fori_loop(0, owners * parts, list_units, (0, 0))
-
-    @pl.when(number % 2 == 1)
-    def _():
-        units[2 * number] = dead // parts
-        units[2 * number + 1] = dead % parts
-
-    pairs = (number + 1) // 2
-
-    def unit(index):
-        return units[2 * index], units[2 * index + 1]
-
-    def first(index, buffer):
-        first_stage(unit(index), ins, buffers[buffer])
-
-    def second(index, buffer):
-        second_stage(unit(index), counts, ins, buffers[buffer], outs, sums)
-
-    def both(pair, carry):
-        first(2 * pair, 0)
-        first(2 * pair + 1, 1)
-        second(2 * pair, 0)
-        second(2 * pair + 1, 1)
+            for n in range(TOGETHER):
+                listed[2 * (number + n)] = owner
+                listed[2 * (number + n) + 1] = group
+
+        return jnp.where(live, number + 1, number)
+
+    number = lax.fori_loop(0, owners * groups, list_groups, 0)
+
+    def step(index, carry):
+        first = TOGETHER * index
+        taken = [
+            (listed[2 * (first + n)], listed[2 * (first + n) + 1]) for n in range(TOGETHER)
+        ]
+        marker_groups(taken, counts, ins, outs, buffers, sums)
         return carry
 
-    lax.fori_loop(0, pairs, both, 0)
+    lax.fori_loop(0, (number + TOGETHER - 1) // TOGETHER, step, 0)
 
 
 def marker_work(counts, positions, start_visc, marker_dens, bricks, after):
@@ -325,10 +333,10 @@
         + [pl.BlockSpec(memory_space=pl.ANY)],
         out_specs=(whole, whole),
         scratch_shapes=[
-            pltpu.SMEM((2 * (owners * parts + 1),), jnp.int32),
-            pltpu.VMEM((32, BY * BZ * HALF), f32),
+            pltpu.SMEM((2 * (owners * groups + TOGETHER),), jnp.int32),
+            pltpu.VMEM((32 * TOGETHER, 2 * BY * BZ * HALF), f32),
         ]
-        + [buffer for buffer in buffers for _ in range(2)],
+        + [buffer for buffer in buffers for _ in range(2 * TOGETHER)],
         compiler_params=vmem_limit(60),
         cost_estimate=cost(25),
         name="marker_work",
@@ -415,7 +423,8 @@
         settle_body,
         out_shape=(shape, shape),
         in_specs=[pl.BlockSpec(memory_space=pltpu.SMEM)]
-        + [pl.BlockSpec(memory_space=pl.ANY)] * 3,
+        + [pl.BlockSpec(memory_space=pl.ANY)]
+        + [pl.BlockSpec(memory_space=pltpu.HBM)] * 2,
         out_specs=(whole, whole),
         scratch_shapes=[
             pltpu.VMEM(moments.shape, f32),
@@ -424,7 +433,7 @@
             pltpu.SemaphoreType.DMA((3,)),
         ]
         + [pltpu.VMEM((places, ROWS, LANES), f32)] * 2,
-        compiler_params=vmem_limit(24),
+        compiler_params=vmem_limit(60),
         cost_estimate=cost(7),
         name="settle",
     )(asked, moments, cell_visc, cell_dens)
@@ -523,10 +532,10 @@
 
 
 def sweep_body(vel, pres, visc, dens, low_x, high_x, low_y, high_y, vel_out, pres_out, *work):
-    blocks, sides_x, sides_y, results, fields, coefs, relax, forcing, rate, done = work
+    blocks, sides_x, sides_y, results, even, odd, cells, coefs, relax, forcing, rate, done = work
     size_x, size_y, size_z = blocks.shape[1:]
     width = SWEEPS
-    per, halves = fields.shape[1:3]
+    per, halves = even.shape[1:3]
     long_y = size_y + 2 * width
     inputs = (
         (visc, blocks.at[4]),
@@ -549,14 +558,14 @@
 
     def put(field, x, y, rows, value):
         plane, lines = place(x, y, rows)
+        target = even.at[field] if field < 4 else cells.at[field - 4]
         for half in range(halves):
-            fields[field, plane, half, lines, :] = value[:, half * LANES : (half + 1) * LANES]
-
-    def own_planes(field, carry):
+            target[plane, half, lines, :] = value[:, half * LANES : (half + 1) * LANES]
+
+    def own_planes(field):
         for i in range(size_x):
             for y in range(0, size_y, SUBLANES):
                 put(field, i + width, y + width, SUBLANES, blocks[field, i, y : y + SUBLANES, :])
-        return carry
 
     def side_planes(field):
         rows = slice(field * width, (field + 1) * width)
@@ -571,9 +580,10 @@
             for i in range(size_x):
                 put(field, i + width, begin, width, sides_y[side, i, rows, :])
 
-    for copy in copies[:4]:
+    for copy, held in zip(copies, ((4,), (0, 1, 2), (3,), (5,))):
         copy.wait()
-    lax.fori_loop(0, 6, own_planes, 0)
+        for field in held:
+            own_planes(field)
     for copy in copies[4:]:
         copy.wait()
     for field in range(6):
@@ -593,13 +603,12 @@
 
     def take(field, plane, y):
         return jnp.concatenate(
-            [fields[field, plane, half, tile(y), :] for half in range(halves)], axis=1
+            [field[plane, half, tile(y), :] for half in range(halves)], axis=1
         )
 
     def store(field, plane, y, value):
         for half in range(halves):
-            part = value[:, half * LANES : (half + 1) * LANES]
-            fields[field, plane, half, tile(y), :] = part
+            field[plane, half, tile(y), :] = value[:, half * LANES : (half + 1) * LANES]
 
     def up_x(field, plane, y):
         if plane < per - 1:
@@ -618,13 +627,14 @@
         return pltpu.roll(a, 1, 1)
 
     def prepare(y, carry):
+        visc, dens = cells.at[0], cells.at[1]
         for plane in range(per):
-            here = take(4, plane, y)
+            here = take(visc, plane, y)
             near = [
-                up_x(4, plane, y),
-                down_x(4, plane, y),
-                take(4, plane, y + 1),
-                take(4, plane, y - 1),
+                up_x(visc, plane, y),
+                down_x(visc, plane, y),
+                take(visc, plane, y + 1),
+                take(visc, plane, y - 1),
                 up_z(here) * not_last,
                 down_z(here) * not_first,
             ]
@@ -635,52 +645,54 @@
             for n in range(6):
                 coefs[n, plane, tile(y), :] = links[n] * scale
             relax[plane, tile(y), :] = scale
-            forcing[plane, tile(y), :] = take(5, plane, y) * (-GRAVITY * scale)
+            forcing[plane, tile(y), :] = take(dens, plane, y) * (-GRAVITY * scale)
             rate[plane, tile(y), :] = PRESSURE_RATE * here
         return carry
 
-    lax.fori_loop(1, long_y - 1, prepare, 0)
+    lax.fori_loop(1, long_y - 1, prepare, 0, unroll=2)
 
     for sweep in range(SWEEPS):
-        old, new = (6, 0) if sweep % 2 else (0, 6)
+        old, new = (odd, even) if sweep % 2 else (even, odd)
 
         def one_row(y, carry, old=old, new=new):
             for plane in range(per):
-                pressure = take(old + 3, plane, y)
+                links = [coefs[n, plane, tile(y), :] for n in range(6)]
                 scale = relax[plane, tile(y), :]
+                pressure = take(old.at[3], plane, y)
                 before = (
-                    down_x(old + 3, plane, y),
-                    take(old + 3, plane, y - 1),
+                    down_x(old.at[3], plane, y),
+                    take(old.at[3], plane, y - 1),
                     down_z(pressure) * not_first,
                 )
-                divergence = None
+                changes = []
                 for c in range(3):
-                    here = take(old + c, plane, y)
+                    field = old.at[c]
+                    here = take(field, plane, y)
                     near = [
-                        up_x(old + c, plane, y),
-                        down_x(old + c, plane, y),
-                        take(old + c, plane, y + 1),
-                        take(old + c, plane, y - 1),
+                        up_x(field, plane, y),
+                        down_x(field, plane, y),
+                        take(field, plane, y + 1),
+                        take(field, plane, y - 1),
                         up_z(here),
                         down_z(here),
                     ]
-                    total = (1.0 - RELAX) * here - scale * (pressure - before[c])
-                    for n, other in enumerate(near):
-                        total = total + coefs[n, plane, tile(y), :] * other
+                    terms = [link * other for link, other in zip(links, near)]
+                    total = (terms[0] + terms[1]) + (terms[2] + terms[3])
+                    total = total + (terms[4] + terms[5])
+                    rest = (1.0 - RELAX) * here - scale * (pressure - before[c])
                     ahead = near[2 * c]
                     if c == 2:
-                        total = total + forcing[plane, tile(y), :]
+                        rest = rest + forcing[plane, tile(y), :]
                         ahead = ahead * not_last
-                    change = ahead - here
-                    divergence = change if divergence is None else divergence + change
-                    store(new + c, plane, y, total)
-                pressed = pressure - rate[plane, tile(y), :] * divergence
-                store(new + 3, plane, y, pressed)
+                    changes.append(ahead - here)
+                    store(new.at[c], plane, y, total + rest)
+                pressed = pressure - rate[plane, tile(y), :] * add_all(changes)
+                store(new.at[3], plane, y, pressed)
             return carry
 
-        lax.fori_loop(1 + sweep, long_y - 1 - sweep, one_row, 0)
-
-    final = 6 if SWEEPS % 2 else 0
+        lax.fori_loop(1 + sweep, long_y - 1 - sweep, one_row, 0, unroll=2)
+
+    final = odd if SWEEPS % 2 else even
     outs = [vel_out.at[0], vel_out.at[1], vel_out.at[2], pres_out]
     sends = [
         pltpu.make_async_copy(results.at[n], out, done.at[n]) for n, out in enumerate(outs)
@@ -692,7 +704,7 @@
                 for half in range(halves):
                     results[
                         field, i, y : y + SUBLANES, half * LANES : (half + 1) * LANES
-                    ] = fields[final + field, plane, half, lines, :]
+                    ] = final[field, plane, half, lines, :]
         send.start()
     for send in sends:
         send.wait()
@@ -704,20 +716,23 @@
     per, rows = (size_x + 2 * width) // SUBLANES, (size_y + 2 * width) * SUBLANES
     block = (per, rows, size_z)
     anywhere = pl.BlockSpec(memory_space=pl.ANY)
+    in_hbm = pl.BlockSpec(memory_space=pltpu.HBM)
     return pl.pallas_call(
         sweep_body,
         out_shape=(
             jax.ShapeDtypeStruct(velocity.shape, f32),
             jax.ShapeDtypeStruct(pressure.shape, f32),
         ),
-        in_specs=[anywhere] * 8,
+        in_specs=[in_hbm] * 4 + [anywhere] * 4,
         out_specs=(anywhere, anywhere),
         scratch_shapes=[
             pltpu.VMEM((6,) + cell_visc.shape, f32),
             pltpu.VMEM((2,) + low_x.shape, f32),
             pltpu.VMEM((2,) + low_y.shape, f32),
             pltpu.VMEM((4,) + cell_visc.shape, f32),
-            pltpu.VMEM((10, per, size_z // LANES, rows, LANES), f32),
+            pltpu.VMEM((4, per, size_z // LANES, rows, LANES), f32),
+            pltpu.VMEM((4, per, size_z // LANES, rows, LANES), f32),
+            pltpu.VMEM((2, per, size_z // LANES, rows, LANES), f32),
             pltpu.VMEM((6,) + block, f32),
             pltpu.VMEM(block, f32),
             pltpu.VMEM(block, f32),

time: 112 us -> 109 us (0.973)
  Pallas kernels: 68.8 us -> 50.1 us
  waiting for transfers between devices: 4.43 us -> 21.3 us
  starting transfers between devices: 33.9 us -> 31.7 us
    ppermute x4, waiting for transfers between devices: 0.01 us -> 16.7 us  [shift(): return lax.ppermute(value, axis, pairs)]
    pallas_call x1, Pallas kernels: 29.5 us -> 15.6 us  [marker_work(): pl.pallas_call(marker_body, out_shape=(jax.ShapeDtypeStruct((owners, part...]
    pallas_call x1, Pallas kernels: 21.4 us -> 15.9 us  [all_sweeps(): pl.pallas_call(sweep_body, out_shape=(jax.ShapeDtypeStruct(velocity.shape...]
    all_to_all x1, starting transfers between devices: 9.4 us -> 7.29 us  [per_device(): gathered = lax.all_to_all(moments, 'mark', 0, 0, tiled=True)]
    unnamed x16 -> x20, local copies, waits for them, and re-layouts: 4.18 us -> 4.15 us
  transfers between devices with their start and end apart: 7 -> 7, of which waited for: 1 -> 3; matrix products, arithmetic and copies ran while one was open for 0% -> 0% of each run, Pallas kernels for 55% -> 39%
where the time goes in v8:
time: 109 us; the launch traced here: 108 us
  Pallas kernels  50.1 us (46%)
  starting transfers between devices  31.7 us (29%)
  waiting for transfers between devices  21.3 us (20%)
  local copies, waits for them, and re-layouts  4.15 us (4%)
    ppermute x4, waiting for transfers between devices, shift(): return lax.ppermute(value, axis, pairs)  16.7 us
    pallas_call x1, Pallas kernels, all_sweeps(): pl.pallas_call(sweep_body, out_shape=(jax.ShapeDtypeStruct(velocity.shape...  15.9 us
    pallas_call x1, Pallas kernels, marker_work(): pl.pallas_call(marker_body, out_shape=(jax.ShapeDtypeStruct((owners, part...  15.6 us
    ppermute x4, starting transfers between devices, shift(): return lax.ppermute(value, axis, pairs)  12.3 us
    pallas_call x1, Pallas kernels, settle(): pl.pallas_call(settle_body, out_shape=(shape, shape), in_specs=[pl.BlockS...  7.6 us
    all_to_all x1, starting transfers between devices, per_device(): gathered = lax.all_to_all(moments, 'mark', 0, 0, tiled=True)  7.29 us
    all_to_all x1, starting transfers between devices, per_device(): asked = lax.all_to_all(block_brick, 'mark', 0, 0, tiled=True)  6.18 us
    all_to_all x1, starting transfers between devices, per_device(): bricks = lax.all_to_all(picked, 'mark', 0, 0, tiled=True)  6 us
  transfers between devices with their start and end apart: 7, of which 3 were waited for; matrix products, arithmetic and copies ran while one was open for 0% of the time, Pallas kernels for 39%

profile of v8, /device:TPU:18, one launch (start us, length us, event | category | flops | bytes accessed | tf_op | source)
XLA Modules:
  0.0 108.1 jit_solution(11530900456274066624)
XLA Ops:
  0.6 6.2 %all-to-all-start = ((s32[8,1,48]{2,1,0:T(1,128)}), s32[8,1,48]{2,1,0:T(1,128)S(1)}, u32[]{:S(2)}, u32[]{:S(2)}) async-start(s32[8,1,48]{2,1,0:T(1,128)} %bitcast.8), calls=%async_computation | async-start | bytes 8192 | tf_op jit(solution)/shard_map/all_to_all | solution.py:765
  6.8 2.2 %pack_x.1 = (f32[6,4,16,256]{3,2,1,0:T(8,128)}, f32[6,4,16,256]{3,2,1,0:T(8,128)}) custom-call(f32[3,32,16,256]{3,2,1,0:T(8,128)} %vel.5, f32[3,32,16,256]{3,2,1,0:T(8,128)} %vel.5, f32[32,16,256]{2,1,0:T(8,128)} %pres.3, f32[32,16,256]{2,1,0:T(8,128)} %pres.3, f32[32,16,256]{2,1,0:T(8,128)} %visc_in.1, f32[32,16,256]{2,1,0:T(8,128)} %visc_in.1, ...), custom_call_target="tpu_custom_call" | custom-call | flops 2300000000 | tf_op jit(solution)/shard_map/pack_x/pallas_call | solution.py:463
  9.0 1.9 %collective-permute-start = (f32[6,4,16,256]{3,2,1,0:T(8,128)}, f32[6,4,16,256]{3,2,1,0:T(8,128)S(1)}, u32[]{:S(2)}, u32[]{:S(2)}) collective-permute-start(f32[6,4,16,256]{3,2,1,0:T(8,128)} %get-tuple-element.15), channel_id=1, source_target_pairs={{0,8},{8,16},{16,24},{1,9},{9,17},{17,25},{2,10},{10,18},{18,26},{... | collective-permute-start | bytes 1179656 | tf_op jit(solution)/shard_map/ppermute | solution.py:751
  10.9 3.6 %collective-permute-start.1 = (f32[6,4,16,256]{3,2,1,0:T(8,128)}, f32[6,4,16,256]{3,2,1,0:T(8,128)}, u32[]{:S(2)}, u32[]{:S(2)}) collective-permute-start(f32[6,4,16,256]{3,2,1,0:T(8,128)} %get-tuple-element.16), channel_id=1, source_target_pairs={{8,0},{16,8},{24,16},{9,1},{17,9},{25,17},{10,2},{18,10},{26,18},{... | collective-permute-start | bytes 1179656 | tf_op jit(solution)/shard_map/ppermute | solution.py:751
  14.6 0.0 all-to-all-done
  14.6 0.0 copy-start.2
  14.6 0.0 copy-start.4
  14.6 0.0 copy-start.6
  14.6 6.0 %pick_bricks.1 = f32[8,3,48,128]{3,2,1,0:T(8,128)} custom-call(s32[8,48]{1,0:T(8,128)S(1)} %bitcast.6, f32[3,32,16,256]{3,2,1,0:T(8,128)S(1)} %copy-done.1), custom_call_target="tpu_custom_call" | custom-call | flops 28750000128 | tf_op jit(solution)/shard_map/pick_bricks/pallas_call | solution.py:82
  20.6 6.0 %all-to-all-start.1 = ((f32[8,3,48,128]{3,2,1,0:T(8,128)}), f32[8,3,48,128]{3,2,1,0:T(8,128)}, u32[]{:S(2)}, u32[]{:S(2)}) async-start(f32[8,3,48,128]{3,2,1,0:T(8,128)} %pick_bricks.1), calls=%async_computation.1 | async-start | bytes 1179648 | tf_op jit(solution)/shard_map/all_to_all | solution.py:773
  26.6 2.8 %pack_y.1 = (f32[35,24,256]{2,1,0:T(8,128)}, f32[35,24,256]{2,1,0:T(8,128)}) custom-call(f32[3,32,16,256]{3,2,1,0:T(8,128)S(1)} %copy-done.1, f32[32,16,256]{2,1,0:T(8,128)S(1)} %copy-done.2, f32[32,16,256]{2,1,0:T(8,128)S(1)} %copy-done.4, f32[32,16,256]{2,1,0:T(8,128)S(1)} %copy-done.6, f32[6,4,16,256]{3,2,1,0:T(8,128)S(1)} %collective-permute-done.low_x, ...), custom_call_target="tpu_custom_call" | custom-call | flops 17250000896 | tf_op jit(solution)/shard_map/pack_y/pallas_call | solution.py:515
  29.5 3.4 %collective-permute-start.2 = (f32[35,24,256]{2,1,0:T(8,128)}, f32[35,24,256]{2,1,0:T(8,128)S(1)}, u32[]{:S(2)}, u32[]{:S(2)}) collective-permute-start(f32[35,24,256]{2,1,0:T(8,128)} %get-tuple-element.17.refs_6_), channel_id=1, source_target_pairs={{0,1},{1,2},{2,3},{3,4},{4,5},{5,6},{6,7},{8,9},{9,10},{10,11},{11... | collective-permute-start | bytes 2580488 | tf_op jit(solution)/shard_map/ppermute | solution.py:751
  32.8 3.4 %collective-permute-start.3 = (f32[35,24,256]{2,1,0:T(8,128)}, f32[35,24,256]{2,1,0:T(8,128)S(1)}, u32[]{:S(2)}, u32[]{:S(2)}) collective-permute-start(f32[35,24,256]{2,1,0:T(8,128)} %get-tuple-element.18), channel_id=1, source_target_pairs={{1,0},{2,1},{3,2},{4,3},{5,4},{6,5},{7,6},{9,8},{10,9},{11,10},{12... | collective-permute-start | bytes 2580488 | tf_op jit(solution)/shard_map/ppermute | solution.py:751
  36.2 4.5 %all-to-all-done.1.refs_5_ = f32[8,3,48,128]{3,2,1,0:T(8,128)} async-done(((f32[8,3,48,128]{3,2,1,0:T(8,128)}), f32[8,3,48,128]{3,2,1,0:T(8,128)}, u32[]{:S(2)}, u32[]{:S(2)}) %all-to-all-start.1) | async-done | bytes 589856 | tf_op jit(solution)/shard_map/all_to_all | solution.py:773
  40.7 15.6 %marker_work.1 = (f32[8,6,8,256]{3,2,1,0:T(8,128)}, f32[8,3,48,128]{3,2,1,0:T(8,128)}) custom-call(s32[1,8]{1,0:T(1,128)} %counts.1, bf16[2,2,128,256]{3,2,1,0:T(8,128)(2,1)} %constant.4.clone.refs_0_, bf16[512,512]{1,0:T(8,128)(2,1)} %constant.5.clone.refs_1_, f32[8,3,6,8,256]{4,3,2,1,0:T(8,128)} %bitcast.9, f32[8,6,8,256]{3,2,1,0:T(8,128)} %bitcast.10, ...), custom_call_target="tpu_custom_call" | custom-call | flops 28750000128 | tf_op jit(solution)/shard_map/marker_work/pallas_call | solution.py:325
  56.4 7.3 %all-to-all-start.2 = ((f32[8,3,48,128]{3,2,1,0:T(8,128)}), f32[8,3,48,128]{3,2,1,0:T(8,128)}, u32[]{:S(2)}, u32[]{:S(2)}) async-start(f32[8,3,48,128]{3,2,1,0:T(8,128)} %get-tuple-element.21), calls=%async_computation.2 | async-start | bytes 1179648 | tf_op jit(solution)/shard_map/all_to_all | solution.py:777
  63.7 11.8 %collective-permute-done.2.low_y = f32[35,24,256]{2,1,0:T(8,128)S(1)} collective-permute-done((f32[35,24,256]{2,1,0:T(8,128)}, f32[35,24,256]{2,1,0:T(8,128)S(1)}, u32[]{:S(2)}, u32[]{:S(2)}) %collective-permute-start.2) | collective-permute-done | bytes 860192 | tf_op jit(solution)/shard_map/ppermute | solution.py:751
  75.5 4.9 %collective-permute-done.3.high_y = f32[35,24,256]{2,1,0:T(8,128)S(1)} collective-permute-done((f32[35,24,256]{2,1,0:T(8,128)}, f32[35,24,256]{2,1,0:T(8,128)S(1)}, u32[]{:S(2)}, u32[]{:S(2)}) %collective-permute-start.3) | collective-permute-done | bytes 860192 | tf_op jit(solution)/shard_map/ppermute | solution.py:751
  80.4 1.0 copy-done.3
  81.4 1.0 copy-done.5
  82.5 1.0 copy-done.7
  83.5 1.0 copy-done.9
  84.5 15.9 %all_sweeps.1 = (f32[3,32,16,256]{3,2,1,0:T(8,128)}, f32[32,16,256]{2,1,0:T(8,128)}) custom-call(f32[3,32,16,256]{3,2,1,0:T(8,128)S(1)} %copy-done.1, f32[32,16,256]{2,1,0:T(8,128)S(1)} %copy-done.3, f32[32,16,256]{2,1,0:T(8,128)S(1)} %copy-done.5, f32[32,16,256]{2,1,0:T(8,128)S(1)} %copy-done.7, f32[6,4,16,256]{3,2,1,0:T(8,128)S(1)} %copy-done.9, ...), custom_call_target="tpu_custom_call" | custom-call | flops 23000000512 | tf_op jit(solution)/shard_map/all_sweeps/pallas_call | solution.py:720
  100.5 7.6 %settle.1 = (f32[32,16,256]{2,1,0:T(8,128)}, f32[32,16,256]{2,1,0:T(8,128)}) custom-call(s32[8,48]{1,0:T(8,128)} %bitcast.7, f32[8,3,48,128]{3,2,1,0:T(8,128)} %all-to-all-done.2.moments_in, f32[32,16,256]{2,1,0:T(8,128)} %visc_in.1, f32[32,16,256]{2,1,0:T(8,128)} %dens_in.1), custom_call_target="tpu_custom_call" | custom-call | flops 8049999872 | tf_op jit(solution)/shard_map/settle/pallas_call | solution.py:422
  (16 shorter events, 0.0 us)
Async XLA Ops:
  0.6 13.9 %all-to-all-start = ((s32[8,1,48]{2,1,0:T(1,128)}), s32[8,1,48]{2,1,0:T(1,128)S(1)}, u32[]{:S(2)}, u32[]{:S(2)}) async-start(s32[8,1,48]{2,1,0:T(1,128)} %bitcast.8), calls=%async_computation | async-start | bytes 8192 | tf_op jit(solution)/shard_map/all_to_all | solution.py:765
  6.8 7.8 %copy-start.1 = (f32[3,32,16,256]{3,2,1,0:T(8,128)S(1)}, f32[3,32,16,256]{3,2,1,0:T(8,128)}, u32[]{:S(2)}) copy-start(f32[3,32,16,256]{3,2,1,0:T(8,128)} %vel.5) | copy-start | bytes 4718596
  9.0 17.6 %collective-permute-start = (f32[6,4,16,256]{3,2,1,0:T(8,128)}, f32[6,4,16,256]{3,2,1,0:T(8,128)S(1)}, u32[]{:S(2)}, u32[]{:S(2)}) collective-permute-start(f32[6,4,16,256]{3,2,1,0:T(8,128)} %get-tuple-element.15), channel_id=1, source_target_pairs={{0,8},{8,16},{16,24},{1,9},{9,17},{17,25},{2,10},{10,18},{18,26},{... | collective-permute-start | bytes 1179656 | tf_op jit(solution)/shard_map/ppermute | solution.py:751
  10.9 15.7 %collective-permute-start.1 = (f32[6,4,16,256]{3,2,1,0:T(8,128)}, f32[6,4,16,256]{3,2,1,0:T(8,128)}, u32[]{:S(2)}, u32[]{:S(2)}) collective-permute-start(f32[6,4,16,256]{3,2,1,0:T(8,128)} %get-tuple-element.16), channel_id=1, source_target_pairs={{8,0},{16,8},{24,16},{9,1},{17,9},{25,17},{10,2},{18,10},{26,18},{... | collective-permute-start | bytes 1179656 | tf_op jit(solution)/shard_map/ppermute | solution.py:751
  14.6 6.0 %copy-start = (s32[8,1,48]{2,1,0:T(1,128)}, s32[8,1,48]{2,1,0:T(1,128)S(1)}, u32[]{:S(2)}) copy-start(s32[8,1,48]{2,1,0:T(1,128)S(1)} %all-to-all-done) | copy-start | bytes 4612
  14.6 12.0 %copy-start.2 = (f32[32,16,256]{2,1,0:T(8,128)S(1)}, f32[32,16,256]{2,1,0:T(8,128)}, u32[]{:S(2)}) copy-start(f32[32,16,256]{2,1,0:T(8,128)} %pres.3) | copy-start | bytes 1572868
  14.6 12.0 %copy-start.4 = (f32[32,16,256]{2,1,0:T(8,128)S(1)}, f32[32,16,256]{2,1,0:T(8,128)}, u32[]{:S(2)}) copy-start(f32[32,16,256]{2,1,0:T(8,128)} %visc_in.1) | copy-start | bytes 1572868
  14.6 12.0 %copy-start.6 = (f32[32,16,256]{2,1,0:T(8,128)S(1)}, f32[32,16,256]{2,1,0:T(8,128)}, u32[]{:S(2)}) copy-start(f32[32,16,256]{2,1,0:T(8,128)} %dens_in.1) | copy-start | bytes 1572868
  20.6 20.1 %all-to-all-start.1 = ((f32[8,3,48,128]{3,2,1,0:T(8,128)}), f32[8,3,48,128]{3,2,1,0:T(8,128)}, u32[]{:S(2)}, u32[]{:S(2)}) async-start(f32[8,3,48,128]{3,2,1,0:T(8,128)} %pick_bricks.1), calls=%async_computation.1 | async-start | bytes 1179648 | tf_op jit(solution)/shard_map/all_to_all | solution.py:773
  26.6 2.9 %copy-start.8 = (f32[6,4,16,256]{3,2,1,0:T(8,128)}, f32[6,4,16,256]{3,2,1,0:T(8,128)S(1)}, u32[]{:S(2)}) copy-start(f32[6,4,16,256]{3,2,1,0:T(8,128)S(1)} %collective-permute-done.low_x) | copy-start | bytes 1179652
  29.5 46.0 %collective-permute-start.2 = (f32[35,24,256]{2,1,0:T(8,128)}, f32[35,24,256]{2,1,0:T(8,128)S(1)}, u32[]{:S(2)}, u32[]{:S(2)}) collective-permute-start(f32[35,24,256]{2,1,0:T(8,128)} %get-tuple-element.17.refs_6_), channel_id=1, source_target_pairs={{0,1},{1,2},{2,3},{3,4},{4,5},{5,6},{6,7},{8,9},{9,10},{10,11},{11... | collective-permute-start | bytes 2580488 | tf_op jit(solution)/shard_map/ppermute | solution.py:751
  32.8 47.6 %collective-permute-start.3 = (f32[35,24,256]{2,1,0:T(8,128)}, f32[35,24,256]{2,1,0:T(8,128)S(1)}, u32[]{:S(2)}, u32[]{:S(2)}) collective-permute-start(f32[35,24,256]{2,1,0:T(8,128)} %get-tuple-element.18), channel_id=1, source_target_pairs={{1,0},{2,1},{3,2},{4,3},{5,4},{6,5},{7,6},{9,8},{10,9},{11,10},{12... | collective-permute-start | bytes 2580488 | tf_op jit(solution)/shard_map/ppermute | solution.py:751
  56.4 44.1 %all-to-all-start.2 = ((f32[8,3,48,128]{3,2,1,0:T(8,128)}), f32[8,3,48,128]{3,2,1,0:T(8,128)}, u32[]{:S(2)}, u32[]{:S(2)}) async-start(f32[8,3,48,128]{3,2,1,0:T(8,128)} %get-tuple-element.21), calls=%async_computation.2 | async-start | bytes 1179648 | tf_op jit(solution)/shard_map/all_to_all | solution.py:777
  80.4 1.0 copy-start.3
  81.4 1.0 copy-start.5
  82.5 1.0 copy-start.7
  83.5 1.0 copy-start.9
